TPU v7x, 32 devices: a whole 2x2x4 slice. The times are simulated.
32 devices in a mesh: dp: 8 (over y, x, core), tensor: 4 (over z).
Axes of the slice: x: 2, y: 2, z: 4, core: 2. Of those that a mesh axis runs over, the one named last changes fastest.
Arguments:
- raw_series: bfloat16 [2, 32, 1024, 144], P(None, ('dp', 'tensor')), may hold values from -6 to 6
- median_code: int32 [2, 32], P(None, ('dp', 'tensor')), may hold values from -20 to 20
- scale_code: int32 [2, 32], P(None, ('dp', 'tensor')), may hold values from 2 to 8
- qkv_weight: bfloat16 [144, 432], replicated, may hold values from -0.5 to 0.5
- out_weight: bfloat16 [144, 144], replicated, may hold values from -2 to 2
- attn_gain: float32 [144], replicated, may hold values from 0.5 to 1.5
- gate_weight: bfloat16 [144, 512], P(None, 'tensor'), may hold values from -0.5 to 0.5
- up_weight: bfloat16 [144, 512], P(None, 'tensor'), may hold values from -0.5 to 0.5
- down_weight: bfloat16 [512, 144], P('tensor'), may hold values from -0.25 to 0.25
- mlp_gain: float32 [144], replicated, may hold values from 0.5 to 1.5
- cotangent: bfloat16 [2, 32, 1024, 144], P(None, ('dp', 'tensor')), may hold values from -6 to 6
Outputs:
- result: bfloat16 [2, 32, 1024, 144], P(None, ('dp', 'tensor'))
- input_grad: float32 [2, 32, 1024, 144], P(None, ('dp', 'tensor'))
- qkv_grad: float32 [144, 432], replicated
- out_grad: float32 [144, 144], replicated
- attn_gain_grad: float32 [144], replicated
- gate_grad: float32 [144, 512], P(None, 'tensor')
- up_grad: float32 [144, 512], P(None, 'tensor')
- down_grad: float32 [512, 144], P('tensor')
- mlp_gain_grad: float32 [144], replicated
All inputs are finite; a program needn't handle non-finite values.
Results may differ from a plain program's by a relative error of at most 0.009.
Values may be sent and summed in bfloat16 or wider, within the bound.
A program may use at most 128 MiB of HBM per device.

v0:
```python
import jax
import jax.numpy as jnp
from jax import lax
from jax.sharding import PartitionSpec as P

HEADS = 9
HEAD_DIM = 16
QBLK = 512


epsilon = 1e-05
masked_value = -1e30


def rope_tables(length, head_width):
    half_width = head_width // 2
    frequency = 10000.0 ** (-(jnp.arange(half_width, dtype=jnp.float32) * 2.0 / head_width))
    angles = jnp.arange(length, dtype=jnp.float32)[:, None] * frequency[None, :]
    return (jnp.cos(angles), jnp.sin(angles))


def rotate(values, cosine, sine_table):
    half_width = values.shape[-1] // 2
    first_half = values[..., :half_width]
    second_half = values[..., half_width:]
    return jnp.concatenate(
        [
            first_half * cosine - second_half * sine_table,
            first_half * sine_table + second_half * cosine,
        ],
        axis=-1,
    )


def rotate_back(gradient, cosine, sine_table):
    half_width = gradient.shape[-1] // 2
    first_half = gradient[..., :half_width]
    second_half = gradient[..., half_width:]
    return jnp.concatenate(
        [
            first_half * cosine + second_half * sine_table,
            second_half * cosine - first_half * sine_table,
        ],
        axis=-1,
    )


def norm_forward(inputs, gain):
    inverse = lax.rsqrt(jnp.mean(inputs * inputs, axis=-1, keepdims=True) + epsilon)
    scaled = inputs * inverse
    return ((scaled * gain).astype(jnp.bfloat16), scaled, inverse)


def norm_backward(incoming, scaled, inverse, gain):
    weighted = incoming * gain
    input_part = inverse * (weighted - scaled * jnp.mean(weighted * scaled, axis=-1, keepdims=True))
    return (input_part, jnp.sum(incoming * scaled, axis=(0, 1)))


def causal_mask(block_start, block_rows, key_end):
    query_pos = block_start + lax.broadcasted_iota(jnp.int32, (block_rows, key_end), 0)
    key_pos = lax.broadcasted_iota(jnp.int32, (block_rows, key_end), 1)
    return key_pos <= query_pos


def block_scores(query_block, keys_rot, block_start, block_rows, key_end):
    scores = jnp.einsum(
        "hqd,hkd->hqk", query_block, keys_rot[:, :key_end], preferred_element_type=jnp.float32
    ) * HEAD_DIM ** (-0.5)
    return jnp.where(causal_mask(block_start, block_rows, key_end), scores, masked_value)


def series_forward(operands):
    queries, keys_rot, values_in = operands
    length = queries.shape[1]
    block_rows = min(QBLK, length)
    outputs = []
    log_totals = []
    for block_start in range(0, length, block_rows):
        key_end = block_start + block_rows
        masked = block_scores(
            queries[:, block_start:key_end], keys_rot, block_start, block_rows, key_end
        )
        largest = jnp.max(masked, axis=-1, keepdims=True)
        weights = jnp.exp(masked - largest)
        summed = jnp.sum(weights, axis=-1, keepdims=True)
        probs = (weights / summed).astype(jnp.bfloat16)
        mixed = jnp.einsum(
            "hqk,hkd->hqd", probs, values_in[:, :key_end], preferred_element_type=jnp.float32
        )
        outputs.append(mixed.astype(jnp.bfloat16))
        log_totals.append((largest + jnp.log(summed))[..., 0])
    return (jnp.concatenate(outputs, axis=1), jnp.concatenate(log_totals, axis=1))


def series_backward(operands):
    queries, keys_rot, values_in, row_lse, attended_grad = operands
    length = queries.shape[1]
    block_rows = min(QBLK, length)
    score_scale = HEAD_DIM ** (-0.5)
    query_grads = []
    key_grad = jnp.zeros(queries.shape, jnp.float32)
    value_grad = jnp.zeros(queries.shape, jnp.float32)
    for block_start in range(0, length, block_rows):
        key_end = block_start + block_rows
        query_block = queries[:, block_start:key_end]
        masked = block_scores(query_block, keys_rot, block_start, block_rows, key_end)
        probs = jnp.exp(masked - row_lse[:, block_start:key_end, None])
        probs_low = probs.astype(jnp.bfloat16)
        grad_block = attended_grad[:, block_start:key_end]
        grad_probs = jnp.einsum(
            "hqd,hkd->hqk", grad_block, values_in[:, :key_end], preferred_element_type=jnp.float32
        )
        row_delta = jnp.sum(grad_probs * probs, axis=-1, keepdims=True)
        grad_scores = (probs * (grad_probs - row_delta)).astype(jnp.bfloat16)
        query_grads.append(
            jnp.einsum(
                "hqk,hkd->hqd",
                grad_scores,
                keys_rot[:, :key_end],
                preferred_element_type=jnp.float32,
            )
            * score_scale
        )
        key_piece = (
            jnp.einsum("hqk,hqd->hkd", grad_scores, query_block, preferred_element_type=jnp.float32)
            * score_scale
        )
        value_piece = jnp.einsum(
            "hqk,hqd->hkd", probs_low, grad_block, preferred_element_type=jnp.float32
        )
        padding = ((0, 0), (0, length - key_end), (0, 0))
        key_grad = key_grad + jnp.pad(key_piece, padding)
        value_grad = value_grad + jnp.pad(value_piece, padding)
    return (jnp.concatenate(query_grads, axis=1), key_grad, value_grad)


def project_heads(rows_all, qkv_local, local_heads):
    groups, length, model_width = rows_all.shape
    projected = jnp.dot(
        rows_all.reshape(-1, model_width), qkv_local, preferred_element_type=jnp.float32
    )
    projected = projected.reshape(groups, length, 3, local_heads, HEAD_DIM).transpose(2, 0, 3, 1, 4)
    cosine, sine_table = rope_tables(length, HEAD_DIM)
    queries = rotate(projected[0], cosine, sine_table).astype(jnp.bfloat16)
    keys_rot = rotate(projected[1], cosine, sine_table).astype(jnp.bfloat16)
    return (queries, keys_rot, projected[2].astype(jnp.bfloat16), cosine, sine_table)


def local(
    raw_series,
    median_code,
    scale_code,
    qkv_weight,
    out_weight,
    attn_gain,
    gate_weight,
    up_weight,
    down_weight,
    mlp_gain,
    cotangent,
):
    micro_count, series_local, length, model_width = raw_series.shape
    gate_local, up_local, down_local = (gate_weight, up_weight, down_weight)
    local_heads = 3
    device = lax.axis_index("tensor")
    first_head = jnp.where(device == 0, 0, 2 * device + 1)
    head_count = jnp.where(device == 0, 3, 2)
    slot_iota = jnp.arange(local_heads, dtype=jnp.int32)
    slot_heads = jnp.minimum(first_head + slot_iota, HEADS - 1)
    slot_live = slot_iota < head_count
    matches = (slot_heads[:, None] == jnp.arange(HEADS, dtype=jnp.int32)[None, :]) & slot_live[
        :, None
    ]
    selector = jnp.where(matches, 1.0, 0.0).astype(jnp.float32)
    qkv_local = jnp.take(
        qkv_weight.reshape(model_width, 3, HEADS, HEAD_DIM), slot_heads, axis=2
    ).reshape(model_width, -1)
    out_rows = jnp.take(out_weight.reshape(HEADS, HEAD_DIM, model_width), slot_heads, axis=0)
    out_local = jnp.where(slot_live[:, None, None], out_rows, jnp.zeros_like(out_rows)).reshape(
        -1, model_width
    )
    qkv_acc = jnp.zeros(qkv_local.shape, jnp.float32)
    out_acc = jnp.zeros(out_local.shape, jnp.float32)
    gate_acc = jnp.zeros(gate_local.shape, jnp.float32)
    up_acc = jnp.zeros(up_local.shape, jnp.float32)
    down_acc = jnp.zeros(down_local.shape, jnp.float32)
    attn_gain_acc = jnp.zeros(attn_gain.shape, jnp.float32)
    mlp_gain_acc = jnp.zeros(mlp_gain.shape, jnp.float32)
    results = []
    input_grads = []
    for micro_index in range(micro_count):
        shifts = median_code[micro_index].astype(jnp.float32) * 0.05
        spreads = scale_code[micro_index].astype(jnp.float32) * 0.25
        scaled_series = (
            raw_series[micro_index].astype(jnp.float32) - shifts[:, None, None]
        ) / spreads[:, None, None]
        attn_rows, attn_scaled, attn_inverse = norm_forward(scaled_series, attn_gain)
        rows_all = lax.all_gather(attn_rows, "tensor", axis=0, tiled=True)
        groups = rows_all.shape[0]
        rows_flat = rows_all.reshape(-1, model_width)
        queries, keys_rot, values_in, cosine, sine_table = project_heads(
            rows_all, qkv_local, local_heads
        )
        attended, row_lse = lax.map(series_forward, (queries, keys_rot, values_in))
        attended_flat = attended.transpose(0, 2, 1, 3).reshape(-1, local_heads * HEAD_DIM)
        attn_part = jnp.dot(attended_flat, out_local, preferred_element_type=jnp.float32).reshape(
            groups, length, model_width
        )
        hidden = scaled_series + lax.psum_scatter(
            attn_part, "tensor", scatter_dimension=0, tiled=True
        )
        mlp_rows, mlp_scaled, mlp_inverse = norm_forward(hidden, mlp_gain)
        mlp_flat = lax.all_gather(mlp_rows, "tensor", axis=0, tiled=True).reshape(-1, model_width)
        gate = jnp.dot(mlp_flat, gate_local, preferred_element_type=jnp.float32)
        upper = jnp.dot(mlp_flat, up_local, preferred_element_type=jnp.float32)
        sigma = 1.0 / (1.0 + jnp.exp(-gate))
        inner = (gate * sigma * upper).astype(jnp.bfloat16)
        mlp_part = jnp.dot(inner, down_local, preferred_element_type=jnp.float32).reshape(
            groups, length, model_width
        )
        results.append(
            (
                hidden
                + lax.psum_scatter(
                    mlp_part.astype(jnp.bfloat16), "tensor", scatter_dimension=0, tiled=True
                ).astype(jnp.float32)
            ).astype(jnp.bfloat16)
        )
        grad_top = cotangent[micro_index].astype(jnp.float32)
        upstream_all = lax.all_gather(
            grad_top.astype(jnp.bfloat16), "tensor", axis=0, tiled=True
        ).reshape(-1, model_width)
        down_acc = down_acc + jnp.dot(inner.T, upstream_all, preferred_element_type=jnp.float32)
        grad_inner = jnp.dot(upstream_all, down_local.T, preferred_element_type=jnp.float32)
        grad_gate = (grad_inner * upper * sigma * (1.0 + gate * (1.0 - sigma))).astype(jnp.bfloat16)
        grad_up = (grad_inner * gate * sigma).astype(jnp.bfloat16)
        gate_acc = gate_acc + jnp.dot(mlp_flat.T, grad_gate, preferred_element_type=jnp.float32)
        up_acc = up_acc + jnp.dot(mlp_flat.T, grad_up, preferred_element_type=jnp.float32)
        mlp_back = jnp.dot(grad_gate, gate_local.T, preferred_element_type=jnp.float32) + jnp.dot(
            grad_up, up_local.T, preferred_element_type=jnp.float32
        )
        hidden_part, mlp_gain_piece = norm_backward(
            lax.psum_scatter(
                mlp_back.reshape(groups, length, model_width),
                "tensor",
                scatter_dimension=0,
                tiled=True,
            ),
            mlp_scaled,
            mlp_inverse,
            mlp_gain,
        )
        mlp_gain_acc = mlp_gain_acc + mlp_gain_piece
        grad_hidden = grad_top + hidden_part
        branch_all = lax.all_gather(
            grad_hidden.astype(jnp.bfloat16), "tensor", axis=0, tiled=True
        ).reshape(-1, model_width)
        out_acc = out_acc + jnp.dot(attended_flat.T, branch_all, preferred_element_type=jnp.float32)
        attended_grad = jnp.dot(branch_all, out_local.T, preferred_element_type=jnp.float32).astype(
            jnp.bfloat16
        )
        attended_grad = attended_grad.reshape(groups, length, local_heads, HEAD_DIM).transpose(
            0, 2, 1, 3
        )
        query_grad, key_grad, value_grad = lax.map(
            series_backward, (queries, keys_rot, values_in, row_lse, attended_grad)
        )
        raw_grads = jnp.stack(
            [
                rotate_back(query_grad, cosine, sine_table),
                rotate_back(key_grad, cosine, sine_table),
                value_grad,
            ]
        ).astype(jnp.bfloat16)
        qkv_grad_flat = raw_grads.transpose(1, 3, 0, 2, 4).reshape(-1, 3 * local_heads * HEAD_DIM)
        qkv_acc = qkv_acc + jnp.dot(rows_flat.T, qkv_grad_flat, preferred_element_type=jnp.float32)
        attn_back = jnp.dot(qkv_grad_flat, qkv_local.T, preferred_element_type=jnp.float32)
        series_part, attn_gain_piece = norm_backward(
            lax.psum_scatter(
                attn_back.reshape(groups, length, model_width),
                "tensor",
                scatter_dimension=0,
                tiled=True,
            ),
            attn_scaled,
            attn_inverse,
            attn_gain,
        )
        attn_gain_acc = attn_gain_acc + attn_gain_piece
        input_grads.append((grad_hidden + series_part) / spreads[:, None, None])
    qkv_full = jnp.einsum(
        "acsd,sn->acnd",
        qkv_acc.reshape(model_width, 3, local_heads, HEAD_DIM),
        selector,
        precision=lax.Precision.HIGHEST,
    ).reshape(model_width, -1)
    out_full = jnp.einsum(
        "sdw,sn->ndw",
        out_acc.reshape(local_heads, HEAD_DIM, model_width),
        selector,
        precision=lax.Precision.HIGHEST,
    ).reshape(-1, model_width)
    qkv_grad, out_grad, attn_gain_grad, mlp_gain_grad = lax.psum(
        (qkv_full, out_full, attn_gain_acc, mlp_gain_acc), ("dp", "tensor")
    )
    gate_grad, up_grad, down_grad = lax.psum((gate_acc, up_acc, down_acc), "dp")
    return (
        jnp.stack(results),
        jnp.stack(input_grads),
        qkv_grad,
        out_grad,
        attn_gain_grad,
        gate_grad,
        up_grad,
        down_grad,
        mlp_gain_grad,
    )


def solution(mesh):
    placed = (
        P(None, ("dp", "tensor"), None, None),
        P(None, ("dp", "tensor")),
        P(None, ("dp", "tensor")),
        P(),
        P(),
        P(),
        P(None, "tensor"),
        P(None, "tensor"),
        P("tensor", None),
        P(),
        P(None, ("dp", "tensor"), None, None),
    )
    return jax.shard_map(
        local,
        mesh=mesh,
        in_specs=placed,
        out_specs=(
            P(None, ("dp", "tensor"), None, None),
            P(None, ("dp", "tensor"), None, None),
            P(),
            P(),
            P(),
            P(None, "tensor"),
            P(None, "tensor"),
            P("tensor", None),
            P(),
        ),
        check_vma=False,
    )
```

profile of v0, /device:TPU:0, one launch (start us, length us, event | category | flops | bytes accessed | tf_op | source)
XLA Modules:
  0.0 993.0 jit_solution(14850425048771366351)
XLA Ops:
  13.8 2.1 multiply_convert_fusion.13
  19.9 29.3 %all-gather.15.cloned.1.call-done = bf16[4,1024,144]{1,2,0:T(8,128)(2,1)} async-done(((bf16[1,1024,144]{1,2,0:T(8,128)(2,1)}), bf16[4,1024,144]{1,2,0:T(8,128)(2,1)}) %all-gather.15.cloned.1.call-update) | async-done | bytes 1179664 | tf_op jit(solution)/shard_map/all_gather | solution.py:199
  51.2 29.7 %all-gather.11.cloned.1.call-done = bf16[4,1024,144]{1,2,0:T(8,128)(2,1)} async-done(((bf16[1,1024,144]{1,2,0:T(8,128)(2,1)}), bf16[4,1024,144]{1,2,0:T(8,128)(2,1)}) %all-gather.11.cloned.1.call-update) | async-done | bytes 1179664 | tf_op jit(solution)/shard_map/all_gather | solution.py:199
  84.1 33.3 %while.56 = (s32[]{:T(128)}, bf16[4,3,1024,16]{2,3,1,0:T(8,128)(2,1)S(1)}, f32[4,3,1024]{2,1,0:T(4,128)S(1)}, bf16[4,3,1024,16]{2,3,1,0:T(8,128)(2,1)S(1)}, bf16...) while((s32[]{:T(128)}, bf16[4,3,1024,16]{2,3,1,0:T(8,128)(2,1)S(1)}, ...), condition=%wide.region_6.7_spmd, body=%wide.region_1.6_spmd.sunk | while | flops 180339200 | bytes 32874596 | solution.py:205
  90.3 2.1 fusion.305
  98.6 2.1 fusion.305
  107.0 2.1 fusion.305
  115.3 2.1 fusion.305
  119.8 33.3 %while.57 = (s32[]{:T(128)}, bf16[4,3,1024,16]{2,3,1,0:T(8,128)(2,1)S(1)}, f32[4,3,1024]{2,1,0:T(4,128)S(1)}, bf16[4,3,1024,16]{2,3,1,0:T(8,128)(2,1)S(1)}, bf16...) while((s32[]{:T(128)}, bf16[4,3,1024,16]{2,3,1,0:T(8,128)(2,1)S(1)}, ...), condition=%wide.region_16.17_spmd, body=%wide.region_11.16_spmd.sunk | while | flops 180339200 | bytes 32874596 | solution.py:205
  126.0 2.1 fusion.316
  134.3 2.1 fusion.316
  142.7 2.1 fusion.316
  157.7 9.1 reduce-scatter.9.cloned.1.call-done
  166.7 49.7 %reduce-scatter.13.cloned.1.call-done = f32[1,1024,144]{1,2,0:T(8,128)} async-done(((f32[4,1024,144]{1,2,0:T(8,128)}), f32[1,1024,144]{1,2,0:T(8,128)}) %reduce-scatter.13.cloned.1.call-update) | async-done | bytes 589840 | tf_op jit(solution)/shard_map/reduce_scatter | solution.py:210
  219.3 29.1 %all-gather.23.cloned.1.call-done = bf16[4,1,1024,144]{2,3,1,0:T(8,128)(2,1)} async-done(((bf16[1,1,1024,144]{2,3,1,0:T(8,128)(2,1)}), bf16[4,1,1024,144]{2,3,1,0:T(8,128)(2,1)}) %all-gather.23.cloned.1.call-update) | async-done | bytes 1179664 | tf_op jit(solution)/shard_map/all_gather | solution.py:231
  248.4 2.2 copy.127
  252.1 27.9 %all-gather.13.cloned.1.call-done = bf16[4,1024,144]{1,2,0:T(8,128)(2,1)} async-done(((bf16[1,1024,144]{1,2,0:T(8,128)(2,1)}), bf16[4,1024,144]{1,2,0:T(8,128)(2,1)}) %all-gather.13.cloned.1.call-update) | async-done | bytes 1179664 | tf_op jit(solution)/shard_map/all_gather | solution.py:214
  283.5 2.5 multiply_convert_fusion.6
  290.1 46.5 %reduce-scatter.17.cloned.1.call-done = f32[1,1024,144]{1,2,0:T(8,128)} async-done(((f32[4,1024,144]{1,2,0:T(8,128)}), f32[1,1024,144]{1,2,0:T(8,128)}) %reduce-scatter.17.cloned.1.call-update) | async-done | bytes 589840 | tf_op jit(solution)/shard_map/reduce_scatter | solution.py:244
  336.5 2.5 multiply_reduce_fusion.5
  339.2 28.9 %all-gather.25.cloned.1.call-done = bf16[4,1,1024,144]{2,3,1,0:T(8,128)(2,1)} async-done(((bf16[1,1,1024,144]{2,3,1,0:T(8,128)(2,1)}), bf16[4,1,1024,144]{2,3,1,0:T(8,128)(2,1)}) %all-gather.25.cloned.1.call-update) | async-done | bytes 1179664 | tf_op jit(solution)/shard_map/all_gather | solution.py:231
  368.1 2.2 copy.132
  371.8 28.0 %all-gather.17.cloned.1.call-done = bf16[4,1024,144]{1,2,0:T(8,128)(2,1)} async-done(((bf16[1,1024,144]{1,2,0:T(8,128)(2,1)}), bf16[4,1024,144]{1,2,0:T(8,128)(2,1)}) %all-gather.17.cloned.1.call-update) | async-done | bytes 1179664 | tf_op jit(solution)/shard_map/all_gather | solution.py:214
  403.3 2.5 multiply_convert_fusion.4
  413.0 43.2 %reduce-scatter.21.cloned.1.call-done = f32[1,1024,144]{1,2,0:T(8,128)} async-done(((f32[4,1024,144]{1,2,0:T(8,128)}), f32[1,1024,144]{1,2,0:T(8,128)}) %reduce-scatter.21.cloned.1.call-update) | async-done | bytes 589840 | tf_op jit(solution)/shard_map/reduce_scatter | solution.py:244
  458.0 29.2 %reduce-scatter.15.cloned.1.call-done = bf16[1,1024,144]{1,2,0:T(8,128)(2,1)} async-done(((bf16[4,1024,144]{1,2,0:T(8,128)(2,1)}), bf16[1,1024,144]{1,2,0:T(8,128)(2,1)}) %reduce-scatter.15.cloned.1.call-update) | async-done | bytes 294928 | tf_op jit(solution)/shard_map/reduce_scatter | solution.py:225
  487.2 2.4 fusion.123
  491.1 2.5 copy.181
  497.2 21.8 %all-gather.19.cloned.1.call-done = bf16[4,1024,144]{1,2,0:T(8,128)(2,1)} async-done(((bf16[1,1024,144]{1,2,0:T(8,128)(2,1)}), bf16[4,1024,144]{1,2,0:T(8,128)(2,1)}) %all-gather.19.cloned.1.call-update) | async-done | bytes 1179664 | tf_op jit(solution)/shard_map/all_gather | solution.py:256
  523.0 60.9 %while.58 = (s32[]{:T(128)}, f32[4,3,1024,16]{2,3,1,0:T(8,128)}, f32[4,3,1024,16]{2,3,1,0:T(8,128)S(1)}, bf16[4,3,1024,16]{2,3,1,0:T(8,128)(2,1)S(1)}, bf16[4,3,...) while((s32[]{:T(128)}, f32[4,3,1024,16]{2,3,1,0:T(8,128)}, ...), condition=%wide.region_25.26_spmd, body=%wide.region_22.25_spmd.sunk | while | flops 409212416 | bytes 76507272 | solution.py:266
  531.7 2.5 multiply_reduce_fusion.18
  546.9 2.5 multiply_reduce_fusion.18
  562.2 2.5 multiply_reduce_fusion.18
  577.4 2.5 multiply_reduce_fusion.18
  583.9 2.4 fusion.160
  589.5 65.1 %while.59 = (s32[]{:T(128)}, f32[4,3,1024,16]{2,3,1,0:T(8,128)S(1)}, f32[4,3,1024,16]{2,3,1,0:T(8,128)}, bf16[4,3,1024,16]{2,3,1,0:T(8,128)(2,1)}, bf16[4,3,1024...) while((s32[]{:T(128)}, ...), condition=%wide.region_33.34_spmd, body=%wide.region_30.33_spmd.sunk | while | flops 409212416 | bytes 79653056 | solution.py:266
  599.4 2.5 multiply_reduce_fusion.20
  615.6 2.5 multiply_reduce_fusion.20
  631.8 2.5 multiply_reduce_fusion.20
  648.0 2.5 multiply_reduce_fusion.20
  665.7 2.1 convolution_bitcast_fusion
  667.8 2.1 convolution_bitcast_fusion.1
  680.5 112.1 %all-reduce.10.cloned.1.call-done = (f32[144,432]{0,1:T(8,128)}, f32[144,144]{1,0:T(8,128)}) async-done(((f32[144,432]{0,1:T(8,128)}, f32[144,144]{1,0:T(8,128)}), (f32[144,432]{0,1:T(8,128)}, f32[144,144]{1,0:T(8,128)})) %all-reduce.10.cloned.1.call-update) | async-done | bytes 331792 | tf_op jit(solution)/shard_map/psum | solution.py:304
  794.5 48.7 %reduce-scatter.23.cloned.1.call-done = f32[1,1024,144]{1,2,0:T(8,128)} async-done(((f32[4,1024,144]{1,2,0:T(8,128)}), f32[1,1024,144]{1,2,0:T(8,128)}) %reduce-scatter.23.cloned.1.call-update) | async-done | bytes 589840 | tf_op jit(solution)/shard_map/reduce_scatter | solution.py:280
  843.2 49.9 %reduce-scatter.19.cloned.1.call-done = f32[1,1024,144]{1,2,0:T(8,128)} async-done(((f32[4,1024,144]{1,2,0:T(8,128)}), f32[1,1024,144]{1,2,0:T(8,128)}) %reduce-scatter.19.cloned.1.call-update) | async-done | bytes 589840 | tf_op jit(solution)/shard_map/reduce_scatter | solution.py:280
  894.8 41.4 %all-reduce.4 = (f32[144]{0:T(256)}, f32[144]{0:T(256)}) all-reduce(f32[144]{0:T(256)S(1)} %add.322, f32[144]{0:T(256)S(1)} %add.326), channel_id=1, replica_groups=mesh['dp'=8,'tensor'=4] {'dp','tensor'}, use_global_device_ids=true, to_apply=%region_40.41 | all-reduce | flops 288 | bytes 2304 | tf_op jit(solution)/shard_map/psum | solution.py:304
  936.2 2.5 divide_bitcast_fusion
  942.4 38.3 %all-reduce.12.cloned.1.call-done = (f32[144,128]{1,0:T(8,128)}, f32[144,128]{1,0:T(8,128)}, f32[128,144]{0,1:T(8,128)}) async-done(((f32[144,128]{1,0:T(8,128)}, f32[144,128]{1,0:T(8,128)}, f32[128,144]{0,1:T(8,128)}), (f32[144,128]{1,0:T(8,128)}, f32[144,128]{1,0:T(8,128)}, f32[128,144]{0,1:T(8,128)})) %all-reduce.12.cloned.1.call-update) | async-done | bytes 221200 | tf_op jit(solution)/shard_map/psum | solution.py:307
  (600 shorter events, 247.6 us)
Async XLA Ops:
  7.2 42.0 %all-gather.15.cloned.1.call-start = ((), (), s32[]{:S(2)}) async-start(), calls=%async_computation.12 | async-start | bytes 1474560 | tf_op jit(solution)/shard_map/all_gather | solution.py:199
  15.9 65.0 %all-gather.11.cloned.1.call-start = ((), (), s32[]{:S(2)}) async-start(), calls=%async_computation.8 | async-start | bytes 1474560 | tf_op jit(solution)/shard_map/all_gather | solution.py:199
  16.7 150.1 %reduce-scatter.9.cloned.1.call-start = ((), (), s32[]{:S(2)}) async-start(), calls=%async_computation.9 | async-start | bytes 2949120 | tf_op jit(solution)/shard_map/reduce_scatter | solution.py:210
  16.7 34.2 %copy-start.77 = (pred[3]{0:T(512)(128)(4,1)}, pred[3]{0:T(512)(128)(4,1)S(1)}, u32[]{:S(2)}) copy-start(pred[3]{0:T(512)(128)(4,1)S(1)} %get-tuple-element.516) | copy-start | bytes 13
  16.7 34.2 %copy-start.79 = (pred[3]{0:T(512)(128)(4,1)}, pred[3]{0:T(512)(128)(4,1)S(1)}, u32[]{:S(2)}) copy-start(pred[3]{0:T(512)(128)(4,1)S(1)} %get-tuple-element.515) | copy-start | bytes 13
  18.2 32.8 %copy-start.36 = (bf16[3,144,3,16]{1,3,2,0:T(8,128)(2,1)}, bf16[3,144,3,16]{1,3,2,0:T(8,128)(2,1)S(1)}, u32[]{:S(2)}) copy-start(bf16[3,144,3,16]{1,3,2,0:T(8,128)(2,1)S(1)} %gather_fusion) | copy-start | bytes 124420
  84.1 33.4 %copy-start.49 = (bf16[3,16,144]{2,1,0:T(8,128)(2,1)S(1)}, bf16[3,16,144]{2,1,0:T(8,128)(2,1)}, u32[]{:S(2)}) copy-start(bf16[3,16,144]{2,1,0:T(8,128)(2,1)} %select_select_fusion) | copy-start | bytes 41476
  119.5 97.0 %reduce-scatter.13.cloned.1.call-start = ((), (), s32[]{:S(2)}) async-start(), calls=%async_computation.13 | async-start | bytes 2949120 | tf_op jit(solution)/shard_map/reduce_scatter | solution.py:210
  156.6 59.9 %copy-start.10 = (bf16[2,1,1024,144]{2,3,1,0:T(8,128)(2,1)S(1)}, bf16[2,1,1024,144]{2,3,1,0:T(8,128)(2,1)}, u32[]{:S(2)}) copy-start(bf16[2,1,1024,144]{2,3,1,0:T(8,128)(2,1)} %param.19) | copy-start | bytes 1769476
  156.7 61.4 %copy-start.74 = (f32[144]{0:T(256)S(1)}, f32[144]{0:T(256)}, u32[]{:S(2)}) copy-start(f32[144]{0:T(256)} %param.28) | copy-start | bytes 1732
  156.7 91.8 %all-gather.23.cloned.1.call-start = ((), (), s32[]{:S(2)}) async-start(), calls=%async_computation.22 | async-start | bytes 1474560 | tf_op jit(solution)/shard_map/all_gather | solution.py:231
  157.6 122.4 %all-gather.13.cloned.1.call-start = ((), (), s32[]{:S(2)}) async-start(), calls=%async_computation.10 | async-start | bytes 1474560 | tf_op jit(solution)/shard_map/all_gather | solution.py:214
  218.0 269.3 %copy-start.6 = (f32[1,1024,144]{1,2,0:T(8,128)}, f32[1,1024,144]{1,2,0:T(8,128)S(1)}, u32[]{:S(2)}) copy-start(f32[1,1024,144]{1,2,0:T(8,128)S(1)} %get-tuple-element.422) | copy-start | bytes 1769476
  218.0 269.2 %copy-start.8 = (f32[1,1024,144]{1,2,0:T(8,128)}, f32[1,1024,144]{1,2,0:T(8,128)S(1)}, u32[]{:S(2)}) copy-start(f32[1,1024,144]{1,2,0:T(8,128)S(1)} %get-tuple-element.495) | copy-start | bytes 1769476
  218.0 269.2 %copy-start.64 = (f32[1024]{0:T(1024)}, f32[1024]{0:T(1024)S(1)}, u32[]{:S(2)}) copy-start(f32[1024]{0:T(1024)S(1)} %add_rsqrt_fusion.2) | copy-start | bytes 12292
  219.0 117.5 %reduce-scatter.17.cloned.1.call-start = ((), (), s32[]{:S(2)}) async-start(), calls=%async_computation.16 | async-start | bytes 2949120 | tf_op jit(solution)/shard_map/reduce_scatter | solution.py:244
  289.3 78.8 %all-gather.25.cloned.1.call-start = ((), (), s32[]{:S(2)}) async-start(), calls=%async_computation.23 | async-start | bytes 1474560 | tf_op jit(solution)/shard_map/all_gather | solution.py:231
  290.0 109.8 %all-gather.17.cloned.1.call-start = ((), (), s32[]{:S(2)}) async-start(), calls=%async_computation.14 | async-start | bytes 1474560 | tf_op jit(solution)/shard_map/all_gather | solution.py:214
  290.1 197.2 %copy-start.62 = (f32[1024]{0:T(1024)}, f32[1024]{0:T(1024)S(1)}, u32[]{:S(2)}) copy-start(f32[1024]{0:T(1024)S(1)} %add_rsqrt_fusion) | copy-start | bytes 12292
  339.1 117.1 %reduce-scatter.21.cloned.1.call-start = ((), (), s32[]{:S(2)}) async-start(), calls=%async_computation.19 | async-start | bytes 2949120 | tf_op jit(solution)/shard_map/reduce_scatter | solution.py:244
  408.9 78.3 %reduce-scatter.15.cloned.1.call-start = ((), (), s32[]{:S(2)}) async-start(), calls=%async_computation.15 | async-start | bytes 1474560 | tf_op jit(solution)/shard_map/reduce_scatter | solution.py:225
  410.6 76.6 %copy-start.13 = (f32[1,1024,144]{1,2,0:T(8,128)S(1)}, f32[1,1024,144]{1,2,0:T(8,128)}, u32[]{:S(2)}) copy-start(f32[1,1024,144]{1,2,0:T(8,128)} %reduce-scatter.17.cloned.1.call-done) | copy-start | bytes 1769476
  411.8 107.2 %all-gather.19.cloned.1.call-start = ((), (), s32[]{:S(2)}) async-start(), calls=%async_computation.17 | async-start | bytes 1474560 | tf_op jit(solution)/shard_map/all_gather | solution.py:256
  413.0 76.7 %copy-start.72 = (f32[1024]{0:T(1024)}, f32[1024]{0:T(1024)S(1)}, u32[]{:S(2)}) copy-start(f32[1024]{0:T(1024)S(1)} %broadcast_multiply_fusion.3) | copy-start | bytes 12292
  458.0 31.8 %copy-start.70 = (f32[1024]{0:T(1024)}, f32[1024]{0:T(1024)S(1)}, u32[]{:S(2)}) copy-start(f32[1024]{0:T(1024)S(1)} %broadcast_multiply_fusion.1) | copy-start | bytes 12292
  489.7 96.6 %all-gather.21.cloned.1.call-start = ((), (), s32[]{:S(2)}) async-start(), calls=%async_computation.20 | async-start | bytes 1474560 | tf_op jit(solution)/shard_map/all_gather | solution.py:256
  497.2 295.4 %all-reduce.10.cloned.1.call-start = ((), (), s32[]{:S(2)}) async-start(), calls=%async_computation.24 | async-start | bytes 1179648 | tf_op jit(solution)/shard_map/psum | solution.py:304
  589.5 66.9 %copy-start.78 = (pred[3]{0:T(512)(128)(4,1)S(1)}, pred[3]{0:T(512)(128)(4,1)}, u32[]{:S(2)}) copy-start(pred[3]{0:T(512)(128)(4,1)} %copy-done.77) | copy-start | bytes 13
  589.5 66.9 %copy-start.83 = (s32[3]{0:T(128)S(1)}, s32[3]{0:T(128)}, u32[]{:S(2)}) copy-start(s32[3]{0:T(128)} %add_minimum_fusion) | copy-start | bytes 40
  665.6 177.6 %reduce-scatter.23.cloned.1.call-start = ((), (), s32[]{:S(2)}) async-start(), calls=%async_computation.21 | async-start | bytes 2949120 | tf_op jit(solution)/shard_map/reduce_scatter | solution.py:280
  667.8 225.3 %reduce-scatter.19.cloned.1.call-start = ((), (), s32[]{:S(2)}) async-start(), calls=%async_computation.18 | async-start | bytes 2949120 | tf_op jit(solution)/shard_map/reduce_scatter | solution.py:280
  669.9 268.8 %reduce-scatter.11.cloned.1.call-start = ((), (), s32[]{:S(2)}) async-start(), calls=%async_computation.11 | async-start | bytes 1474560 | tf_op jit(solution)/shard_map/reduce_scatter | solution.py:225
  672.8 307.9 %all-reduce.12.cloned.1.call-start = ((), (), s32[]{:S(2)}) async-start(), calls=%async_computation.25 | async-start | bytes 442368 | tf_op jit(solution)/shard_map/psum | solution.py:307
  678.2 214.9 %copy-start.11 = (bf16[2,1,1024,144]{2,3,1,0:T(8,128)(2,1)S(1)}, bf16[2,1,1024,144]{2,3,1,0:T(8,128)(2,1)}, u32[]{:S(2)}) copy-start(bf16[2,1,1024,144]{2,3,1,0:T(8,128)(2,1)} %param.19) | copy-start | bytes 1769476
  678.2 214.8 %copy-start.67 = (f32[1024]{0:T(1024)S(1)}, f32[1024]{0:T(1024)}, u32[]{:S(2)}) copy-start(f32[1024]{0:T(1024)} %copy-done.66) | copy-start | bytes 12292
  678.2 214.8 %copy-start.69 = (f32[1024]{0:T(1024)S(1)}, f32[1024]{0:T(1024)}, u32[]{:S(2)}) copy-start(f32[1024]{0:T(1024)} %copy-done.68) | copy-start | bytes 12292
  678.2 214.8 %copy-start.76 = (f32[144]{0:T(256)S(1)}, f32[144]{0:T(256)}, u32[]{:S(2)}) copy-start(f32[144]{0:T(256)} %param.24) | copy-start | bytes 1732
  679.3 256.8 %copy-start.9 = (f32[1,1024,144]{1,2,0:T(8,128)S(1)}, f32[1,1024,144]{1,2,0:T(8,128)}, u32[]{:S(2)}) copy-start(f32[1,1024,144]{1,2,0:T(8,128)} %copy-done.8) | copy-start | bytes 1769476
  679.3 256.8 %copy-start.16 = (bf16[2,1,1024,144]{2,3,1,0:T(8,128)(2,1)S(1)}, bf16[2,1,1024,144]{2,3,1,0:T(8,128)(2,1)}, u32[]{:S(2)}) copy-start(bf16[2,1,1024,144]{2,3,1,0:T(8,128)(2,1)} %param.29) | copy-start | bytes 1769476
  679.3 256.8 %copy-start.63 = (f32[1024]{0:T(1024)S(1)}, f32[1024]{0:T(1024)}, u32[]{:S(2)}) copy-start(f32[1024]{0:T(1024)} %copy-done.62) | copy-start | bytes 12292
  679.3 256.9 %copy-start.71 = (f32[1024]{0:T(1024)S(1)}, f32[1024]{0:T(1024)}, u32[]{:S(2)}) copy-start(f32[1024]{0:T(1024)} %copy-done.70) | copy-start | bytes 12292
  679.3 256.9 %copy-start.75 = (f32[144]{0:T(256)S(1)}, f32[144]{0:T(256)}, u32[]{:S(2)}) copy-start(f32[144]{0:T(256)} %param.28) | copy-start | bytes 1732
  794.5 144.2 %copy-start.7 = (f32[1,1024,144]{1,2,0:T(8,128)S(1)}, f32[1,1024,144]{1,2,0:T(8,128)}, u32[]{:S(2)}) copy-start(f32[1,1024,144]{1,2,0:T(8,128)} %copy-done.6) | copy-start | bytes 1769476
  794.5 144.2 %copy-start.14 = (f32[1,1024,144]{1,2,0:T(8,128)S(1)}, f32[1,1024,144]{1,2,0:T(8,128)}, u32[]{:S(2)}) copy-start(f32[1,1024,144]{1,2,0:T(8,128)} %reduce-scatter.17.cloned.1.call-done) | copy-start | bytes 1769476
  794.5 144.2 %copy-start.65 = (f32[1024]{0:T(1024)S(1)}, f32[1024]{0:T(1024)}, u32[]{:S(2)}) copy-start(f32[1024]{0:T(1024)} %copy-done.64) | copy-start | bytes 12292
  794.5 144.2 %copy-start.73 = (f32[1024]{0:T(1024)S(1)}, f32[1024]{0:T(1024)}, u32[]{:S(2)}) copy-start(f32[1024]{0:T(1024)} %copy-done.72) | copy-start | bytes 12292
  938.7 47.2 %copy-start.1 = (bf16[144,144]{1,0:T(8,128)(2,1)S(1)}, bf16[144,144]{1,0:T(8,128)(2,1)}, u32[]{:S(2)}) copy-start(bf16[144,144]{1,0:T(8,128)(2,1)} %param.23) | copy-start | bytes 124420
  940.4 40.3 %copy-start.58 = (f32[144,144]{1,0:T(8,128)S(1)}, f32[144,144]{1,0:T(8,128)}, u32[]{:S(2)}) copy-start(f32[144,144]{1,0:T(8,128)} %get-tuple-element.872) | copy-start | bytes 248836
  (60 other events, 167.4 us)
Sparse Core Ops, SparseCore 0:
  16.0 33.1 all-gather.14
  51.3 29.5 all-gather.10
  119.6 47.1 reduce-scatter.8
  168.9 47.5 reduce-scatter.12
  218.5 29.9 all-gather.22
  250.4 29.5 all-gather.12
  289.4 47.1 reduce-scatter.16
  338.1 29.9 all-gather.24
  370.2 29.5 all-gather.16
  409.0 47.1 reduce-scatter.20
  458.5 28.6 reduce-scatter.14
  489.8 29.1 all-gather.18
  520.6 29.6 all-gather.20
  665.7 126.8 all-reduce.9
  794.8 48.2 reduce-scatter.22
  845.4 47.5 reduce-scatter.18
  895.3 29.4 reduce-scatter.10
  929.0 51.6 all-reduce.11
where the time goes:
time: 1000 us; the launch traced here: 993 us
  waiting for transfers between devices  623 us (62%)
  matrix products  161 us (16%)
  other arithmetic  77.4 us (8%)
  local copies, waits for them, and re-layouts  68.4 us (7%)
  blocking collectives  41.4 us (4%)
  between operations  18.5 us (2%)
    psum x1, waiting for transfers between devices, local(): lax.psum((qkv_full, out_full, attn_gain_acc, mlp_gain_acc), ('dp', 'tenso...  112 us
    reduce_scatter x2, waiting for transfers between devices, local(): lax.psum_scatter(attn_back.reshape(groups, length, model_width), 'tensor'...  98.5 us
    reduce_scatter x2, waiting for transfers between devices, local(): lax.psum_scatter(mlp_back.reshape(groups, length, model_width), 'tensor',...  89.6 us
    all_gather x2, waiting for transfers between devices, local(): rows_all = lax.all_gather(attn_rows, 'tensor', axis=0, tiled=True)  59 us
    reduce_scatter x2, waiting for transfers between devices, local(): lax.psum_scatter(attn_part, 'tensor', scatter_dimension=0, tiled=True)  58.8 us
    all_gather x2, waiting for transfers between devices, local(): lax.all_gather(grad_top.astype(jnp.bfloat16), 'tensor', axis=0, tiled=True)  58 us
    all_gather x2, waiting for transfers between devices, local(): lax.all_gather(mlp_rows, 'tensor', axis=0, tiled=True)  55.9 us
    psum x1, blocking collectives, local(): lax.psum((qkv_full, out_full, attn_gain_acc, mlp_gain_acc), ('dp', 'tenso...  41.4 us
  transfers between devices with their start and end apart: 18, of which 16 were waited for; matrix products, arithmetic and copies ran while one was open for 16% of the time, Pallas kernels for 0%

commit v1 on v0

v1 whole, which is shorter than its diff:
```python
import functools

import jax
import jax.numpy as jnp
import numpy as np
from jax import lax
from jax.experimental import pallas as pl
from jax.experimental.pallas import tpu as pltpu
from jax.sharding import PartitionSpec as P

BF = jnp.bfloat16
F32 = jnp.float32
HEADS = 9
HEAD_DIM = 16
D = HEADS * HEAD_DIM
BLK = 256
EPS = 1e-05
MASKED = -1e30
LOG2E_SCALED = 0.25 * 1.4426950408889634


def mm(a, b):
    return lax.dot_general(a, b, (((1,), (0,)), ((), ())), preferred_element_type=F32)


def mm_tn(a, b):
    return lax.dot_general(a, b, (((0,), (0,)), ((), ())), preferred_element_type=F32)


def mm_nt(a, b):
    return lax.dot_general(a, b, (((1,), (1,)), ((), ())), preferred_element_type=F32)


def eye(n, dtype):
    same = lax.broadcasted_iota(jnp.int32, (n, n), 0) == lax.broadcasted_iota(jnp.int32, (n, n), 1)
    return jnp.where(same, 1.0, 0.0).astype(dtype)


def to_column(row):
    n = row.shape[1]
    return jnp.sum(eye(n, F32) * row, axis=1, keepdims=True)


def to_row(column):
    n = column.shape[0]
    return jnp.sum(eye(n, F32) * column, axis=0, keepdims=True)


def norm_stats(rows):
    r = lax.rsqrt(jnp.mean(rows * rows, axis=0, keepdims=True) + EPS)
    return rows * r, r


def norm_backward(e, n, r, gain):
    weighted = e * gain
    mean = jnp.mean(weighted * n, axis=0, keepdims=True)
    return r * (weighted - n * mean), jnp.sum(e * n, axis=1, keepdims=True)


def rope(x, cosine, sine, sign):
    length = x.shape[1]
    x = x.reshape(HEADS, 2, 8, length)
    a, b = x[:, 0], x[:, 1]
    s = sine * sign
    first = a * cosine - b * s
    second = a * s + b * cosine
    return jnp.concatenate([first[:, None], second[:, None]], axis=1).reshape(HEADS, HEAD_DIM, length)


def kernel(
    median_ref, scale_ref, raw_ref, cot_ref, qkv_ref, out_ref, again_ref, gu_ref, down_ref, mgain_ref, cos_ref, sin_ref,
    result_ref, igrad_ref, qkvg_ref, outg_ref, againg_ref, gug_ref, downg_ref, mgaing_ref,
    e_ref, ds_ref, qa_ref, q_ref, k_ref, v_ref, o_ref, linv_ref, att_ref, datt_ref, dproj_ref, rows_ref, scaled_ref, dh_ref,
):
    length = raw_ref.shape[2]
    series = raw_ref.shape[0]
    slots = gu_ref.shape[0]
    nblk = length // BLK
    cosine, sine = cos_ref[...], sin_ref[...]
    again, mgain = to_column(again_ref[...]), to_column(mgain_ref[...])

    def spread_inverse(s):
        return 1.0 / jnp.full((1, length), scale_ref[s, 0].astype(F32) * 0.25, F32)

    ident = eye(D, BF)
    tail_rows = lax.broadcasted_iota(jnp.int32, (HEAD_DIM, length), 0)

    @pl.loop(0, series)
    def _(s):
        shift = median_ref[s, 0].astype(F32) * 0.05
        scaled = (mm_nt(ident, raw_ref[s, 0]) - shift) * spread_inverse(s)
        scaled_ref[s] = scaled
        n, _ = norm_stats(scaled)
        rows = (n * again).astype(BF)
        rows_ref[s] = rows
        projected = mm_tn(qkv_ref[...], rows)
        queries = rope(projected[:D], cosine, sine, 1.0).astype(BF)
        keys = rope(projected[D : 2 * D], cosine, sine, 1.0).astype(BF)
        values = projected[2 * D :].reshape(HEADS, HEAD_DIM, length).astype(BF)
        q_ref[s] = queries
        k_ref[s] = keys
        wide = queries.astype(F32) * LOG2E_SCALED
        high = wide.astype(BF)
        qa_ref[s, :, :HEAD_DIM] = high
        qa_ref[s, :, HEAD_DIM:] = (wide - high.astype(F32)).astype(BF)
        v_ref[s, :, :HEAD_DIM] = values
        ones = jnp.where(tail_rows < 2, 1.0, 0.0).astype(BF)
        v_ref[s, :, HEAD_DIM:] = jnp.broadcast_to(ones[None], (HEADS, HEAD_DIM, length))

    causal = lax.broadcasted_iota(jnp.int32, (BLK, BLK), 0) <= lax.broadcasted_iota(jnp.int32, (BLK, BLK), 1)

    def offset(j):
        return BLK * (j * (j + 1) // 2)

    @pl.loop(0, series)
    def _(s):
        @pl.loop(0, HEADS)
        def _(h):
            keys = k_ref[s, h]
            keys2 = jnp.concatenate([keys, keys], axis=0)
            for j in range(nblk):
                lo, hi = j * BLK, (j + 1) * BLK
                scores = mm_tn(keys2[:, :hi], qa_ref[s, h, :, lo:hi])
                diagonal = jnp.where(causal, scores[lo:], MASKED)
                scores = jnp.concatenate([scores[:lo], diagonal], axis=0) if j else diagonal
                largest = jnp.max(scores, axis=0, keepdims=True)
                e_ref[s * HEADS + h, offset(j) : offset(j) + hi] = jnp.exp2(scores - largest).astype(BF)
            for j in range(nblk):
                lo, hi = j * BLK, (j + 1) * BLK
                mixed = mm(v_ref[s, h, :, :hi], e_ref[s * HEADS + h, offset(j) : offset(j) + hi])
                inverse = 1.0 / mixed[HEAD_DIM : HEAD_DIM + 1]
                attended = mixed[:HEAD_DIM] * inverse
                linv_ref[s, h, :, lo:hi] = inverse
                o_ref[s, h, :, lo:hi] = attended
                att_ref[s, h, :, lo:hi] = attended.astype(BF)

    @pl.loop(0, series)
    def _(s):
        attended = att_ref[s].reshape(D, length)
        hidden = scaled_ref[s] + mm_tn(out_ref[...], attended)
        n, r = norm_stats(hidden)
        rows = (n * mgain).astype(BF)
        top = mm_nt(ident, cot_ref[s, 0])
        low = top.astype(BF)
        result = hidden
        grad_rows = jnp.zeros((D, length), F32)
        for t in range(slots):
            gu = gu_ref[t]
            both = mm_tn(gu, rows)
            half = both.shape[0] // 2
            gate, up = both[:half], both[half:]
            grad_inner = mm(down_ref[t], low)
            sigma = 1.0 / (1.0 + jnp.exp(-gate))
            act = gate * sigma
            inner = (act * up).astype(BF)
            grad_gate = (grad_inner * up * (sigma + act * (1.0 - sigma))).astype(BF)
            grad_up = (grad_inner * act).astype(BF)
            grad_both = jnp.concatenate([grad_gate, grad_up], axis=0)
            result = result + mm_tn(down_ref[t], inner)
            grad_rows = grad_rows + mm(gu, grad_both)
            gu_piece = mm_nt(rows, grad_both)
            down_piece = mm_nt(inner, low)

            @pl.when(s == 0)
            def _():
                gug_ref[t] = gu_piece
                downg_ref[t] = down_piece

            @pl.when(s != 0)
            def _():
                gug_ref[t] += gu_piece
                downg_ref[t] += down_piece

        result_ref[s, 0] = result.T.astype(BF)
        part, gain_part = norm_backward(grad_rows, n, r, mgain)
        grad_hidden = top + part
        dh_ref[s] = grad_hidden
        branch = grad_hidden.astype(BF)
        out_piece = mm_nt(attended, branch)
        gain_row = to_row(gain_part)
        datt_ref[s] = mm(out_ref[...], branch).astype(BF).reshape(HEADS, HEAD_DIM, length)

        @pl.when(s == 0)
        def _():
            outg_ref[...] = out_piece
            mgaing_ref[...] = gain_row

        @pl.when(s != 0)
        def _():
            outg_ref[...] += out_piece
            mgaing_ref[...] += gain_row

    @pl.loop(0, series)
    def _(s):
        @pl.loop(0, HEADS)
        def _(h):
            grad = (datt_ref[s, h].astype(F32) * linv_ref[s, h]).astype(BF)
            delta = -jnp.sum(grad.astype(F32) * o_ref[s, h], axis=0, keepdims=True)
            high = delta.astype(BF).astype(F32)
            tail = jnp.where(tail_rows == 0, high, jnp.where(tail_rows == 1, delta - high, 0.0))
            grad_all = jnp.concatenate([grad, tail.astype(BF)], axis=0)
            values = v_ref[s, h]
            queries, keys = q_ref[s, h], k_ref[s, h]
            for j in range(nblk):
                lo, hi = j * BLK, (j + 1) * BLK
                weights = e_ref[s * HEADS + h, offset(j) : offset(j) + hi]
                centred = mm_tn(values[:, :hi], grad_all[:, lo:hi])
                ds_ref[offset(j) : offset(j) + hi] = centred.astype(BF) * weights
            value_grads, key_grads, query_grads = [], [], []
            for j in range(nblk):
                lo, hi = j * BLK, (j + 1) * BLK
                query_grads.append(mm(keys[:, :hi], ds_ref[offset(j) : offset(j) + hi]))
            for i in range(nblk):
                value_grad = key_grad = None
                for j in range(i, nblk):
                    at = offset(j) + i * BLK
                    cols = slice(j * BLK, (j + 1) * BLK)
                    piece = mm_nt(grad[:, cols], e_ref[s * HEADS + h, at : at + BLK])
                    value_grad = piece if value_grad is None else value_grad + piece
                    piece = mm_nt(queries[:, cols], ds_ref[at : at + BLK])
                    key_grad = piece if key_grad is None else key_grad + piece
                value_grads.append(value_grad)
                key_grads.append(key_grad)

            def unrotate(g):
                a, b = g[:8], g[8:]
                return jnp.concatenate([a * cosine + b * sine, b * cosine - a * sine], axis=0)

            query_grad = jnp.concatenate(query_grads, axis=1) * 0.25
            key_grad = jnp.concatenate(key_grads, axis=1) * 0.25
            dproj_ref[s, h] = unrotate(query_grad).astype(BF)
            dproj_ref[s, HEADS + h] = unrotate(key_grad).astype(BF)
            dproj_ref[s, 2 * HEADS + h] = jnp.concatenate(value_grads, axis=1).astype(BF)

    @pl.loop(0, series)
    def _(s):
        grad = dproj_ref[s].reshape(3 * D, length)
        qkv_piece = mm_nt(rows_ref[s], grad)
        grad_rows = mm(qkv_ref[...], grad)
        n, r = norm_stats(scaled_ref[s])
        part, gain_part = norm_backward(grad_rows, n, r, again)
        igrad_ref[s, 0] = ((dh_ref[s] + part) * spread_inverse(s)).T
        gain_row = to_row(gain_part)

        @pl.when(s == 0)
        def _():
            qkvg_ref[...] = qkv_piece
            againg_ref[...] = gain_row

        @pl.when(s != 0)
        def _():
            qkvg_ref[...] += qkv_piece
            againg_ref[...] += gain_row


def rope_tables(length):
    half = HEAD_DIM // 2
    frequency = np.float32(10000.0) ** (-(np.arange(half, dtype=np.float32) * np.float32(2.0) / np.float32(HEAD_DIM)))
    angles = np.arange(length, dtype=np.float32)[None, :] * frequency.astype(np.float32)[:, None]
    return np.cos(angles).astype(np.float32), np.sin(angles).astype(np.float32)


def layer(median_code, scale_code, raw, cot, qkv, out, again, gu, down, mgain):
    series, _, length, width = raw.shape
    slots, _, pair = gu.shape
    cosine, sine = rope_tables(length)
    packed = BLK * (length // BLK) * (length // BLK + 1) // 2
    vmem = pl.BlockSpec(memory_space=pltpu.VMEM)
    smem = pl.BlockSpec(memory_space=pltpu.SMEM)
    per_head = (series, HEADS, HEAD_DIM, length)
    return pl.pallas_call(
        kernel,
        out_shape=[
            jax.ShapeDtypeStruct(raw.shape, BF),
            jax.ShapeDtypeStruct(raw.shape, F32),
            jax.ShapeDtypeStruct((width, 3 * width), F32),
            jax.ShapeDtypeStruct((width, width), F32),
            jax.ShapeDtypeStruct((1, width), F32),
            jax.ShapeDtypeStruct((slots, width, pair), F32),
            jax.ShapeDtypeStruct((slots, pair // 2, width), F32),
            jax.ShapeDtypeStruct((1, width), F32),
        ],
        in_specs=[smem, smem] + [vmem] * 10,
        out_specs=[vmem] * 8,
        scratch_shapes=[
            pltpu.VMEM((series * HEADS, packed, BLK), BF),
            pltpu.VMEM((packed, BLK), BF),
            pltpu.VMEM((series, HEADS, 2 * HEAD_DIM, length), BF),
            pltpu.VMEM(per_head, BF),
            pltpu.VMEM(per_head, BF),
            pltpu.VMEM((series, HEADS, 2 * HEAD_DIM, length), BF),
            pltpu.VMEM(per_head, F32),
            pltpu.VMEM((series, HEADS, 1, length), F32),
            pltpu.VMEM(per_head, BF),
            pltpu.VMEM(per_head, BF),
            pltpu.VMEM((series, 3 * HEADS, HEAD_DIM, length), BF),
            pltpu.VMEM((series, width, length), BF),
            pltpu.VMEM((series, width, length), F32),
            pltpu.VMEM((series, width, length), F32),
        ],
        compiler_params=pltpu.CompilerParams(vmem_limit_bytes=60 * 2**20),
    )(median_code, scale_code, raw, cot, qkv, out, again.reshape(1, -1), gu, down, mgain.reshape(1, -1), cosine, sine)


def local(raw_series, median_code, scale_code, qkv_weight, out_weight, attn_gain, gate_weight, up_weight, down_weight, mlp_gain, cotangent):
    gu = lax.all_gather(jnp.concatenate([gate_weight, up_weight], axis=1), "tensor")
    down = lax.all_gather(down_weight, "tensor")
    result, input_grad, qkv_grad, out_grad, again_grad, gu_grad, down_grad, mgain_grad = layer(
        median_code, scale_code, raw_series, cotangent, qkv_weight, out_weight, attn_gain, gu, down, mlp_gain
    )
    qkv_grad, out_grad, again_grad, mgain_grad = lax.psum((qkv_grad, out_grad, again_grad, mgain_grad), ("dp", "tensor"))
    gu_grad = lax.psum_scatter(gu_grad, "tensor", scatter_dimension=0, tiled=False)
    down_grad = lax.psum_scatter(down_grad, "tensor", scatter_dimension=0, tiled=False)
    gu_grad, down_grad = lax.psum((gu_grad, down_grad), "dp")
    half = gu_grad.shape[1] // 2
    return (
        result, input_grad, qkv_grad, out_grad, again_grad[0], gu_grad[:, :half], gu_grad[:, half:], down_grad, mgain_grad[0],
    )


def solution(mesh):
    placed = (
        P(None, ("dp", "tensor"), None, None), P(None, ("dp", "tensor")), P(None, ("dp", "tensor")), P(), P(), P(),
        P(None, "tensor"), P(None, "tensor"), P("tensor", None), P(), P(None, ("dp", "tensor"), None, None),
    )
    return jax.shard_map(
        local, mesh=mesh, in_specs=placed,
        out_specs=(
            P(None, ("dp", "tensor"), None, None), P(None, ("dp", "tensor"), None, None), P(), P(), P(),
            P(None, "tensor"), P(None, "tensor"), P("tensor", None), P(),
        ),
        check_vma=False,
    )
```

time: 1000 us -> 346 us (0.35)
  waiting for transfers between devices: 623 us -> 186 us
  matrix products: 161 us -> 0 us
  other arithmetic: 77.4 us -> 0.8 us
  Pallas kernels: 0 us -> 59.1 us
  local copies, waits for them, and re-layouts: 68.4 us -> 17.2 us
  blocking collectives: 41.4 us -> 68.1 us
    reduce_scatter x8 -> x2, waiting for transfers between devices: 276 us -> 43.9 us  [the longest x1 23.1 us: local(): lax.psum_scatter(gu_grad, 'tensor', scatter_dimension=0, tiled=False)]
    all_gather x8 -> x0, waiting for transfers between devices: 195 us -> none  [the longest x2 59 us: local(): rows_all = lax.all_gather(attn_rows, 'tensor', axis=0, tiled=True)]
    dot_general x144 -> x0, matrix products: 161 us -> none  [the longest x32 33 us: block_scores(): jnp.einsum('hqd,hkd->hqk', query_block, keys_rot[:, :key_end], preferred_...]
    pallas_call x0 -> x1, Pallas kernels: none -> 59.1 us  [layer(): pl.pallas_call(kernel, out_shape=[jax.ShapeDtypeStruct(raw.shape, BF), ja...]
    all_gather x0 -> x2, blocking collectives: none -> 29.4 us  [the longest x1 15.2 us: local(): lax.all_gather(jnp.concatenate([gate_weight, up_weight], axis=1), 'tensor')]
    reduce_sum x21 -> x0, other arithmetic: 28.8 us -> none  [the longest x16 20 us: series_forward(): summed = jnp.sum(weights, axis=-1, keepdims=True)]
    convert_element_type x19 -> x0, other arithmetic: 26.9 us -> none  [the longest x16 21.4 us: series_backward(): grad_scores = (probs * (grad_probs - row_delta)).astype(jnp.bfloat16)]
    squeeze x42 -> x0, local copies, waits for them, and re-layouts: 17.5 us -> none  [the longest x32 11.5 us: local(): attended, row_lse = lax.map(series_forward, (queries, keys_rot, values_in))]
  transfers between devices with their start and end apart: 18 -> 4, of which waited for: 16 -> 4; matrix products, arithmetic and copies ran while one was open for 16% -> 2% of each run, Pallas kernels for 0% -> 0%
where the time goes in v1:
time: 346 us; the launch traced here: 345 us
  waiting for transfers between devices  186 us (54%)
  blocking collectives  68.1 us (20%)
  Pallas kernels  59.1 us (17%)
  local copies, waits for them, and re-layouts  17.2 us (5%)
  between operations  13.8 us (4%)
    psum x1, waiting for transfers between devices, local(): lax.psum((qkv_grad, out_grad, again_grad, mgain_grad), ('dp', 'tensor'))  130 us
    pallas_call x1, Pallas kernels, layer(): pl.pallas_call(kernel, out_shape=[jax.ShapeDtypeStruct(raw.shape, BF), ja...  59.1 us
    psum x1, blocking collectives, local(): lax.psum((qkv_grad, out_grad, again_grad, mgain_grad), ('dp', 'tensor'))  38.7 us
    reduce_scatter x1, waiting for transfers between devices, local(): lax.psum_scatter(gu_grad, 'tensor', scatter_dimension=0, tiled=False)  23.1 us
    reduce_scatter x1, waiting for transfers between devices, local(): lax.psum_scatter(down_grad, 'tensor', scatter_dimension=0, tiled=False)  20.9 us
    all_gather x1, blocking collectives, local(): lax.all_gather(jnp.concatenate([gate_weight, up_weight], axis=1), 'tensor')  15.2 us
    unnamed x17, local copies, waits for them, and re-layouts  14.7 us
    all_gather x1, blocking collectives, local(): down = lax.all_gather(down_weight, 'tensor')  14.2 us
  transfers between devices with their start and end apart: 4, of which 4 were waited for; matrix products, arithmetic and copies ran while one was open for 2% of the time, Pallas kernels for 0%

profile of v1, /device:TPU:0, one launch (start us, length us, event | category | flops | bytes accessed | tf_op | source)
XLA Modules:
  0.0 345.2 jit_solution(13632100349118433597)
XLA Ops:
  7.2 0.0 copy-start.1
  7.2 0.0 reduce-scatter.5.cloned.1.call-start
  7.2 1.3 copy.23.median_ref
  8.6 1.3 copy.24.scale_ref
  9.9 14.2 %all-gather.1 = bf16[512,144]{0,1:T(8,128)(2,1)S(1)} all-gather(bf16[128,144]{0,1:T(8,128)(2,1)} %param.21), channel_id=3, replica_groups=mesh['dp'=8,'tensor'=4] {'tensor'}, dimensions={0}, use_global_device_ids=true | all-gather | bytes 184320 | tf_op jit(solution)/shard_map/all_gather | solution.py:307
  24.1 0.8 copy.22
  24.9 0.8 pad_maximum_fusion
  25.7 15.2 %all-gather = bf16[576,256]{1,0:T(8,128)(2,1)} all-gather(bf16[144,256]{1,0:T(8,128)(2,1)S(1)} %pad_maximum_fusion), channel_id=2, replica_groups=mesh['dp'=8,'tensor'=4] {'tensor'}, dimensions={0}, use_global_device_ids=true | all-gather | bytes 368640 | tf_op jit(solution)/shard_map/all_gather | solution.py:306
  40.9 2.2 copy.25.raw_ref
  43.1 0.0 copy-done.1
  43.1 1.3 copy.26.cot_ref
  44.4 59.1 %shard_map.196 = (bf16[2,1,1024,144]{3,2,1,0:T(8,128)(2,1)}, f32[2,1,1024,144]{3,2,1,0:T(8,128)}, f32[144,432]{1,0:T(8,128)}, f32[144,144]{1,0:T(8,128)}, f32[1,...) custom-call(s32[2,1]{1,0:T(2,128)} %copy.23.median_ref, ...), custom_call_target="tpu_custom_call" | custom-call | tf_op jit(solution)/shard_map/pallas_call | solution.py:271
  103.5 0.0 copy-start
  103.5 0.0 reduce-scatter.5.cloned.1.call-update
  103.5 0.0 reduce-scatter.3.cloned.1.call-start
  103.5 0.7 reduce-scatter.3.cloned.1.call-update
  104.2 0.0 all-reduce.8.cloned.1.call-start
  104.3 20.9 %reduce-scatter.5.cloned.1.call-done = f32[1,128,144]{2,1,0:T(8,128)} async-done(((f32[4,128,144]{2,1,0:T(8,128)}), f32[1,128,144]{2,1,0:T(8,128)}) %reduce-scatter.5.cloned.1.call-update) | async-done | bytes 73744 | tf_op jit(solution)/shard_map/reduce_scatter | solution.py:313
  125.2 23.1 %reduce-scatter.3.cloned.1.call-done = f32[1,144,256]{2,1,0:T(8,128)} async-done(((f32[4,144,256]{2,1,0:T(8,128)}), f32[1,144,256]{2,1,0:T(8,128)}) %reduce-scatter.3.cloned.1.call-update) | async-done | bytes 147472 | tf_op jit(solution)/shard_map/reduce_scatter | solution.py:312
  148.2 0.0 all-reduce.8.cloned.1.call-update
  148.3 0.0 all-reduce.6.cloned.1.call-start
  148.3 0.5 all-reduce.6.cloned.1.call-update
  148.8 0.0 copy-start.2
  148.9 0.0 copy-start.3
  148.9 2.1 copy.27
  151.0 0.0 copy-done
  151.0 1.6 copy.28
  152.6 0.0 copy-done.2
  152.6 0.0 copy-done.3
  152.6 38.7 %all-reduce = (f32[144]{0:T(256)}, f32[144]{0:T(256)}) all-reduce(f32[144]{0:T(256)S(1)} %bitcast.14, f32[144]{0:T(256)S(1)} %bitcast.15), channel_id=1, replica_groups=mesh['dp'=8,'tensor'=4] {'dp','tensor'}, use_global_device_ids=true, to_apply=%region_2.0 | all-reduce | flops 288 | bytes 2304 | tf_op jit(solution)/shard_map/psum | solution.py:311
  191.2 11.3 %all-reduce.8.cloned.1.call-done = (f32[144,256]{1,0:T(8,128)}, f32[128,144]{1,0:T(8,128)}) async-done(((f32[144,256]{1,0:T(8,128)}, f32[128,144]{1,0:T(8,128)}), (f32[144,256]{1,0:T(8,128)}, f32[128,144]{1,0:T(8,128)})) %all-reduce.8.cloned.1.call-update) | async-done | bytes 221200 | tf_op jit(solution)/shard_map/psum | solution.py:314
  202.6 1.6 copy.29
  204.2 1.6 fusion
  205.8 129.6 %all-reduce.6.cloned.1.call-done = (f32[144,432]{1,0:T(8,128)}, f32[144,144]{1,0:T(8,128)}) async-done(((f32[144,432]{1,0:T(8,128)}, f32[144,144]{1,0:T(8,128)}), (f32[144,432]{1,0:T(8,128)}, f32[144,144]{1,0:T(8,128)})) %all-reduce.6.cloned.1.call-update) | async-done | bytes 331792 | tf_op jit(solution)/shard_map/psum | solution.py:311
  335.4 1.7 copy.34
  337.1 1.6 copy.35
Async XLA Ops:
  7.2 35.9 %copy-start.1 = (bf16[2,1,1024,144]{2,3,1,0:T(8,128)(2,1)S(1)}, bf16[2,1,1024,144]{2,3,1,0:T(8,128)(2,1)}, u32[]{:S(2)}) copy-start(bf16[2,1,1024,144]{2,3,1,0:T(8,128)(2,1)} %param.23) | copy-start | bytes 1769476
  7.2 118.0 %reduce-scatter.5.cloned.1.call-start = ((), (), s32[]{:S(2)}) async-start(), calls=%async_computation.3 | async-start | bytes 655360 | tf_op jit(solution)/shard_map/reduce_scatter | solution.py:313
  103.5 47.5 %copy-start = (f32[2,1,1024,144]{3,2,1,0:T(8,128)S(1)}, f32[2,1,1024,144]{3,2,1,0:T(8,128)}, u32[]{:S(2)}) copy-start(f32[2,1,1024,144]{3,2,1,0:T(8,128)} %get-tuple-element.26) | copy-start | bytes 3538948
  103.5 44.7 %reduce-scatter.3.cloned.1.call-start = ((), (), s32[]{:S(2)}) async-start(), calls=%async_computation.2 | async-start | bytes 737280 | tf_op jit(solution)/shard_map/reduce_scatter | solution.py:312
  104.2 98.3 %all-reduce.8.cloned.1.call-start = ((), (), s32[]{:S(2)}) async-start(), calls=%async_computation.5 | async-start | bytes 557056 | tf_op jit(solution)/shard_map/psum | solution.py:314
  148.3 187.1 %all-reduce.6.cloned.1.call-start = ((), (), s32[]{:S(2)}) async-start(), calls=%async_computation.4 | async-start | bytes 884736 | tf_op jit(solution)/shard_map/psum | solution.py:311
  148.8 3.7 %copy-start.2 = (f32[1,144]{1,0:T(1,128)S(1)}, f32[1,144]{1,0:T(1,128)}, u32[]{:S(2)}) copy-start(f32[1,144]{1,0:T(1,128)} %get-tuple-element.21) | copy-start | bytes 1732
  148.9 3.7 %copy-start.3 = (f32[1,144]{1,0:T(1,128)S(1)}, f32[1,144]{1,0:T(1,128)}, u32[]{:S(2)}) copy-start(f32[1,144]{1,0:T(1,128)} %get-tuple-element.24) | copy-start | bytes 1732
Sparse Core Ops, SparseCore 0:
  103.6 21.4 reduce-scatter.4
  128.0 20.1 reduce-scatter.2
  151.5 51.0 all-reduce.7
  208.4 126.9 all-reduce.5

commit v2 on v1

--- a/solution.py
+++ b/solution.py
@@ -16,6 +16,9 @@
 BLK = 256
 EPS = 1e-05
 MASKED = -1e30
+EARLY = 7
+FF_AT = 4
+MESH = pl.DeviceIdType.MESH
 LOG2E_SCALED = 0.25 * 1.4426950408889634
 
 
@@ -67,28 +70,102 @@
     return jnp.concatenate([first[:, None], second[:, None]], axis=1).reshape(HEADS, HEAD_DIM, length)
 
 
+def group_owner_reduce(index, count, stage, recv, out, send_sem, recv_sem, spread_sem, gather_sem, to):
+    groups = stage.shape[0]
+
+    def part(owner):
+        return pltpu.make_async_remote_copy(
+            src_ref=stage.at[owner], dst_ref=recv.at[lax.rem(owner - index + count, count) - 1],
+            send_sem=send_sem.at[owner], recv_sem=recv_sem, device_id=to(owner), device_id_type=MESH,
+        )
+
+    def whole(k):
+        return pltpu.make_async_remote_copy(
+            src_ref=out.at[index], dst_ref=out.at[index], send_sem=spread_sem, recv_sem=gather_sem.at[index],
+            device_id=to(lax.rem(index + k, count)), device_id_type=MESH,
+        )
+
+    def each_other_owner(body):
+        @pl.loop(0, groups)
+        def _(owner):
+            @pl.when(owner != index)
+            def _():
+                body(owner)
+
+    def send():
+        each_other_owner(lambda owner: part(owner).start())
+
+    def reduce():
+        @pl.when(index < groups)
+        def _():
+            pltpu.make_async_remote_copy(
+                src_ref=recv, dst_ref=recv, send_sem=spread_sem, recv_sem=recv_sem, device_id=to(index), device_id_type=MESH,
+            ).wait_recv()
+            total = stage[index].astype(F32) + jnp.sum(recv[...].astype(F32), axis=0)
+            out[index] = total.astype(BF)
+
+            @pl.loop(1, count)
+            def _(k):
+                whole(k).start()
+
+    def finish():
+        def landed(owner):
+            pltpu.make_async_remote_copy(
+                src_ref=out.at[owner], dst_ref=out.at[owner], send_sem=spread_sem, recv_sem=gather_sem.at[owner],
+                device_id=to(owner), device_id_type=MESH,
+            ).wait_recv()
+
+        each_other_owner(landed)
+        each_other_owner(lambda owner: part(owner).wait_send())
+
+        @pl.when(index < groups)
+        def _():
+            pltpu.make_async_remote_copy(
+                src_ref=recv, dst_ref=recv, send_sem=spread_sem, recv_sem=recv_sem, device_id=to(index), device_id_type=MESH,
+            ).wait_send()
+
+    return send, reduce, finish
+
+
 def kernel(
-    median_ref, scale_ref, raw_ref, cot_ref, qkv_ref, out_ref, again_ref, gu_ref, down_ref, mgain_ref, cos_ref, sin_ref,
-    result_ref, igrad_ref, qkvg_ref, outg_ref, againg_ref, gug_ref, downg_ref, mgaing_ref,
+    n_dp, n_t,
+    median_ref, scale_ref, raw_ref, cot_ref, qkv_ref, out_ref, again_ref, gate_ref, up_ref, down_ref, mgain_ref, cos_ref, sin_ref,
+    result_ref, igrad_ref, qkvg_ref, outg_ref, againg_ref, gateg_ref, upg_ref, downg_ref, mgaing_ref,
     e_ref, ds_ref, qa_ref, q_ref, k_ref, v_ref, o_ref, linv_ref, att_ref, datt_ref, dproj_ref, rows_ref, scaled_ref, dh_ref,
+    w_ref, ffacc_ref, ffstage_ref, ffrecv_ref, ffout_ref, outacc_ref,
+    estage_ref, erecv_ref, eout_ref, lstage_ref, lrecv_ref, lout_ref, gains_ref,
+    w_send, w_recv, ff_send, ff_recv, ff_spread, ff_gather,
+    e_send, e_recv, e_spread, e_gather, l_send, l_recv, l_spread, l_gather,
 ):
-    length = raw_ref.shape[2]
+    length = raw_ref.shape[3]
     series = raw_ref.shape[0]
-    slots = gu_ref.shape[0]
     nblk = length // BLK
+    hidden_local = gate_ref.shape[1]
+    count = n_dp * n_t
+    my_dp, my_t = lax.axis_index("dp"), lax.axis_index("tensor")
+    index = my_dp * n_t + my_t
+
+    def to(device):
+        return (device // n_t, lax.rem(device, n_t))
+
+    barrier = pltpu.get_barrier_semaphore()
+
+    @pl.loop(1, count)
+    def _(k):
+        pl.semaphore_signal(barrier, inc=1, device_id=to(lax.rem(index + k, count)), device_id_type=MESH)
+
     cosine, sine = cos_ref[...], sin_ref[...]
     again, mgain = to_column(again_ref[...]), to_column(mgain_ref[...])
 
     def spread_inverse(s):
-        return 1.0 / jnp.full((1, length), scale_ref[s, 0].astype(F32) * 0.25, F32)
-
-    ident = eye(D, BF)
+        return 1.0 / jnp.full((1, length), scale_ref[0, s].astype(F32) * 0.25, F32)
+
     tail_rows = lax.broadcasted_iota(jnp.int32, (HEAD_DIM, length), 0)
 
     @pl.loop(0, series)
     def _(s):
-        shift = median_ref[s, 0].astype(F32) * 0.05
-        scaled = (mm_nt(ident, raw_ref[s, 0]) - shift) * spread_inverse(s)
+        shift = median_ref[0, s].astype(F32) * 0.05
+        scaled = (raw_ref[s, 0].astype(F32) - shift) * spread_inverse(s)
         scaled_ref[s] = scaled
         n, _ = norm_stats(scaled)
         rows = (n * again).astype(BF)
@@ -106,6 +183,20 @@
         v_ref[s, :, :HEAD_DIM] = values
         ones = jnp.where(tail_rows < 2, 1.0, 0.0).astype(BF)
         v_ref[s, :, HEAD_DIM:] = jnp.broadcast_to(ones[None], (HEADS, HEAD_DIM, length))
+
+    w_ref[0, :, :hidden_local] = gate_ref[...]
+    w_ref[0, :, hidden_local : 2 * hidden_local] = up_ref[...]
+    w_ref[0, :, 2 * hidden_local :] = down_ref[...]
+    pl.semaphore_wait(barrier, count - 1)
+
+    def weights(k):
+        return pltpu.make_async_remote_copy(
+            src_ref=w_ref.at[0], dst_ref=w_ref.at[k], send_sem=w_send.at[k], recv_sem=w_recv.at[k],
+            device_id=(my_dp, lax.rem(my_t + k, n_t)), device_id_type=MESH,
+        )
+
+    for k in range(1, n_t):
+        weights(k).start()
 
     causal = lax.broadcasted_iota(jnp.int32, (BLK, BLK), 0) <= lax.broadcasted_iota(jnp.int32, (BLK, BLK), 1)
 
@@ -134,66 +225,122 @@
                 o_ref[s, h, :, lo:hi] = attended
                 att_ref[s, h, :, lo:hi] = attended.astype(BF)
 
+    for k in range(1, n_t):
+        weights(k).wait()
+
+    ffacc_ref[...] = jnp.zeros_like(ffacc_ref)
+    outacc_ref[...] = jnp.zeros_like(outacc_ref)
+    gains_ref[...] = jnp.zeros_like(gains_ref)
+
     @pl.loop(0, series)
     def _(s):
         attended = att_ref[s].reshape(D, length)
         hidden = scaled_ref[s] + mm_tn(out_ref[...], attended)
         n, r = norm_stats(hidden)
         rows = (n * mgain).astype(BF)
-        top = mm_nt(ident, cot_ref[s, 0])
-        low = top.astype(BF)
+        low = cot_ref[s, 0]
+        top = low.astype(F32)
         result = hidden
         grad_rows = jnp.zeros((D, length), F32)
-        for t in range(slots):
-            gu = gu_ref[t]
+        for t in range(n_t):
+            gu = w_ref[t, :, : 2 * hidden_local]
+            down = w_ref[t, :, 2 * hidden_local :]
             both = mm_tn(gu, rows)
-            half = both.shape[0] // 2
-            gate, up = both[:half], both[half:]
-            grad_inner = mm(down_ref[t], low)
+            gate, up = both[:hidden_local], both[hidden_local:]
+            grad_inner = mm_tn(down, low)
             sigma = 1.0 / (1.0 + jnp.exp(-gate))
             act = gate * sigma
             inner = (act * up).astype(BF)
             grad_gate = (grad_inner * up * (sigma + act * (1.0 - sigma))).astype(BF)
             grad_up = (grad_inner * act).astype(BF)
             grad_both = jnp.concatenate([grad_gate, grad_up], axis=0)
-            result = result + mm_tn(down_ref[t], inner)
+            result = result + mm(down, inner)
             grad_rows = grad_rows + mm(gu, grad_both)
             gu_piece = mm_nt(rows, grad_both)
-            down_piece = mm_nt(inner, low)
-
-            @pl.when(s == 0)
-            def _():
-                gug_ref[t] = gu_piece
-                downg_ref[t] = down_piece
-
-            @pl.when(s != 0)
-            def _():
-                gug_ref[t] += gu_piece
-                downg_ref[t] += down_piece
-
-        result_ref[s, 0] = result.T.astype(BF)
+            ffacc_ref[t, :D] += gu_piece[:, :hidden_local]
+            ffacc_ref[t, D : 2 * D] += gu_piece[:, hidden_local:]
+            ffacc_ref[t, 2 * D : 3 * D] += mm_nt(low, inner)
+
+        result_ref[s, 0] = result.astype(BF)
         part, gain_part = norm_backward(grad_rows, n, r, mgain)
         grad_hidden = top + part
         dh_ref[s] = grad_hidden
         branch = grad_hidden.astype(BF)
-        out_piece = mm_nt(attended, branch)
-        gain_row = to_row(gain_part)
+        outacc_ref[...] += mm_nt(attended, branch)
+        gains_ref[0:1] += to_row(gain_part)
         datt_ref[s] = mm(out_ref[...], branch).astype(BF).reshape(HEADS, HEAD_DIM, length)
 
-        @pl.when(s == 0)
-        def _():
-            outg_ref[...] = out_piece
-            mgaing_ref[...] = gain_row
-
-        @pl.when(s != 0)
-        def _():
-            outg_ref[...] += out_piece
-            mgaing_ref[...] += gain_row
-
-    @pl.loop(0, series)
-    def _(s):
-        @pl.loop(0, HEADS)
-        def _(h):
+    ffstage_ref[...] = ffacc_ref[...].astype(BF).reshape(ffstage_ref.shape)
+
+    def ff_part(k):
+        peer = lax.rem(index + k, count)
+        peer_dp, peer_t = peer // n_t, lax.rem(peer, n_t)
+        return pltpu.make_async_remote_copy(
+            src_ref=ffstage_ref.at[lax.rem(my_t - peer_t + n_t, n_t), peer_dp], dst_ref=ffrecv_ref.at[k - 1],
+            send_sem=ff_send.at[k - 1], recv_sem=ff_recv, device_id=(peer_dp, peer_t), device_id_type=MESH,
+        )
+
+    def ff_whole(k):
+        return pltpu.make_async_remote_copy(
+            src_ref=ffout_ref.at[my_dp], dst_ref=ffout_ref.at[my_dp], send_sem=ff_spread.at[k - 1], recv_sem=ff_gather,
+            device_id=(lax.rem(my_dp + k, n_dp), my_t), device_id_type=MESH,
+        )
+
+    @pl.loop(1, count)
+    def _(k):
+        ff_part(k).start()
+
+    def ff_reduce():
+        pltpu.make_async_remote_copy(
+            src_ref=ffrecv_ref, dst_ref=ffrecv_ref, send_sem=ff_spread.at[0], recv_sem=ff_recv, device_id=to(index),
+            device_id_type=MESH,
+        ).wait_recv()
+        total = ffstage_ref[0, my_dp].astype(F32) + jnp.sum(ffrecv_ref[...].astype(F32), axis=0)
+        ffout_ref[my_dp] = total.astype(BF)
+
+        @pl.loop(1, n_dp)
+        def _(k):
+            ff_whole(k).start()
+
+    def ff_finish():
+        others = ffout_ref.at[pl.ds(0, n_dp - 1)]
+        pltpu.make_async_remote_copy(
+            src_ref=others, dst_ref=others, send_sem=ff_spread.at[0], recv_sem=ff_gather, device_id=to(index),
+            device_id_type=MESH,
+        ).wait_recv()
+
+        @pl.loop(1, count)
+        def _(k):
+            ff_part(k).wait_send()
+
+        @pl.loop(1, n_dp)
+        def _(k):
+            ff_whole(k).wait_send()
+
+    e_go, e_reduce, e_finish = group_owner_reduce(
+        index, count, estage_ref, erecv_ref, eout_ref, e_send, e_recv, e_spread, e_gather, to
+    )
+    l_go, l_reduce, l_finish = group_owner_reduce(
+        index, count, lstage_ref, lrecv_ref, lout_ref, l_send, l_recv, l_spread, l_gather, to
+    )
+
+    def head_grads(first, last):
+        total = None
+        for s in range(series):
+            parts = [dproj_ref[s, c * HEADS + first : c * HEADS + last] for c in range(3)]
+            grads = jnp.concatenate(parts, axis=0).reshape(3 * (last - first) * HEAD_DIM, length)
+            piece = mm_nt(grads, rows_ref[s])
+            total = piece if total is None else total + piece
+        return total.astype(BF).reshape(3 * (last - first), HEAD_DIM, D)
+
+    def gain_group(row):
+        first = lax.broadcasted_iota(jnp.int32, (HEAD_DIM, D), 0) == 0
+        return jnp.where(first, jnp.broadcast_to(row, (HEAD_DIM, D)), 0.0).astype(BF)
+
+    @pl.loop(0, HEADS)
+    def _(h):
+        @pl.loop(0, series)
+        def _(s):
             grad = (datt_ref[s, h].astype(F32) * linv_ref[s, h]).astype(BF)
             delta = -jnp.sum(grad.astype(F32) * o_ref[s, h], axis=0, keepdims=True)
             high = delta.astype(BF).astype(F32)
@@ -232,25 +379,48 @@
             dproj_ref[s, HEADS + h] = unrotate(key_grad).astype(BF)
             dproj_ref[s, 2 * HEADS + h] = jnp.concatenate(value_grads, axis=1).astype(BF)
 
+        @pl.when(h == FF_AT)
+        def _():
+            ff_reduce()
+
+        @pl.when(h == EARLY - 1)
+        def _():
+            estage_ref[0 : 3 * EARLY] = head_grads(0, EARLY)
+            estage_ref[3 * EARLY : 3 * EARLY + HEADS] = outacc_ref[...].astype(BF).reshape(HEADS, HEAD_DIM, D)
+            estage_ref[3 * EARLY + HEADS] = gain_group(gains_ref[0:1])
+            e_go()
+
+    late = 3 * (HEADS - EARLY)
+    lstage_ref[0:late] = head_grads(EARLY, HEADS)
+
     @pl.loop(0, series)
     def _(s):
         grad = dproj_ref[s].reshape(3 * D, length)
-        qkv_piece = mm_nt(rows_ref[s], grad)
         grad_rows = mm(qkv_ref[...], grad)
         n, r = norm_stats(scaled_ref[s])
         part, gain_part = norm_backward(grad_rows, n, r, again)
-        igrad_ref[s, 0] = ((dh_ref[s] + part) * spread_inverse(s)).T
-        gain_row = to_row(gain_part)
-
-        @pl.when(s == 0)
-        def _():
-            qkvg_ref[...] = qkv_piece
-            againg_ref[...] = gain_row
-
-        @pl.when(s != 0)
-        def _():
-            qkvg_ref[...] += qkv_piece
-            againg_ref[...] += gain_row
+        igrad_ref[s, 0] = (dh_ref[s] + part) * spread_inverse(s)
+        gains_ref[8:9] += to_row(gain_part)
+
+    lstage_ref[late] = gain_group(gains_ref[8:9])
+    l_go()
+    e_reduce()
+    l_reduce()
+    ff_finish()
+    ffout = ffout_ref[...].astype(F32).reshape(-1, hidden_local)
+    gateg_ref[...] = ffout[:D]
+    upg_ref[...] = ffout[D : 2 * D]
+    downg_ref[...] = ffout[2 * D : 3 * D]
+    e_finish()
+    outg_ref[...] = eout_ref[3 * EARLY : 3 * EARLY + HEADS].reshape(D, D).astype(F32)
+    mgaing_ref[...] = eout_ref[3 * EARLY + HEADS].astype(F32)[0:1]
+    l_finish()
+    againg_ref[...] = lout_ref[late].astype(F32)[0:1]
+    parts = []
+    for c in range(3):
+        parts.append(eout_ref[c * EARLY : (c + 1) * EARLY].reshape(EARLY * HEAD_DIM, D))
+        parts.append(lout_ref[c * (HEADS - EARLY) : (c + 1) * (HEADS - EARLY)].reshape((HEADS - EARLY) * HEAD_DIM, D))
+    qkvg_ref[...] = jnp.concatenate(parts, axis=0).astype(F32).T
 
 
 def rope_tables(length):
@@ -260,28 +430,36 @@
     return np.cos(angles).astype(np.float32), np.sin(angles).astype(np.float32)
 
 
-def layer(median_code, scale_code, raw, cot, qkv, out, again, gu, down, mgain):
-    series, _, length, width = raw.shape
-    slots, _, pair = gu.shape
+def layer(n_dp, n_t, median_code, scale_code, raw, cot, qkv, out, again, gate, up, down, mgain):
+    series, _, width, length = raw.shape
     cosine, sine = rope_tables(length)
-    packed = BLK * (length // BLK) * (length // BLK + 1) // 2
+    blocks = length // BLK
+    packed = BLK * blocks * (blocks + 1) // 2
     vmem = pl.BlockSpec(memory_space=pltpu.VMEM)
     smem = pl.BlockSpec(memory_space=pltpu.SMEM)
     per_head = (series, HEADS, HEAD_DIM, length)
+    count = n_dp * n_t
+    hidden = gate.shape[1]
+    share = -(-3 * width // (16 * n_dp)) * 16
+    early = 3 * EARLY + HEADS + 1
+    late = 3 * (HEADS - EARLY) + 1
+    dma = pltpu.SemaphoreType.DMA
+    group = (HEAD_DIM, width)
     return pl.pallas_call(
-        kernel,
+        functools.partial(kernel, n_dp, n_t),
         out_shape=[
             jax.ShapeDtypeStruct(raw.shape, BF),
             jax.ShapeDtypeStruct(raw.shape, F32),
             jax.ShapeDtypeStruct((width, 3 * width), F32),
             jax.ShapeDtypeStruct((width, width), F32),
             jax.ShapeDtypeStruct((1, width), F32),
-            jax.ShapeDtypeStruct((slots, width, pair), F32),
-            jax.ShapeDtypeStruct((slots, pair // 2, width), F32),
+            jax.ShapeDtypeStruct((width, hidden), F32),
+            jax.ShapeDtypeStruct((width, hidden), F32),
+            jax.ShapeDtypeStruct((width, hidden), F32),
             jax.ShapeDtypeStruct((1, width), F32),
         ],
-        in_specs=[smem, smem] + [vmem] * 10,
-        out_specs=[vmem] * 8,
+        in_specs=[smem, smem] + [vmem] * 11,
+        out_specs=[vmem] * 9,
         scratch_shapes=[
             pltpu.VMEM((series * HEADS, packed, BLK), BF),
             pltpu.VMEM((packed, BLK), BF),
@@ -297,24 +475,38 @@
             pltpu.VMEM((series, width, length), BF),
             pltpu.VMEM((series, width, length), F32),
             pltpu.VMEM((series, width, length), F32),
+            pltpu.VMEM((n_t, width, 3 * hidden), BF),
+            pltpu.VMEM((n_t, n_dp * share, hidden), F32),
+            pltpu.VMEM((n_t, n_dp, share, hidden), BF),
+            pltpu.VMEM((count - 1, share, hidden), BF),
+            pltpu.VMEM((n_dp, share, hidden), BF),
+            pltpu.VMEM((width, width), F32),
+            pltpu.VMEM((early,) + group, BF),
+            pltpu.VMEM((count - 1,) + group, BF),
+            pltpu.VMEM((early,) + group, BF),
+            pltpu.VMEM((late,) + group, BF),
+            pltpu.VMEM((count - 1,) + group, BF),
+            pltpu.VMEM((late,) + group, BF),
+            pltpu.VMEM((16, width), F32),
+            dma((n_t,)), dma((n_t,)), dma((count - 1,)), dma, dma((max(n_dp - 1, 1),)), dma,
+            dma((early,)), dma, dma, dma((early,)),
+            dma((late,)), dma, dma, dma((late,)),
         ],
-        compiler_params=pltpu.CompilerParams(vmem_limit_bytes=60 * 2**20),
-    )(median_code, scale_code, raw, cot, qkv, out, again.reshape(1, -1), gu, down, mgain.reshape(1, -1), cosine, sine)
-
-
-def local(raw_series, median_code, scale_code, qkv_weight, out_weight, attn_gain, gate_weight, up_weight, down_weight, mlp_gain, cotangent):
-    gu = lax.all_gather(jnp.concatenate([gate_weight, up_weight], axis=1), "tensor")
-    down = lax.all_gather(down_weight, "tensor")
-    result, input_grad, qkv_grad, out_grad, again_grad, gu_grad, down_grad, mgain_grad = layer(
-        median_code, scale_code, raw_series, cotangent, qkv_weight, out_weight, attn_gain, gu, down, mlp_gain
+        compiler_params=pltpu.CompilerParams(vmem_limit_bytes=60 * 2**20, collective_id=0, has_side_effects=True),
+    )(median_code, scale_code, raw, cot, qkv, out, again.reshape(1, -1), gate, up, down, mgain.reshape(1, -1), cosine, sine)
+
+
+def local(
+    n_dp, n_t, raw_series, median_code, scale_code, qkv_weight, out_weight, attn_gain, gate_weight, up_weight, down_weight,
+    mlp_gain, cotangent,
+):
+    result, input_grad, qkv_grad, out_grad, again_grad, gate_grad, up_grad, down_grad, mgain_grad = layer(
+        n_dp, n_t, median_code.T, scale_code.T, raw_series.transpose(0, 1, 3, 2), cotangent.transpose(0, 1, 3, 2), qkv_weight,
+        out_weight, attn_gain, gate_weight, up_weight, down_weight.T, mlp_gain,
     )
-    qkv_grad, out_grad, again_grad, mgain_grad = lax.psum((qkv_grad, out_grad, again_grad, mgain_grad), ("dp", "tensor"))
-    gu_grad = lax.psum_scatter(gu_grad, "tensor", scatter_dimension=0, tiled=False)
-    down_grad = lax.psum_scatter(down_grad, "tensor", scatter_dimension=0, tiled=False)
-    gu_grad, down_grad = lax.psum((gu_grad, down_grad), "dp")
-    half = gu_grad.shape[1] // 2
     return (
-        result, input_grad, qkv_grad, out_grad, again_grad[0], gu_grad[:, :half], gu_grad[:, half:], down_grad, mgain_grad[0],
+        result.transpose(0, 1, 3, 2), input_grad.transpose(0, 1, 3, 2), qkv_grad, out_grad, again_grad[0], gate_grad, up_grad,
+        down_grad.T, mgain_grad[0],
     )
 
 
@@ -324,7 +516,7 @@
         P(None, "tensor"), P(None, "tensor"), P("tensor", None), P(), P(None, ("dp", "tensor"), None, None),
     )
     return jax.shard_map(
-        local, mesh=mesh, in_specs=placed,
+        functools.partial(local, mesh.shape["dp"], mesh.shape["tensor"]), mesh=mesh, in_specs=placed,
         out_specs=(
             P(None, ("dp", "tensor"), None, None), P(None, ("dp", "tensor"), None, None), P(), P(), P(),
             P(None, "tensor"), P(None, "tensor"), P("tensor", None), P(),

time: 346 us -> 84.8 us (0.25)
  waiting for transfers between devices: 186 us -> 0 us
  blocking collectives: 68.1 us -> 0 us
  Pallas kernels: 59.1 us -> 76.5 us
  between operations: 13.8 us -> 0.69 us
  local copies, waits for them, and re-layouts: 17.2 us -> 7.47 us
    psum x2 -> x0, waiting for transfers between devices: 141 us -> none  [the longest x1 130 us: local(): lax.psum((qkv_grad, out_grad, again_grad, mgain_grad), ('dp', 'tensor'))]
    reduce_scatter x2 -> x0, waiting for transfers between devices: 43.9 us -> none  [the longest x1 23.1 us: local(): lax.psum_scatter(gu_grad, 'tensor', scatter_dimension=0, tiled=False)]
    psum x1 -> x0, blocking collectives: 38.7 us -> none  [local(): lax.psum((qkv_grad, out_grad, again_grad, mgain_grad), ('dp', 'tensor'))]
    all_gather x2 -> x0, blocking collectives: 29.4 us -> none  [the longest x1 15.2 us: local(): lax.all_gather(jnp.concatenate([gate_weight, up_weight], axis=1), 'tensor')]
    pallas_call x1, Pallas kernels: 59.1 us -> 76.5 us  [layer(): pl.pallas_call(functools.partial(kernel, n_dp, n_t), out_shape=[jax.Shape...]
    unnamed x17 -> x25, local copies, waits for them, and re-layouts: 14.7 us -> 7.47 us
  transfers between devices with their start and end apart: 4 -> 0, of which waited for: 4 -> 0; matrix products, arithmetic and copies ran while one was open for 2% -> 0% of each run, Pallas kernels for 0% -> 0%
where the time goes in v2:
time: 84.8 us; the launch traced here: 84.7 us
  Pallas kernels  76.5 us (90%)
  local copies, waits for them, and re-layouts  7.47 us (9%)
    pallas_call x1, Pallas kernels, layer(): pl.pallas_call(functools.partial(kernel, n_dp, n_t), out_shape=[jax.Shape...  76.5 us
    unnamed x25, local copies, waits for them, and re-layouts  7.47 us

profile of v2, /device:TPU:0, one launch (start us, length us, event | category | flops | bytes accessed | tf_op | source)
XLA Modules:
  0.0 84.7 jit_solution(7305579760830321259)
XLA Ops:
  0.6 76.5 %shard_map.196 = (bf16[2,1,144,1024]{3,2,1,0:T(8,128)(2,1)}, f32[2,1,144,1024]{3,2,1,0:T(8,128)}, f32[144,432]{1,0:T(8,128)}, f32[144,144]{1,0:T(8,128)}, f32[1,...) custom-call(s32[1,2]{1,0:T(1,128)} %bitcast.22, ...), custom_call_target="tpu_custom_call" | custom-call | tf_op jit(solution)/shard_map/pallas_call | solution.py:448
  77.2 0.0 copy-start
  77.2 2.0 %copy.31 = bf16[2,1,1024,144]{2,3,1,0:T(8,128)(2,1)} copy(bf16[2,1,1024,144]{2,3,1,0:T(8,128)(2,1)} %bitcast.15) | data formatting | bytes 1179648
  79.2 0.0 copy-done
  79.2 0.0 copy-start.1
  79.2 0.0 copy-start.2
  79.2 0.0 copy-start.7
  79.2 0.0 copy-start.5
  79.2 0.0 copy-start.4
  79.2 1.0 %copy.32 = f32[2,1,1024,144]{2,3,1,0:T(8,128)} copy(f32[2,1,1024,144]{2,3,1,0:T(8,128)S(1)} %bitcast.12) | data formatting | bytes 2359296
  80.2 0.0 copy-done.1
  80.2 0.0 copy-start.3
  80.2 0.0 copy-start.6
  80.2 0.7 copy.33
  81.0 0.0 copy-done.2
  81.0 0.7 copy.34
  81.6 0.0 copy-done.7
  81.6 0.6 copy.35
  82.2 0.0 copy-done.5
  82.2 0.6 copy.36
  82.8 0.0 copy-done.4
  82.8 0.6 copy.37
  83.5 0.0 copy-done.3
  83.5 0.6 copy.38
  84.1 0.0 copy-done.6
  84.1 0.6 copy.39
Async XLA Ops:
  77.2 2.0 %copy-start = (f32[2,1,144,1024]{3,2,1,0:T(8,128)S(1)}, f32[2,1,144,1024]{3,2,1,0:T(8,128)}, u32[]{:S(2)}) copy-start(f32[2,1,144,1024]{3,2,1,0:T(8,128)} %get-tuple-element.19) | copy-start | bytes 3538948
  79.2 1.1 %copy-start.1 = (f32[144,432]{1,0:T(8,128)S(1)}, f32[144,432]{1,0:T(8,128)}, u32[]{:S(2)}) copy-start(f32[144,432]{1,0:T(8,128)} %get-tuple-element.38) | copy-start | bytes 746500
  79.2 1.8 %copy-start.2 = (f32[144,144]{1,0:T(8,128)S(1)}, f32[144,144]{1,0:T(8,128)}, u32[]{:S(2)}) copy-start(f32[144,144]{1,0:T(8,128)} %get-tuple-element.39) | copy-start | bytes 248836
  79.2 2.4 %copy-start.7 = (f32[1,144]{1,0:T(1,128)S(1)}, f32[1,144]{1,0:T(1,128)}, u32[]{:S(2)}) copy-start(f32[1,144]{1,0:T(1,128)} %get-tuple-element.22) | copy-start | bytes 1732
  79.2 3.0 %copy-start.5 = (f32[144,128]{1,0:T(8,128)S(1)}, f32[144,128]{1,0:T(8,128)}, u32[]{:S(2)}) copy-start(f32[144,128]{1,0:T(8,128)} %get-tuple-element.41) | copy-start | bytes 221188
  79.2 3.6 %copy-start.4 = (f32[144,128]{1,0:T(8,128)S(1)}, f32[144,128]{1,0:T(8,128)}, u32[]{:S(2)}) copy-start(f32[144,128]{1,0:T(8,128)} %get-tuple-element.42) | copy-start | bytes 221188
  80.2 3.2 %copy-start.3 = (f32[144,128]{1,0:T(8,128)S(1)}, f32[144,128]{1,0:T(8,128)}, u32[]{:S(2)}) copy-start(f32[144,128]{1,0:T(8,128)} %get-tuple-element.25) | copy-start | bytes 221188
  80.2 3.9 %copy-start.6 = (f32[1,144]{1,0:T(1,128)S(1)}, f32[1,144]{1,0:T(1,128)}, u32[]{:S(2)}) copy-start(f32[1,144]{1,0:T(1,128)} %get-tuple-element.26) | copy-start | bytes 1732

commit v3 on v1

v3 whole, which is shorter than its diff:
```python
import functools

import jax
import jax.numpy as jnp
import numpy as np
from jax import lax
from jax.experimental import pallas as pl
from jax.experimental.pallas import tpu as pltpu
from jax.sharding import PartitionSpec as P

BF = jnp.bfloat16
F32 = jnp.float32
MESH = pl.DeviceIdType.MESH
HEADS = 9
HEAD_DIM = 16
D = HEADS * HEAD_DIM
LANES = 128
GROUPS = D // 16
BLK = 256
EPS = 1e-05
MASKED = -1e30
LOG2E_SCALED = 0.25 * 1.4426950408889634

STAGE1 = [(c, h) for c in range(3) for h in range(5)]
STAGE2 = [(c, h) for c in range(3) for h in range(5, 8)][:8]
STAGE3 = [(2, 7), (0, 8), (1, 8), (2, 8)]
TILES = (3, 1, 1)
OUT_AT = 16 * len(STAGE1)
GAIN_AT = 16 * len(STAGE3)


def mm(a, b):
    return lax.dot_general(a, b, (((1,), (0,)), ((), ())), preferred_element_type=F32)


def mm_tn(a, b):
    return lax.dot_general(a, b, (((0,), (0,)), ((), ())), preferred_element_type=F32)


def mm_nt(a, b):
    return lax.dot_general(a, b, (((1,), (1,)), ((), ())), preferred_element_type=F32)


def eye(n):
    same = lax.broadcasted_iota(jnp.int32, (n, n), 0) == lax.broadcasted_iota(jnp.int32, (n, n), 1)
    return jnp.where(same, 1.0, 0.0)


def to_column(row):
    return jnp.sum(eye(row.shape[1]) * row, axis=1, keepdims=True)


def to_row(column):
    return jnp.sum(eye(column.shape[0]) * column, axis=0, keepdims=True)


def norm_stats(rows):
    r = lax.rsqrt(jnp.mean(rows * rows, axis=0, keepdims=True) + EPS)
    return rows * r, r


def norm_backward(e, n, r, gain):
    weighted = e * gain
    mean = jnp.mean(weighted * n, axis=0, keepdims=True)
    return r * (weighted - n * mean), jnp.sum(e * n, axis=1, keepdims=True)


def rope(x, cosine, sine):
    length = x.shape[1]
    x = x.reshape(HEADS, 2, 8, length)
    a, b = x[:, 0], x[:, 1]
    first = a * cosine - b * sine
    second = a * sine + b * cosine
    return jnp.concatenate([first[:, None], second[:, None]], axis=1).reshape(HEADS, HEAD_DIM, length)


def each(first, last, body):
    if last - first <= 40:
        for k in range(first, last):
            body(k)
    else:
        pl.loop(first, last)(body)


def remote(src, dst, send_sem, recv_sem, device):
    return pltpu.make_async_remote_copy(
        src_ref=src, dst_ref=dst, send_sem=send_sem, recv_sem=recv_sem, device_id=device, device_id_type=MESH
    )


class GroupSum:
    def __init__(self, index, count, to, stage, recv, out, sems):
        self.index, self.count, self.to = index, count, to
        self.stage, self.recv, self.out = stage, recv, out
        self.send, self.land, self.spread, self.gather = (sems.at[i] for i in range(4))
        self.groups = stage.shape[0]
        self.stride = max(count // self.groups, 1)
        self.mine = index // self.stride
        self.owner = (lax.rem(index, self.stride) == 0) & (self.mine < self.groups)

    def go(self):
        def part(g):
            owner = g * self.stride

            @pl.when(owner != self.index)
            def _():
                slot = lax.rem(owner - self.index + self.count, self.count) - 1
                remote(self.stage.at[g], self.recv.at[slot], self.send, self.land, self.to(owner)).start()

        each(0, self.groups, part)

    def _all_parts(self):
        return remote(self.recv, self.recv, self.spread, self.land, self.to(self.index))

    def reduce(self):
        @pl.when(self.owner)
        def _():
            self._all_parts().wait_recv()
            total = self.stage[self.mine].astype(F32) + jnp.sum(self.recv[...].astype(F32), axis=0)
            self.out[self.mine] = total.astype(BF)

            def whole(k):
                device = self.to(lax.rem(self.index + k, self.count))
                remote(self.out.at[self.mine], self.out.at[self.mine], self.spread, self.gather, device).start()

            each(1, self.count, whole)

    def finish(self):
        def landed(n):
            stage, out = self.stage.at[pl.ds(0, n)], self.out.at[pl.ds(0, n)]
            both = remote(stage, out, self.send, self.gather, self.to(self.index))
            both.wait_recv()
            both.wait_send()

        @pl.when(self.owner)
        def _():
            if self.groups > 1:
                landed(self.groups - 1)
            self._all_parts().wait_send()

        @pl.when(jnp.logical_not(self.owner))
        def _():
            landed(self.groups)


def kernel(
    n_dp, n_t,
    median_ref, scale_ref, raw_hbm, cot_hbm, qkv_ref, out_ref, again_ref, gate_ref, up_ref, down_ref, mgain_ref, cos_ref, sin_ref,
    source_ref,
    result_hbm, igrad_hbm, qkvg_ref, outg_ref, againg_ref, gateg_ref, upg_ref, downg_ref, mgaing_ref,
    raw_ref, cot_ref, result_ref, igrad_ref,
    e_ref, ds_ref, qa_ref, q_ref, k_ref, v_ref, o_ref, linv_ref, att_ref, datt_ref, dproj_ref, rows_ref, scaled_ref, dh_ref,
    w_ref, ffacc_ref, ffstage_ref, ffpair_ref, ffhalf_ref, ffrecv_ref, ffout_ref, outacc_ref, gains_ref,
    stage1, recv1, out1, stage2, recv2, out2, stage3, recv3, out3,
    local_sem, w_send, w_recv, w_send2, w_recv2, ff_sem, sems1, sems2, sems3,
):
    series, _, _, length = raw_hbm.shape
    nblk = length // BLK
    hidden_local = gate_ref.shape[1]
    count = n_dp * n_t
    my_dp, my_t = lax.axis_index("dp"), lax.axis_index("tensor")
    index = my_dp * n_t + my_t
    core = lax.rem(my_dp, 2)
    pair = my_dp // 2
    partner = (my_dp + 1 - 2 * core, my_t)
    pairs = n_dp // 2

    def to(device):
        return (device // n_t, lax.rem(device, n_t))

    loads = [pltpu.make_async_copy(raw_hbm.at[s, 0], raw_ref.at[s], local_sem.at[s]) for s in range(series)]
    loads += [pltpu.make_async_copy(cot_hbm.at[s, 0], cot_ref.at[s], local_sem.at[series + s]) for s in range(series)]
    for copy in loads:
        copy.start()

    barrier = pltpu.get_barrier_semaphore()

    def greet(k):
        pl.semaphore_signal(barrier, inc=1, device_id=to(lax.rem(index + k, count)), device_id_type=MESH)

    each(1, count, greet)

    cosine, sine = cos_ref[...], sin_ref[...]
    again, mgain = to_column(again_ref[...]), to_column(mgain_ref[...])

    def spread_inverse(s):
        return 1.0 / jnp.full((1, length), scale_ref[0, s].astype(F32) * 0.25, F32)

    tail_rows = lax.broadcasted_iota(jnp.int32, (HEAD_DIM, length), 0)
    w_ref[0, :, :hidden_local] = gate_ref[...]
    w_ref[0, :, hidden_local : 2 * hidden_local] = up_ref[...]
    w_ref[0, :, 2 * hidden_local :] = down_ref[...]
    for copy in loads:
        copy.wait()

    @pl.loop(0, series)
    def _(s):
        shift = median_ref[0, s].astype(F32) * 0.05
        scaled = (raw_ref[s].astype(F32) - shift) * spread_inverse(s)
        scaled_ref[s] = scaled
        n, _ = norm_stats(scaled)
        rows = (n * again).astype(BF)
        rows_ref[s] = rows
        projected = mm_tn(qkv_ref[...], rows)
        queries = rope(projected[:D], cosine, sine).astype(BF)
        keys = rope(projected[D : 2 * D], cosine, sine).astype(BF)
        values = projected[2 * D :].reshape(HEADS, HEAD_DIM, length).astype(BF)
        q_ref[s] = queries
        k_ref[s] = keys
        wide = queries.astype(F32) * LOG2E_SCALED
        high = wide.astype(BF)
        qa_ref[s, :, :HEAD_DIM] = high
        qa_ref[s, :, HEAD_DIM:] = (wide - high.astype(F32)).astype(BF)
        v_ref[s, :, :HEAD_DIM] = values
        ones = jnp.where(tail_rows < 2, 1.0, 0.0).astype(BF)
        v_ref[s, :, HEAD_DIM:] = jnp.broadcast_to(ones[None], (HEADS, HEAD_DIM, length))

    cut = 16 * ((GROUPS + 1) // 2)

    def half_rows(which, body):
        for c, (lo, hi) in enumerate(((0, cut), (cut, D))):
            @pl.when(core == (c if which == 0 else 1 - c))
            def _():
                body(pl.ds(lo, hi - lo))

    def over_links(k, rows):
        device = (my_dp, lax.rem(my_t + k, n_t))
        return remote(w_ref.at[0, rows], w_ref.at[k, rows], w_send.at[k], w_recv.at[k], device)

    def within_pair(k, rows):
        return remote(w_ref.at[k, rows], w_ref.at[k, rows], w_send2.at[k], w_recv2.at[k], partner)

    def send_weights():
        pl.semaphore_wait(barrier, count - 1)

        def start(rows):
            for k in range(1, n_t):
                over_links(k, rows).start()

        half_rows(0, start)

    def exchange_weights():
        def forward(rows):
            for k in range(1, n_t):
                over_links(k, rows).wait()
                within_pair(k, rows).start()

        half_rows(0, forward)

    def finish_weights():
        def sent(rows):
            for k in range(1, n_t):
                within_pair(k, rows).wait_send()

        def landed(rows):
            for k in range(1, n_t):
                within_pair(k, rows).wait_recv()

        half_rows(0, sent)
        half_rows(1, landed)

    causal = lax.broadcasted_iota(jnp.int32, (BLK, BLK), 0) <= lax.broadcasted_iota(jnp.int32, (BLK, BLK), 1)

    def offset(j):
        return BLK * (j * (j + 1) // 2)

    @pl.loop(0, series)
    def _(s):
        @pl.loop(0, HEADS)
        def _(h):
            keys = k_ref[s, h]
            keys2 = jnp.concatenate([keys, keys], axis=0)
            for j in range(nblk):
                lo, hi = j * BLK, (j + 1) * BLK
                scores = mm_tn(keys2[:, :hi], qa_ref[s, h, :, lo:hi])
                diagonal = jnp.where(causal, scores[lo:], MASKED)
                scores = jnp.concatenate([scores[:lo], diagonal], axis=0) if j else diagonal
                largest = jnp.max(scores, axis=0, keepdims=True)
                e_ref[s * HEADS + h, offset(j) : offset(j) + hi] = jnp.exp2(scores - largest).astype(BF)
            for j in range(nblk):
                lo, hi = j * BLK, (j + 1) * BLK
                mixed = mm(v_ref[s, h, :, :hi], e_ref[s * HEADS + h, offset(j) : offset(j) + hi])
                inverse = 1.0 / mixed[HEAD_DIM : HEAD_DIM + 1]
                attended = mixed[:HEAD_DIM] * inverse
                linv_ref[s, h, :, lo:hi] = inverse
                o_ref[s, h, :, lo:hi] = attended
                att_ref[s, h, :, lo:hi] = attended.astype(BF)

            @pl.when((s == 0) & (h == 5))
            def _():
                send_weights()

            @pl.when((s == series - 1) & (h == 5))
            def _():
                exchange_weights()

    finish_weights()

    ffacc_ref[...] = jnp.zeros_like(ffacc_ref)
    outacc_ref[...] = jnp.zeros_like(outacc_ref)
    gains_ref[...] = jnp.zeros_like(gains_ref)

    @pl.loop(0, series)
    def _(s):
        attended = att_ref[s].reshape(D, length)
        hidden = scaled_ref[s] + mm_tn(out_ref[...], attended)
        n, r = norm_stats(hidden)
        rows = (n * mgain).astype(BF)
        low = cot_ref[s]
        top = low.astype(F32)
        result = hidden
        grad_rows = jnp.zeros((D, length), F32)
        for t in range(n_t):
            gu = w_ref[t, :, : 2 * hidden_local]
            down = w_ref[t, :, 2 * hidden_local :]
            both = mm_tn(gu, rows)
            gate, up = both[:hidden_local], both[hidden_local:]
            grad_inner = mm_tn(down, low)
            sigma = 1.0 / (1.0 + jnp.exp(-gate))
            act = gate * sigma
            inner = (act * up).astype(BF)
            grad_gate = (grad_inner * up * (sigma + act * (1.0 - sigma))).astype(BF)
            grad_up = (grad_inner * act).astype(BF)
            grad_both = jnp.concatenate([grad_gate, grad_up], axis=0)
            result = result + mm(down, inner)
            grad_rows = grad_rows + mm(gu, grad_both)
            gu_piece = mm_nt(rows, grad_both)
            ffacc_ref[t, :D] += gu_piece[:, :hidden_local]
            ffacc_ref[t, D : 2 * D] += gu_piece[:, hidden_local:]
            ffacc_ref[t, 2 * D : 3 * D] += mm_nt(low, inner)

        result_ref[s] = result.astype(BF)
        part, gain_part = norm_backward(grad_rows, n, r, mgain)
        grad_hidden = top + part
        dh_ref[s] = grad_hidden
        branch = grad_hidden.astype(BF)
        outacc_ref[...] += mm_nt(attended, branch)
        gains_ref[:, 1:2] += gain_part
        datt_ref[s] = mm(out_ref[...], branch).astype(BF).reshape(HEADS, HEAD_DIM, length)

    def store_result(s):
        return pltpu.make_async_copy(result_ref.at[s], result_hbm.at[s, 0], local_sem.at[s])

    def store_igrad(s):
        return pltpu.make_async_copy(igrad_ref.at[s], igrad_hbm.at[s, 0], local_sem.at[series + s])

    for s in range(series):
        store_result(s).start()

    share = ffout_ref.shape[1]
    for t in range(n_t):
        staged = ffacc_ref[t].astype(BF).reshape(pairs, 2, share, hidden_local)
        for c in range(2):
            ffstage_ref[c, t] = staged[:, c]
    peers = pairs * n_t
    place = pair * n_t + my_t

    def ff_pair():
        return remote(ffstage_ref.at[1 - core], ffpair_ref, ff_sem.at[0], ff_sem.at[1], partner)

    ff_pair().start()

    def ff_send():
        ff_pair().wait()
        ffhalf_ref[...] = (ffstage_ref[core].astype(F32) + ffpair_ref[...].astype(F32)).astype(BF)

        def part(k):
            peer = lax.rem(place + k, peers)
            peer_pair, peer_t = peer // n_t, lax.rem(peer, n_t)
            piece = ffhalf_ref.at[lax.rem(my_t - peer_t + n_t, n_t), peer_pair]
            remote(piece, ffrecv_ref.at[k - 1], ff_sem.at[2], ff_sem.at[3], (2 * peer_pair + core, peer_t)).start()

        each(1, peers, part)

    def ff_parts():
        return remote(ffrecv_ref, ffrecv_ref, ff_sem.at[2], ff_sem.at[3], to(index))

    def ff_reduce():
        ff_parts().wait_recv()
        total = ffhalf_ref[0, pair].astype(F32) + jnp.sum(ffrecv_ref[...].astype(F32), axis=0)
        ffout_ref[my_dp] = total.astype(BF)

        def whole(k):
            device = (lax.rem(my_dp + k, n_dp), my_t)
            remote(ffout_ref.at[my_dp], ffout_ref.at[my_dp], ff_sem.at[4], ff_sem.at[5], device).start()

        each(1, n_dp, whole)

    def ff_finish():
        ff_parts().wait_send()
        others = ffout_ref.at[pl.ds(0, n_dp - 1)]
        remote(others, others, ff_sem.at[4], ff_sem.at[5], to(index)).wait()
        sums = ffout_ref[...].astype(F32).reshape(-1, hidden_local)
        gateg_ref[...] = sums[:D]
        upg_ref[...] = sums[D : 2 * D]
        downg_ref[...] = sums[2 * D : 3 * D]

    sum1 = GroupSum(index, count, to, stage1, recv1, out1, sems1)
    sum2 = GroupSum(index, count, to, stage2, recv2, out2, sems2)
    sum3 = GroupSum(index, count, to, stage3, recv3, out3, sems3)

    def head_grads(parts):
        total = None
        for s in range(series):
            grads = jnp.concatenate([dproj_ref[s, c * HEADS + h] for c, h in parts], axis=0)
            piece = mm_nt(rows_ref[s], grads)
            total = piece if total is None else total + piece
        return total

    def put(stage, grads):
        for t in range(grads.shape[1] // LANES):
            tile = grads[:, t * LANES : (t + 1) * LANES].astype(BF)
            stage[t * GROUPS : (t + 1) * GROUPS] = tile.reshape(GROUPS, 16, LANES)

    @pl.loop(0, HEADS)
    def _(h):
        @pl.loop(0, series)
        def _(s):
            grad = (datt_ref[s, h].astype(F32) * linv_ref[s, h]).astype(BF)
            delta = -jnp.sum(grad.astype(F32) * o_ref[s, h], axis=0, keepdims=True)
            high = delta.astype(BF).astype(F32)
            tail = jnp.where(tail_rows == 0, high, jnp.where(tail_rows == 1, delta - high, 0.0))
            grad_all = jnp.concatenate([grad, tail.astype(BF)], axis=0)
            values = v_ref[s, h]
            queries, keys = q_ref[s, h], k_ref[s, h]
            for j in range(nblk):
                lo, hi = j * BLK, (j + 1) * BLK
                weights = e_ref[s * HEADS + h, offset(j) : offset(j) + hi]
                centred = mm_tn(values[:, :hi], grad_all[:, lo:hi])
                ds_ref[offset(j) : offset(j) + hi] = centred.astype(BF) * weights
            value_grads, key_grads, query_grads = [], [], []
            for j in range(nblk):
                lo, hi = j * BLK, (j + 1) * BLK
                query_grads.append(mm(keys[:, :hi], ds_ref[offset(j) : offset(j) + hi]))
            for i in range(nblk):
                value_grad = key_grad = None
                for j in range(i, nblk):
                    at = offset(j) + i * BLK
                    cols = slice(j * BLK, (j + 1) * BLK)
                    piece = mm_nt(grad[:, cols], e_ref[s * HEADS + h, at : at + BLK])
                    value_grad = piece if value_grad is None else value_grad + piece
                    piece = mm_nt(queries[:, cols], ds_ref[at : at + BLK])
                    key_grad = piece if key_grad is None else key_grad + piece
                value_grads.append(value_grad)
                key_grads.append(key_grad)

            def unrotate(g):
                a, b = g[:8], g[8:]
                return jnp.concatenate([a * cosine + b * sine, b * cosine - a * sine], axis=0)

            query_grad = jnp.concatenate(query_grads, axis=1) * 0.25
            key_grad = jnp.concatenate(key_grads, axis=1) * 0.25
            dproj_ref[s, h] = unrotate(query_grad).astype(BF)
            dproj_ref[s, HEADS + h] = unrotate(key_grad).astype(BF)
            dproj_ref[s, 2 * HEADS + h] = jnp.concatenate(value_grads, axis=1).astype(BF)

        @pl.when(h == 0)
        def _():
            ff_send()

        @pl.when(h == 4)
        def _():
            ff_reduce()
            put(stage1, jnp.concatenate([head_grads(STAGE1), outacc_ref[...]], axis=1))
            sum1.go()

        @pl.when(h == 6)
        def _():
            sum1.reduce()

        @pl.when(h == 7)
        def _():
            put(stage2, head_grads(STAGE2))
            sum2.go()

    @pl.loop(0, series)
    def _(s):
        grad = dproj_ref[s].reshape(3 * D, length)
        grad_rows = mm(qkv_ref[...], grad)
        n, r = norm_stats(scaled_ref[s])
        part, gain_part = norm_backward(grad_rows, n, r, again)
        igrad_ref[s] = (dh_ref[s] + part) * spread_inverse(s)
        gains_ref[:, 0:1] += gain_part

    last = head_grads(STAGE3)
    put(stage3, jnp.concatenate([last, gains_ref[:, : LANES - GAIN_AT]], axis=1))
    sum3.go()
    for s in range(series):
        store_igrad(s).start()
    sum2.reduce()
    ff_finish()
    sum1.finish()
    place_of = jnp.where(
        lax.broadcasted_iota(jnp.int32, (sum(TILES) * LANES, source_ref.shape[1]), 0) == source_ref[...], 1.0, 0.0
    ).astype(BF)
    sum3.reduce()
    sum2.finish()
    for s in range(series):
        store_result(s).wait()
        store_igrad(s).wait()
    sum3.finish()
    tiles = []
    for out, n in zip((out1, out2, out3), TILES, strict=True):
        tiles += [out[t * GROUPS : (t + 1) * GROUPS].reshape(D, LANES) for t in range(n)]
    sums = mm(jnp.concatenate(tiles, axis=1), place_of)
    qkvg_ref[...] = sums[:, : 3 * D]
    outg_ref[...] = sums[:, 4 * LANES : 4 * LANES + D]
    againg_ref[...] = to_row(tiles[-1][:, GAIN_AT : GAIN_AT + 1].astype(F32))
    mgaing_ref[...] = to_row(tiles[-1][:, GAIN_AT + 1 : GAIN_AT + 2].astype(F32))


def rope_tables(length):
    half = HEAD_DIM // 2
    frequency = np.float32(10000.0) ** (-(np.arange(half, dtype=np.float32) * np.float32(2.0) / np.float32(HEAD_DIM)))
    angles = np.arange(length, dtype=np.float32)[None, :] * frequency.astype(np.float32)[:, None]
    return np.cos(angles).astype(np.float32), np.sin(angles).astype(np.float32)


def column_sources():
    source = np.full((1, 4 * LANES + D), -1, np.int32)
    first = 0
    for parts, tiles in zip((STAGE1, STAGE2, STAGE3), TILES, strict=True):
        for place, (c, h) in enumerate(parts):
            at = c * D + h * HEAD_DIM
            source[0, at : at + HEAD_DIM] = first + place * HEAD_DIM + np.arange(HEAD_DIM)
        first += tiles * LANES
    source[0, 4 * LANES :] = OUT_AT + np.arange(D)
    return source


def copy_kernel(n, *refs):
    sources, results, held, sems = refs[:n], refs[n : 2 * n], refs[2 * n : 3 * n], refs[3 * n]
    takes = [pltpu.make_async_copy(sources[i], held[i], sems.at[0, i]) for i in range(n)]
    gives = [pltpu.make_async_copy(held[i], results[i], sems.at[1, i]) for i in range(n)]
    for copy in takes:
        copy.start()
    for take, give in zip(takes, gives, strict=True):
        take.wait()
        give.start()
    for copy in gives:
        copy.wait()


def hand_over(arrays):
    n = len(arrays)
    place = pl.BlockSpec(memory_space=pltpu.HBM)
    return pl.pallas_call(
        functools.partial(copy_kernel, n),
        out_shape=[jax.ShapeDtypeStruct(a.shape, a.dtype) for a in arrays],
        in_specs=[place] * n,
        out_specs=[place] * n,
        scratch_shapes=[pltpu.VMEM(a.shape, a.dtype) for a in arrays] + [pltpu.SemaphoreType.DMA((2, n))],
    )(*arrays)


def layer(n_dp, n_t, median_code, scale_code, raw, cot, qkv, out, again, gate, up, down, mgain):
    series, _, width, length = raw.shape
    cosine, sine = rope_tables(length)
    source = column_sources()
    blocks = length // BLK
    packed = BLK * blocks * (blocks + 1) // 2
    vmem = pl.BlockSpec(memory_space=pltpu.VMEM)
    smem = pl.BlockSpec(memory_space=pltpu.SMEM)
    anywhere = pl.BlockSpec(memory_space=pl.ANY)
    per_head = (series, HEADS, HEAD_DIM, length)
    rows = (series, width, length)
    count = n_dp * n_t
    pairs = n_dp // 2
    hidden = gate.shape[1]
    share = -(-3 * width // (16 * n_dp)) * 16
    dma = pltpu.SemaphoreType.DMA
    stages = []
    for n in TILES:
        stages += [
            pltpu.VMEM((n * GROUPS, 16, LANES), BF), pltpu.VMEM((count - 1, 16, LANES), BF), pltpu.VMEM((n * GROUPS, 16, LANES), BF),
        ]
    return pl.pallas_call(
        functools.partial(kernel, n_dp, n_t),
        out_shape=[
            jax.ShapeDtypeStruct(raw.shape, BF),
            jax.ShapeDtypeStruct(raw.shape, F32),
            jax.ShapeDtypeStruct((width, 3 * width), F32),
            jax.ShapeDtypeStruct((width, width), F32),
            jax.ShapeDtypeStruct((1, width), F32),
            jax.ShapeDtypeStruct((width, hidden), F32),
            jax.ShapeDtypeStruct((width, hidden), F32),
            jax.ShapeDtypeStruct((width, hidden), F32),
            jax.ShapeDtypeStruct((1, width), F32),
        ],
        in_specs=[smem, smem, anywhere, anywhere] + [vmem] * 10,
        out_specs=[anywhere, anywhere] + [vmem] * 7,
        scratch_shapes=[
            pltpu.VMEM(rows, BF),
            pltpu.VMEM(rows, BF),
            pltpu.VMEM(rows, BF),
            pltpu.VMEM(rows, F32),
            pltpu.VMEM((series * HEADS, packed, BLK), BF),
            pltpu.VMEM((packed, BLK), BF),
            pltpu.VMEM((series, HEADS, 2 * HEAD_DIM, length), BF),
            pltpu.VMEM(per_head, BF),
            pltpu.VMEM(per_head, BF),
            pltpu.VMEM((series, HEADS, 2 * HEAD_DIM, length), BF),
            pltpu.VMEM(per_head, F32),
            pltpu.VMEM((series, HEADS, 1, length), F32),
            pltpu.VMEM(per_head, BF),
            pltpu.VMEM(per_head, BF),
            pltpu.VMEM((series, 3 * HEADS, HEAD_DIM, length), BF),
            pltpu.VMEM(rows, BF),
            pltpu.VMEM(rows, F32),
            pltpu.VMEM(rows, F32),
            pltpu.VMEM((n_t, width, 3 * hidden), BF),
            pltpu.VMEM((n_t, n_dp * share, hidden), F32),
            pltpu.VMEM((2, n_t, pairs, share, hidden), BF),
            pltpu.VMEM((n_t, pairs, share, hidden), BF),
            pltpu.VMEM((n_t, pairs, share, hidden), BF),
            pltpu.VMEM((pairs * n_t - 1, share, hidden), BF),
            pltpu.VMEM((n_dp, share, hidden), BF),
            pltpu.VMEM((width, width), F32),
            pltpu.VMEM((width, LANES), F32),
            *stages,
            dma((2 * series,)), dma((n_t,)), dma((n_t,)), dma((n_t,)), dma((n_t,)), dma((6,)), dma((4,)), dma((4,)), dma((4,)),
        ],
        compiler_params=pltpu.CompilerParams(vmem_limit_bytes=60 * 2**20, collective_id=0, has_side_effects=True),
    )(
        median_code, scale_code, raw, cot, qkv, out, again.reshape(1, -1), gate, up, down, mgain.reshape(1, -1), cosine, sine, source
    )


def local(
    n_dp, n_t, raw_series, median_code, scale_code, qkv_weight, out_weight, attn_gain, gate_weight, up_weight, down_weight,
    mlp_gain, cotangent,
):
    result, input_grad, qkv_grad, out_grad, again_grad, gate_grad, up_grad, down_grad, mgain_grad = hand_over(layer(
        n_dp, n_t, median_code.T, scale_code.T, raw_series.transpose(0, 1, 3, 2), cotangent.transpose(0, 1, 3, 2), qkv_weight,
        out_weight, attn_gain, gate_weight, up_weight, down_weight.T, mlp_gain,
    ))
    return (
        result.transpose(0, 1, 3, 2), input_grad.transpose(0, 1, 3, 2), qkv_grad, out_grad, again_grad[0], gate_grad, up_grad,
        down_grad.T, mgain_grad[0],
    )


def solution(mesh):
    placed = (
        P(None, ("dp", "tensor"), None, None), P(None, ("dp", "tensor")), P(None, ("dp", "tensor")), P(), P(), P(),
        P(None, "tensor"), P(None, "tensor"), P("tensor", None), P(), P(None, ("dp", "tensor"), None, None),
    )
    return jax.shard_map(
        functools.partial(local, mesh.shape["dp"], mesh.shape["tensor"]), mesh=mesh, in_specs=placed,
        out_specs=(
            P(None, ("dp", "tensor"), None, None), P(None, ("dp", "tensor"), None, None), P(), P(), P(),
            P(None, "tensor"), P(None, "tensor"), P("tensor", None), P(),
        ),
        check_vma=False,
    )
```

time: 346 us -> 72.9 us (0.21)
  waiting for transfers between devices: 186 us -> 0 us
  blocking collectives: 68.1 us -> 0 us
  local copies, waits for them, and re-layouts: 17.2 us -> 0 us
  between operations: 13.8 us -> 0.65 us
  Pallas kernels: 59.1 us -> 72.1 us
    psum x2 -> x0, waiting for transfers between devices: 141 us -> none  [the longest x1 130 us: local(): lax.psum((qkv_grad, out_grad, again_grad, mgain_grad), ('dp', 'tensor'))]
    reduce_scatter x2 -> x0, waiting for transfers between devices: 43.9 us -> none  [the longest x1 23.1 us: local(): lax.psum_scatter(gu_grad, 'tensor', scatter_dimension=0, tiled=False)]
    psum x1 -> x0, blocking collectives: 38.7 us -> none  [local(): lax.psum((qkv_grad, out_grad, again_grad, mgain_grad), ('dp', 'tensor'))]
    all_gather x2 -> x0, blocking collectives: 29.4 us -> none  [the longest x1 15.2 us: local(): lax.all_gather(jnp.concatenate([gate_weight, up_weight], axis=1), 'tensor')]
    unnamed x17 -> x0, local copies, waits for them, and re-layouts: 14.7 us -> none
    pallas_call x1 -> x2, Pallas kernels: 59.1 us -> 72.1 us  [the longest x1 69.2 us: layer(): pl.pallas_call(functools.partial(kernel, n_dp, n_t), out_shape=[jax.Shape...]
  transfers between devices with their start and end apart: 4 -> 0, of which waited for: 4 -> 0; matrix products, arithmetic and copies ran while one was open for 2% -> 0% of each run, Pallas kernels for 0% -> 0%
where the time goes in v3:
time: 72.9 us; the launch traced here: 72.7 us
  Pallas kernels  72.1 us (99%)
    pallas_call x1, Pallas kernels, layer(): pl.pallas_call(functools.partial(kernel, n_dp, n_t), out_shape=[jax.Shape...  69.2 us
    pallas_call x1, Pallas kernels, hand_over(): pl.pallas_call(functools.partial(copy_kernel, n), out_shape=[jax.ShapeDty...  2.84 us

profile of v3, /device:TPU:0, one launch (start us, length us, event | category | flops | bytes accessed | tf_op | source)
XLA Modules:
  0.0 72.7 jit_solution(17164894038854543033)
XLA Ops:
  0.6 69.2 %shard_map.205 = (bf16[2,1,144,1024]{3,2,1,0:T(8,128)(2,1)}, f32[2,1,144,1024]{3,2,1,0:T(8,128)}, f32[144,432]{1,0:T(8,128)}, f32[144,144]{1,0:T(8,128)}, f32[1,...) custom-call(s32[1,2]{1,0:T(1,128)} %bitcast.17, ...), custom_call_target="tpu_custom_call" | custom-call | tf_op jit(solution)/shard_map/pallas_call | solution.py:577
  69.9 2.8 %shard_map.206 = (bf16[2,1,144,1024]{3,2,1,0:T(8,128)(2,1)}, f32[2,1,144,1024]{3,2,1,0:T(8,128)}, f32[144,432]{1,0:T(8,128)}, f32[144,144]{1,0:T(8,128)}, f32[1,...) custom-call(bf16[2,1,144,1024]{3,2,1,0:T(8,128)(2,1)} %get-tuple-element.27., ...), custom_call_target="tpu_custom_call" | custom-call | tf_op jit(solution)/shard_map/pallas_call | solution.py:547

commit v4 on v3

--- a/solution.py
+++ b/solution.py
@@ -21,12 +21,11 @@
 MASKED = -1e30
 LOG2E_SCALED = 0.25 * 1.4426950408889634
 
-STAGE1 = [(c, h) for c in range(3) for h in range(5)]
-STAGE2 = [(c, h) for c in range(3) for h in range(5, 8)][:8]
-STAGE3 = [(2, 7), (0, 8), (1, 8), (2, 8)]
-TILES = (3, 1, 1)
-OUT_AT = 16 * len(STAGE1)
-GAIN_AT = 16 * len(STAGE3)
+FIRST = [(c, h) for c in range(3) for h in range(6)]
+STAGE1 = FIRST[:16]
+STAGE2 = FIRST[16:] + [(c, h) for c in range(3) for h in (6, 7)]
+LAST = HEADS - 1
+TILES = (2, 2, 1)
 
 
 def mm(a, b):
@@ -89,18 +88,19 @@
 
 
 class GroupSum:
-    def __init__(self, index, count, to, stage, recv, out, sems):
-        self.index, self.count, self.to = index, count, to
+    def __init__(self, index, count, to, first, stage, recv, out, sems):
+        self.index, self.count, self.to, self.first = index, count, to, first
         self.stage, self.recv, self.out = stage, recv, out
         self.send, self.land, self.spread, self.gather = (sems.at[i] for i in range(4))
         self.groups = stage.shape[0]
         self.stride = max(count // self.groups, 1)
-        self.mine = index // self.stride
-        self.owner = (lax.rem(index, self.stride) == 0) & (self.mine < self.groups)
+        place = lax.rem(index + count - first, count)
+        self.mine = place // self.stride
+        self.owner = (lax.rem(place, self.stride) == 0) & (self.mine < self.groups)
 
     def go(self):
         def part(g):
-            owner = g * self.stride
+            owner = lax.rem(g * self.stride + self.first, self.count)
 
             @pl.when(owner != self.index)
             def _():
@@ -143,17 +143,56 @@
             landed(self.groups)
 
 
+class HeadSum:
+    def __init__(self, own, pair, half, recv, total, sems, core, partner, device_of, peers):
+        self.own, self.pair, self.half, self.recv, self.total = own, pair, half, recv, total
+        self.sems, self.core, self.partner, self.device_of, self.peers = sems, core, partner, device_of, peers
+
+    def _exchange(self):
+        return remote(self.own.at[1 - self.core], self.pair, self.sems.at[0], self.sems.at[1], self.partner)
+
+    def go(self, main, rest):
+        main = main.astype(BF).reshape(3, 16, LANES)
+        self.own[0] = main[:2]
+        self.own[1, 0] = main[2]
+        self.own[1, 1] = jnp.concatenate([rest, jnp.zeros((16, LANES - rest.shape[1]), F32)], axis=1).astype(BF)
+        self._exchange().start()
+
+    def send(self):
+        self._exchange().wait()
+        self.half[...] = (self.own[self.core].astype(F32) + self.pair[...].astype(F32)).astype(BF)
+        for_peer = lambda k: remote(self.half, self.recv.at[k - 1], self.sems.at[2], self.sems.at[3], self.device_of(k)).start()
+        each(1, self.peers, for_peer)
+
+    def _back(self):
+        piece = self.total.at[self.core]
+        return remote(piece, piece, self.sems.at[4], self.sems.at[5], self.partner)
+
+    def reduce(self):
+        remote(self.recv, self.recv, self.sems.at[2], self.sems.at[3], self.partner).wait()
+        self.total[self.core] = (self.half[...].astype(F32) + jnp.sum(self.recv[...].astype(F32), axis=0)).astype(BF)
+        self._back().start()
+
+    def finish(self):
+        self._back().wait()
+        turn = jnp.where(
+            lax.broadcasted_iota(jnp.int32, (48, LANES), 0) == lax.broadcasted_iota(jnp.int32, (48, LANES), 1), 1.0, 0.0
+        ).astype(BF)
+        total = self.total[...].reshape(4, 16, LANES)
+        return jnp.concatenate([mm_tn(total[:3].reshape(48, LANES), turn).astype(BF), total[3]], axis=0)
+
+
 def kernel(
     n_dp, n_t,
     median_ref, scale_ref, raw_hbm, cot_hbm, qkv_ref, out_ref, again_ref, gate_ref, up_ref, down_ref, mgain_ref, cos_ref, sin_ref,
     source_ref,
     result_hbm, igrad_hbm, qkvg_ref, outg_ref, againg_ref, gateg_ref, upg_ref, downg_ref, mgaing_ref,
     raw_ref, cot_ref, result_ref, igrad_ref,
-    e_ref, ds_ref, qa_ref, q_ref, k_ref, v_ref, o_ref, linv_ref, att_ref, datt_ref, dproj_ref, rows_ref, scaled_ref, dh_ref,
+    e_ref, ds_ref, ds2_ref, ga_ref, ga2_ref, qa_ref, q_ref, k_ref, v_ref, o_ref, linv_ref, att_ref, datt_ref, dproj_ref, rows_ref, scaled_ref, dh_ref,
     w_ref, ffacc_ref, ffstage_ref, ffpair_ref, ffhalf_ref, ffrecv_ref, ffout_ref, outacc_ref, gains_ref,
-    stage1, recv1, out1, stage2, recv2, out2, stage3, recv3, out3,
-    local_sem, w_send, w_recv, w_send2, w_recv2, ff_sem, sems1, sems2, sems3,
+    stage0, recv0, out0, stage1, recv1, out1, stage2, recv2, out2, *rest,
 ):
+    local_sem, w_send, w_recv, w_send2, w_recv2, ff_sem, sems0, sems1, sems2, sems3 = rest[5:]
     series, _, _, length = raw_hbm.shape
     nblk = length // BLK
     hidden_local = gate_ref.shape[1]
@@ -264,35 +303,53 @@
     def offset(j):
         return BLK * (j * (j + 1) // 2)
 
-    @pl.loop(0, series)
-    def _(s):
-        @pl.loop(0, HEADS)
-        def _(h):
-            keys = k_ref[s, h]
-            keys2 = jnp.concatenate([keys, keys], axis=0)
-            for j in range(nblk):
-                lo, hi = j * BLK, (j + 1) * BLK
-                scores = mm_tn(keys2[:, :hi], qa_ref[s, h, :, lo:hi])
-                diagonal = jnp.where(causal, scores[lo:], MASKED)
-                scores = jnp.concatenate([scores[:lo], diagonal], axis=0) if j else diagonal
-                largest = jnp.max(scores, axis=0, keepdims=True)
-                e_ref[s * HEADS + h, offset(j) : offset(j) + hi] = jnp.exp2(scores - largest).astype(BF)
-            for j in range(nblk):
-                lo, hi = j * BLK, (j + 1) * BLK
-                mixed = mm(v_ref[s, h, :, :hi], e_ref[s * HEADS + h, offset(j) : offset(j) + hi])
-                inverse = 1.0 / mixed[HEAD_DIM : HEAD_DIM + 1]
-                attended = mixed[:HEAD_DIM] * inverse
-                linv_ref[s, h, :, lo:hi] = inverse
-                o_ref[s, h, :, lo:hi] = attended
-                att_ref[s, h, :, lo:hi] = attended.astype(BF)
-
-            @pl.when((s == 0) & (h == 5))
-            def _():
-                send_weights()
-
-            @pl.when((s == series - 1) & (h == 5))
-            def _():
-                exchange_weights()
+
+    heads_total = series * HEADS
+
+    def score(i, j, target):
+        s, h = i // HEADS, lax.rem(i, HEADS)
+        keys = k_ref[s, h]
+        lo, hi = j * BLK, (j + 1) * BLK
+        scores = mm_tn(jnp.concatenate([keys, keys], axis=0)[:, :hi], qa_ref[s, h, :, lo:hi])
+        diagonal = jnp.where(causal, scores[lo:], MASKED)
+        scores = jnp.concatenate([scores[:lo], diagonal], axis=0) if j else diagonal
+        largest = jnp.max(scores, axis=0, keepdims=True)
+        e = jnp.exp2(scores - largest).astype(BF)
+        e_ref[i, offset(j) : offset(j) + hi] = e
+        if target is not None:
+            target[offset(j) : offset(j) + hi] = e
+
+    def mix(i, j, source):
+        s, h = i // HEADS, lax.rem(i, HEADS)
+        lo, hi = j * BLK, (j + 1) * BLK
+        e = e_ref[i, offset(j) : offset(j) + hi] if source is None else source[offset(j) : offset(j) + hi]
+        mixed = mm(v_ref[s, h, :, :hi], e)
+        inverse = 1.0 / mixed[HEAD_DIM : HEAD_DIM + 1]
+        attended = mixed[:HEAD_DIM] * inverse
+        linv_ref[s, h, :, lo:hi] = inverse
+        o_ref[s, h, :, lo:hi] = attended
+        att_ref[s, h, :, lo:hi] = attended.astype(BF)
+
+
+    for j in range(nblk):
+        score(0, j, ds_ref)
+
+    @pl.loop(1, heads_total, step=2)
+    def _(i):
+        for j in range(nblk):
+            score(i, j, ds2_ref)
+            mix(i - 1, j, ds_ref)
+        for j in range(nblk):
+            score(lax.min(i + 1, heads_total - 1), j, ds_ref)
+            mix(i, j, ds2_ref)
+
+        @pl.when(i == 3)
+        def _():
+            send_weights()
+
+        @pl.when(i == 11)
+        def _():
+            exchange_weights()
 
     finish_weights()
 
@@ -335,7 +392,7 @@
         dh_ref[s] = grad_hidden
         branch = grad_hidden.astype(BF)
         outacc_ref[...] += mm_nt(attended, branch)
-        gains_ref[:, 1:2] += gain_part
+        gains_ref[:, 0:1] += gain_part
         datt_ref[s] = mm(out_ref[...], branch).astype(BF).reshape(HEADS, HEAD_DIM, length)
 
     def store_result(s):
@@ -395,9 +452,9 @@
         upg_ref[...] = sums[D : 2 * D]
         downg_ref[...] = sums[2 * D : 3 * D]
 
-    sum1 = GroupSum(index, count, to, stage1, recv1, out1, sems1)
-    sum2 = GroupSum(index, count, to, stage2, recv2, out2, sems2)
-    sum3 = GroupSum(index, count, to, stage3, recv3, out3, sems3)
+    sum0 = GroupSum(index, count, to, 0, stage0, recv0, out0, sems0)
+    sum1 = GroupSum(index, count, to, count - 18, stage1, recv1, out1, sems1)
+    sum2 = GroupSum(index, count, to, 1, stage2, recv2, out2, sems2)
 
     def head_grads(parts):
         total = None
@@ -412,101 +469,161 @@
             tile = grads[:, t * LANES : (t + 1) * LANES].astype(BF)
             stage[t * GROUPS : (t + 1) * GROUPS] = tile.reshape(GROUPS, 16, LANES)
 
-    @pl.loop(0, HEADS)
-    def _(h):
-        @pl.loop(0, series)
-        def _(s):
-            grad = (datt_ref[s, h].astype(F32) * linv_ref[s, h]).astype(BF)
-            delta = -jnp.sum(grad.astype(F32) * o_ref[s, h], axis=0, keepdims=True)
-            high = delta.astype(BF).astype(F32)
-            tail = jnp.where(tail_rows == 0, high, jnp.where(tail_rows == 1, delta - high, 0.0))
-            grad_all = jnp.concatenate([grad, tail.astype(BF)], axis=0)
-            values = v_ref[s, h]
-            queries, keys = q_ref[s, h], k_ref[s, h]
-            for j in range(nblk):
-                lo, hi = j * BLK, (j + 1) * BLK
-                weights = e_ref[s * HEADS + h, offset(j) : offset(j) + hi]
-                centred = mm_tn(values[:, :hi], grad_all[:, lo:hi])
-                ds_ref[offset(j) : offset(j) + hi] = centred.astype(BF) * weights
-            value_grads, key_grads, query_grads = [], [], []
-            for j in range(nblk):
-                lo, hi = j * BLK, (j + 1) * BLK
-                query_grads.append(mm(keys[:, :hi], ds_ref[offset(j) : offset(j) + hi]))
-            for i in range(nblk):
-                value_grad = key_grad = None
-                for j in range(i, nblk):
-                    at = offset(j) + i * BLK
-                    cols = slice(j * BLK, (j + 1) * BLK)
-                    piece = mm_nt(grad[:, cols], e_ref[s * HEADS + h, at : at + BLK])
-                    value_grad = piece if value_grad is None else value_grad + piece
-                    piece = mm_nt(queries[:, cols], ds_ref[at : at + BLK])
-                    key_grad = piece if key_grad is None else key_grad + piece
-                value_grads.append(value_grad)
-                key_grads.append(key_grad)
-
-            def unrotate(g):
-                a, b = g[:8], g[8:]
-                return jnp.concatenate([a * cosine + b * sine, b * cosine - a * sine], axis=0)
-
-            query_grad = jnp.concatenate(query_grads, axis=1) * 0.25
-            key_grad = jnp.concatenate(key_grads, axis=1) * 0.25
-            dproj_ref[s, h] = unrotate(query_grad).astype(BF)
-            dproj_ref[s, HEADS + h] = unrotate(key_grad).astype(BF)
-            dproj_ref[s, 2 * HEADS + h] = jnp.concatenate(value_grads, axis=1).astype(BF)
-
-        @pl.when(h == 0)
+
+    def place_of_head(i):
+        return lax.rem(i, series), i // series
+
+    def prepare(i, grad_all_ref):
+        s, h = place_of_head(i)
+        grad = (datt_ref[s, h].astype(F32) * linv_ref[s, h]).astype(BF)
+        delta = -jnp.sum(grad.astype(F32) * o_ref[s, h], axis=0, keepdims=True)
+        high = delta.astype(BF).astype(F32)
+        tail = jnp.where(tail_rows == 0, high, jnp.where(tail_rows == 1, delta - high, 0.0))
+        grad_all_ref[:HEAD_DIM] = grad
+        grad_all_ref[HEAD_DIM:] = tail.astype(BF)
+
+    def center(i, j, grad_all_ref, target):
+        s, h = place_of_head(i)
+        lo, hi = j * BLK, (j + 1) * BLK
+        weights = e_ref[s * HEADS + h, offset(j) : offset(j) + hi]
+        centred = mm_tn(v_ref[s, h, :, :hi], grad_all_ref[:, lo:hi])
+        target[offset(j) : offset(j) + hi] = centred.astype(BF) * weights
+
+    def unrotate(g, lo, hi):
+        a, b = g[:8], g[8:]
+        c, d = cosine[:, lo:hi], sine[:, lo:hi]
+        return jnp.concatenate([a * c + b * d, b * c - a * d], axis=0)
+
+    def grad_query(i, j, source):
+        s, h = place_of_head(i)
+        lo, hi = j * BLK, (j + 1) * BLK
+        g = mm(k_ref[s, h, :, :hi], source[offset(j) : offset(j) + hi]) * 0.25
+        dproj_ref[s, h, :, lo:hi] = unrotate(g, lo, hi).astype(BF)
+
+    def grad_key(i, j, source):
+        s, h = place_of_head(i)
+        lo, hi = j * BLK, (j + 1) * BLK
+        total = None
+        for q in range(j, nblk):
+            at = offset(q) + lo
+            piece = mm_nt(q_ref[s, h, :, q * BLK : (q + 1) * BLK], source[at : at + BLK])
+            total = piece if total is None else total + piece
+        dproj_ref[s, HEADS + h, :, lo:hi] = unrotate(total * 0.25, lo, hi).astype(BF)
+
+    def grad_value(i, j, grad_all_ref):
+        s, h = place_of_head(i)
+        lo, hi = j * BLK, (j + 1) * BLK
+        total = None
+        for q in range(j, nblk):
+            at = offset(q) + lo
+            piece = mm_nt(grad_all_ref[:HEAD_DIM, q * BLK : (q + 1) * BLK], e_ref[s * HEADS + h, at : at + BLK])
+            total = piece if total is None else total + piece
+        dproj_ref[s, 2 * HEADS + h, :, lo:hi] = total.astype(BF)
+
+    def device_of(k):
+        peer = lax.rem(place + k, peers)
+        return (2 * (peer // n_t) + core, lax.rem(peer, n_t))
+
+    sum3 = HeadSum(*rest[:5], sems3, core, partner, device_of, peers)
+
+    def one_head_grads(h):
+        main, rest = None, None
+        for s in range(series):
+            grads = jnp.concatenate([dproj_ref[s, c * HEADS + h] for c in range(3)], axis=0)
+            one, two = mm_nt(grads, rows_ref[s, :LANES]), mm_nt(rows_ref[s, LANES:], grads)
+            main, rest = (one, two) if main is None else (main + one, rest + two)
+        return main, rest
+
+    put(stage0, jnp.concatenate([outacc_ref[...], gains_ref[:, : 2 * LANES - D]], axis=1))
+    sum0.go()
+
+    def products(i, j, source, grad_all_ref):
+        grad_query(i, j, source)
+        grad_value(i, j, grad_all_ref)
+        grad_key(i, j, source)
+
+    prepare(0, ga_ref)
+    for j in range(nblk):
+        center(0, j, ga_ref, ds_ref)
+
+    @pl.loop(0, heads_total - series, step=2)
+    def _(i):
+        prepare(i + 1, ga2_ref)
+        for j in range(nblk):
+            center(i + 1, j, ga2_ref, ds2_ref)
+            products(i, j, ds_ref, ga_ref)
+        prepare(i + 2, ga_ref)
+        for j in range(nblk):
+            center(i + 2, j, ga_ref, ds_ref)
+            products(i + 1, j, ds2_ref, ga2_ref)
+
+        @pl.when(i == 0)
         def _():
             ff_send()
 
-        @pl.when(h == 4)
+        @pl.when(i == 3 * series)
         def _():
             ff_reduce()
-            put(stage1, jnp.concatenate([head_grads(STAGE1), outacc_ref[...]], axis=1))
+            sum0.reduce()
+
+        @pl.when(i == 5 * series)
+        def _():
+            put(stage1, head_grads(STAGE1))
             sum1.go()
 
-        @pl.when(h == 6)
+        @pl.when(i == 7 * series)
         def _():
             sum1.reduce()
-
-        @pl.when(h == 7)
-        def _():
             put(stage2, head_grads(STAGE2))
             sum2.go()
 
-    @pl.loop(0, series)
-    def _(s):
+    i = heads_total - 2
+    prepare(i + 1, ga2_ref)
+    for j in range(nblk):
+        center(i + 1, j, ga2_ref, ds2_ref)
+        products(i, j, ds_ref, ga_ref)
+    for j in range(nblk):
+        products(i + 1, j, ds2_ref, ga2_ref)
+    sum3.go(*one_head_grads(LAST))
+
+    def back(s):
         grad = dproj_ref[s].reshape(3 * D, length)
         grad_rows = mm(qkv_ref[...], grad)
         n, r = norm_stats(scaled_ref[s])
-        part, gain_part = norm_backward(grad_rows, n, r, again)
+        part, _ = norm_backward(grad_rows, n, r, again)
         igrad_ref[s] = (dh_ref[s] + part) * spread_inverse(s)
-        gains_ref[:, 0:1] += gain_part
-
-    last = head_grads(STAGE3)
-    put(stage3, jnp.concatenate([last, gains_ref[:, : LANES - GAIN_AT]], axis=1))
-    sum3.go()
+
     for s in range(series):
+        back(s)
+        if s == 0:
+            sum3.send()
         store_igrad(s).start()
+
+    ff_finish()
+    sum0.finish()
+    sum1.finish()
     sum2.reduce()
-    ff_finish()
-    sum1.finish()
+    fixed = sum(TILES) * LANES
     place_of = jnp.where(
-        lax.broadcasted_iota(jnp.int32, (sum(TILES) * LANES, source_ref.shape[1]), 0) == source_ref[...], 1.0, 0.0
+        lax.broadcasted_iota(jnp.int32, (fixed + LANES, source_ref.shape[1]), 0) == source_ref[...], 1.0, 0.0
     ).astype(BF)
-    sum3.reduce()
-    sum2.finish()
+
+    def tiles_of(out, n):
+        return [out[t * GROUPS : (t + 1) * GROUPS].reshape(D, LANES) for t in range(n)]
+
+    tiles = tiles_of(out0, TILES[0]) + tiles_of(out1, TILES[1])
+    mgaing_ref[...] = to_row(tiles[1][:, D - LANES : D - LANES + 1].astype(F32))
+    sums = mm(jnp.concatenate(tiles, axis=1), place_of[: fixed - LANES])
+    outg_ref[...] = sums[:, 4 * LANES : 4 * LANES + D]
     for s in range(series):
         store_result(s).wait()
         store_igrad(s).wait()
-    sum3.finish()
-    tiles = []
-    for out, n in zip((out1, out2, out3), TILES, strict=True):
-        tiles += [out[t * GROUPS : (t + 1) * GROUPS].reshape(D, LANES) for t in range(n)]
-    sums = mm(jnp.concatenate(tiles, axis=1), place_of)
-    qkvg_ref[...] = sums[:, : 3 * D]
-    outg_ref[...] = sums[:, 4 * LANES : 4 * LANES + D]
-    againg_ref[...] = to_row(tiles[-1][:, GAIN_AT : GAIN_AT + 1].astype(F32))
-    mgaing_ref[...] = to_row(tiles[-1][:, GAIN_AT + 1 : GAIN_AT + 2].astype(F32))
+    sum3.reduce()
+    sum2.finish()
+    sums = sums[:, : 3 * D] + mm(tiles_of(out2, 1)[0], place_of[fixed - LANES : fixed, : 3 * D])
+    sums = sums + mm(sum3.finish(), place_of[fixed:, : 3 * D])
+    qkvg_ref[...] = sums
+    againg_ref[...] = to_row(jnp.sum(sums * qkv_ref[...].astype(F32), axis=1, keepdims=True) / again)
 
 
 def rope_tables(length):
@@ -518,13 +635,14 @@
 
 def column_sources():
     source = np.full((1, 4 * LANES + D), -1, np.int32)
-    first = 0
-    for parts, tiles in zip((STAGE1, STAGE2, STAGE3), TILES, strict=True):
+    source[0, 4 * LANES :] = np.arange(D)
+    first = TILES[0] * LANES
+    last = [(c, LAST) for c in range(3)]
+    for parts, tiles in zip((STAGE1, STAGE2, last), TILES[1:] + (1,), strict=True):
         for place, (c, h) in enumerate(parts):
             at = c * D + h * HEAD_DIM
             source[0, at : at + HEAD_DIM] = first + place * HEAD_DIM + np.arange(HEAD_DIM)
         first += tiles * LANES
-    source[0, 4 * LANES :] = OUT_AT + np.arange(D)
     return source
 
 
@@ -574,6 +692,8 @@
         stages += [
             pltpu.VMEM((n * GROUPS, 16, LANES), BF), pltpu.VMEM((count - 1, 16, LANES), BF), pltpu.VMEM((n * GROUPS, 16, LANES), BF),
         ]
+    half = (2, 16, LANES)
+    one_head = [pltpu.VMEM(shape, BF) for shape in ((2,) + half, half, half, (pairs * n_t - 1,) + half, (2,) + half)]
     return pl.pallas_call(
         functools.partial(kernel, n_dp, n_t),
         out_shape=[
@@ -596,6 +716,9 @@
             pltpu.VMEM(rows, F32),
             pltpu.VMEM((series * HEADS, packed, BLK), BF),
             pltpu.VMEM((packed, BLK), BF),
+            pltpu.VMEM((packed, BLK), BF),
+            pltpu.VMEM((2 * HEAD_DIM, length), BF),
+            pltpu.VMEM((2 * HEAD_DIM, length), BF),
             pltpu.VMEM((series, HEADS, 2 * HEAD_DIM, length), BF),
             pltpu.VMEM(per_head, BF),
             pltpu.VMEM(per_head, BF),
@@ -618,7 +741,8 @@
             pltpu.VMEM((width, width), F32),
             pltpu.VMEM((width, LANES), F32),
             *stages,
-            dma((2 * series,)), dma((n_t,)), dma((n_t,)), dma((n_t,)), dma((n_t,)), dma((6,)), dma((4,)), dma((4,)), dma((4,)),
+            *one_head,
+            dma((2 * series,)), dma((n_t,)), dma((n_t,)), dma((n_t,)), dma((n_t,)), dma((6,)), dma((4,)), dma((4,)), dma((4,)), dma((6,)),
         ],
         compiler_params=pltpu.CompilerParams(vmem_limit_bytes=60 * 2**20, collective_id=0, has_side_effects=True),
     )(

time: 72.9 us -> 65.3 us (0.90)
  Pallas kernels: 72.1 us -> 64.3 us
    pallas_call x1, Pallas kernels: 69.2 us -> 61.5 us  [layer(): pl.pallas_call(functools.partial(kernel, n_dp, n_t), out_shape=[jax.Shape...]
where the time goes in v4:
time: 65.3 us; the launch traced here: 65.1 us
  Pallas kernels  64.3 us (98%)
  between operations  0.81 us (1%)
    pallas_call x1, Pallas kernels, layer(): pl.pallas_call(functools.partial(kernel, n_dp, n_t), out_shape=[jax.Shape...  61.5 us
    pallas_call x1, Pallas kernels, hand_over(): pl.pallas_call(functools.partial(copy_kernel, n), out_shape=[jax.ShapeDty...  2.84 us

profile of v4, /device:TPU:0, one launch (start us, length us, event | category | flops | bytes accessed | tf_op | source)
XLA Modules:
  0.0 65.1 jit_solution(3817310157596544350)
XLA Ops:
  0.6 61.5 %shard_map.205 = (bf16[2,1,144,1024]{3,2,1,0:T(8,128)(2,1)}, f32[2,1,144,1024]{3,2,1,0:T(8,128)}, f32[144,432]{1,0:T(8,128)}, f32[144,144]{1,0:T(8,128)}, f32[1,...) custom-call(s32[1,2]{1,0:T(1,128)} %bitcast.17, ...), custom_call_target="tpu_custom_call" | custom-call | tf_op jit(solution)/shard_map/pallas_call | solution.py:697
  62.1 2.8 %shard_map.206 = (bf16[2,1,144,1024]{3,2,1,0:T(8,128)(2,1)}, f32[2,1,144,1024]{3,2,1,0:T(8,128)}, f32[144,432]{1,0:T(8,128)}, f32[144,144]{1,0:T(8,128)}, f32[1,...) custom-call(bf16[2,1,144,1024]{3,2,1,0:T(8,128)(2,1)} %get-tuple-element.27., ...), custom_call_target="tpu_custom_call" | custom-call | tf_op jit(solution)/shard_map/pallas_call | solution.py:665

commit v5 on v4

--- a/solution.py
+++ b/solution.py
@@ -17,15 +17,15 @@
 LANES = 128
 GROUPS = D // 16
 BLK = 256
+HALF = BLK // 2
 EPS = 1e-05
 MASKED = -1e30
 LOG2E_SCALED = 0.25 * 1.4426950408889634
 
-FIRST = [(c, h) for c in range(3) for h in range(6)]
-STAGE1 = FIRST[:16]
-STAGE2 = FIRST[16:] + [(c, h) for c in range(3) for h in (6, 7)]
+STAGE1 = [(c, h) for c in range(3) for h in range(4)]
+STAGE2 = [(c, h) for c in range(3) for h in range(4, 8)]
 LAST = HEADS - 1
-TILES = (2, 2, 1)
+TILES = (2, 2, 2)
 
 
 def mm(a, b):
@@ -186,13 +186,14 @@
     n_dp, n_t,
     median_ref, scale_ref, raw_hbm, cot_hbm, qkv_ref, out_ref, again_ref, gate_ref, up_ref, down_ref, mgain_ref, cos_ref, sin_ref,
     source_ref,
-    result_hbm, igrad_hbm, qkvg_ref, outg_ref, againg_ref, gateg_ref, upg_ref, downg_ref, mgaing_ref,
-    raw_ref, cot_ref, result_ref, igrad_ref,
-    e_ref, ds_ref, ds2_ref, ga_ref, ga2_ref, qa_ref, q_ref, k_ref, v_ref, o_ref, linv_ref, att_ref, datt_ref, dproj_ref, rows_ref, scaled_ref, dh_ref,
-    w_ref, ffacc_ref, ffstage_ref, ffpair_ref, ffhalf_ref, ffrecv_ref, ffout_ref, outacc_ref, gains_ref,
+    result_ref, igrad_ref, qkvg_ref, outg_ref, againg_ref, gateg_ref, upg_ref, downg_ref, mgaing_ref,
+    raw_ref, cot_ref,
+    e_ref, held0_ref, held1_ref, largest_ref, ds_ref, ds2_ref, dt_ref, dt2_ref, ga_ref, ga2_ref, qa_ref, q_ref, k_ref, v_ref, o_ref, linv_ref, att_ref, dproj_ref, rows_ref, scaled_ref,
+    w_ref, inner_ref, ffacc_ref, ffstage_ref, ffpair_ref, ffhalf_ref, ffrecv_ref, ffout_ref, outacc_ref, gains_ref,
     stage0, recv0, out0, stage1, recv1, out1, stage2, recv2, out2, *rest,
 ):
     local_sem, w_send, w_recv, w_send2, w_recv2, ff_sem, sems0, sems1, sems2, sems3 = rest[5:]
+    held_refs = (held0_ref, held1_ref)
     series, _, _, length = raw_hbm.shape
     nblk = length // BLK
     hidden_local = gate_ref.shape[1]
@@ -225,6 +226,9 @@
     def spread_inverse(s):
         return 1.0 / jnp.full((1, length), scale_ref[0, s].astype(F32) * 0.25, F32)
 
+    def scaled_series(s):
+        return (raw_ref[s].astype(F32) - median_ref[0, s].astype(F32) * 0.05) * spread_inverse(s)
+
     tail_rows = lax.broadcasted_iota(jnp.int32, (HEAD_DIM, length), 0)
     w_ref[0, :, :hidden_local] = gate_ref[...]
     w_ref[0, :, hidden_local : 2 * hidden_local] = up_ref[...]
@@ -234,8 +238,7 @@
 
     @pl.loop(0, series)
     def _(s):
-        shift = median_ref[0, s].astype(F32) * 0.05
-        scaled = (raw_ref[s].astype(F32) - shift) * spread_inverse(s)
+        scaled = scaled_series(s)
         scaled_ref[s] = scaled
         n, _ = norm_stats(scaled)
         rows = (n * again).astype(BF)
@@ -298,58 +301,145 @@
         half_rows(0, sent)
         half_rows(1, landed)
 
-    causal = lax.broadcasted_iota(jnp.int32, (BLK, BLK), 0) <= lax.broadcasted_iota(jnp.int32, (BLK, BLK), 1)
-
-    def offset(j):
-        return BLK * (j * (j + 1) // 2)
-
-
-    heads_total = series * HEADS
-
-    def score(i, j, target):
-        s, h = i // HEADS, lax.rem(i, HEADS)
-        keys = k_ref[s, h]
-        lo, hi = j * BLK, (j + 1) * BLK
-        scores = mm_tn(jnp.concatenate([keys, keys], axis=0)[:, :hi], qa_ref[s, h, :, lo:hi])
-        diagonal = jnp.where(causal, scores[lo:], MASKED)
-        scores = jnp.concatenate([scores[:lo], diagonal], axis=0) if j else diagonal
-        largest = jnp.max(scores, axis=0, keepdims=True)
-        e = jnp.exp2(scores - largest).astype(BF)
-        e_ref[i, offset(j) : offset(j) + hi] = e
-        if target is not None:
-            target[offset(j) : offset(j) + hi] = e
-
-    def mix(i, j, source):
-        s, h = i // HEADS, lax.rem(i, HEADS)
-        lo, hi = j * BLK, (j + 1) * BLK
-        e = e_ref[i, offset(j) : offset(j) + hi] if source is None else source[offset(j) : offset(j) + hi]
-        mixed = mm(v_ref[s, h, :, :hi], e)
-        inverse = 1.0 / mixed[HEAD_DIM : HEAD_DIM + 1]
-        attended = mixed[:HEAD_DIM] * inverse
-        linv_ref[s, h, :, lo:hi] = inverse
-        o_ref[s, h, :, lo:hi] = attended
-        att_ref[s, h, :, lo:hi] = attended.astype(BF)
-
-
-    for j in range(nblk):
-        score(0, j, ds_ref)
-
-    @pl.loop(1, heads_total, step=2)
-    def _(i):
+    up_allowed = lax.broadcasted_iota(jnp.int32, (HALF, BLK), 0) <= lax.broadcasted_iota(jnp.int32, (HALF, BLK), 1)
+    side = lax.broadcasted_iota(jnp.int32, (HALF, BLK), 1)
+    side = jnp.where(side < HALF, side, side - HALF)
+    side_allowed = lax.broadcasted_iota(jnp.int32, (HALF, BLK), 0) <= side
+
+    def bounds(j):
+        return j * BLK, j * BLK + HALF, (j + 1) * BLK
+
+    def segments(j):
+        _, mid, _ = bounds(j)
+        at = BLK * j * (j - 1) + (BLK + HALF) * j
+        return slice(at, at + mid), slice(at + mid, at + 2 * mid), slice(at + 2 * mid, at + 2 * mid + HALF)
+
+    def key_segments(i):
+        rest = length - bounds(i)[1]
+        at = sum(2 * (length - bounds(k)[1]) + HALF for k in range(i))
+        return slice(at, at + rest), slice(at + rest, at + 2 * rest), slice(at + 2 * rest, at + 2 * rest + HALF)
+
+    def turn_to_keys(j, own, shared, target):
+        lo, mid, _ = bounds(j)
+        main = key_segments(j)
+        for s in range(2):
+            for i in range(j):
+                at = key_segments(i)[s].start + lo - bounds(i)[1]
+                target[at : at + BLK] = own[s][i * BLK : (i + 1) * BLK].T
+            turned = own[s][lo:mid].T
+            target[main[2], halves(s)] = turned[:HALF]
+            at = main[s].start
+            target[at : at + HALF, halves(0)] = turned[HALF:]
+            target[at : at + HALF, halves(1)] = shared[:, halves(s)].T
+
+    def turn_to_queries(i, own, shared, target):
+        lo, mid, hi = bounds(i)
+        main = segments(i)
+        for s in range(2):
+            turned = own[s][:HALF].T
+            at = main[s].start + lo
+            target[at : at + HALF, halves(1)] = turned[:HALF]
+            target[main[2], halves(s)] = turned[HALF:]
+            target[at : at + HALF, halves(0)] = shared[:, halves(s)].T
+            for j in range(i + 1, nblk):
+                at = segments(j)[s].start + lo
+                first = bounds(j)[0] - mid
+                target[at : at + BLK] = own[s][first : first + BLK].T
+
+    def halves(s):
+        return slice(s * HALF, (s + 1) * HALF)
+
+    def side_by_side(a, b):
+        zero = jnp.zeros_like(a)
+        return jnp.concatenate([jnp.concatenate([a, zero], axis=1), jnp.concatenate([zero, b], axis=1)], axis=0)
+
+    def score(h, j):
+        lo, mid, hi = bounds(j)
+        held = held_refs[j % 2]
+        keys = [jnp.concatenate([k_ref[s, h], k_ref[s, h]], axis=0) for s in range(2)]
+        queries = [qa_ref[s, h, :, lo:hi] for s in range(2)]
+        shared = mm_tn(
+            jnp.concatenate([keys[s][:, mid:hi] for s in range(2)], axis=0),
+            side_by_side(queries[0][:, HALF:], queries[1][:, HALF:]),
+        )
+        shared = jnp.where(side_allowed, shared, MASKED)
+        held[2 * mid : 2 * mid + HALF] = shared
+        shared_largest = jnp.max(shared, axis=0, keepdims=True)
+        for s in range(2):
+            scores = mm_tn(keys[s][:, :mid], queries[s])
+            diagonal = jnp.where(up_allowed, scores[lo:], MASKED)
+            scores = jnp.concatenate([scores[:lo], diagonal], axis=0) if j else diagonal
+            held[s * mid : (s + 1) * mid] = scores
+            top = jnp.max(scores, axis=0, keepdims=True)
+            right = jnp.maximum(top[:, HALF:], shared_largest[:, halves(s)])
+            largest_ref[j % 2, s : s + 1] = jnp.concatenate([top[:, :HALF], right], axis=1)
+
+    def softmax(h, j, target):
+        lo, mid, hi = bounds(j)
+        held = held_refs[j % 2]
+        largest = [largest_ref[j % 2, s : s + 1] for s in range(2)]
+        weights = [jnp.exp2(held[s * mid : (s + 1) * mid] - largest[s]) for s in range(2)]
+        side_largest = jnp.concatenate([largest[0][:, HALF:], largest[1][:, HALF:]], axis=1)
+        weights.append(jnp.exp2(held[2 * mid : 2 * mid + HALF] - side_largest))
+        shared_total = jnp.sum(weights[2], axis=0, keepdims=True)
+        for s in range(2):
+            total = jnp.sum(weights[s], axis=0, keepdims=True)
+            total = jnp.concatenate([total[:, :HALF], total[:, HALF:] + shared_total[:, halves(s)]], axis=1)
+            linv_ref[s, h, :, lo:hi] = 1.0 / total
+        weights = [e.astype(BF) for e in weights]
+        for rows, e in zip(segments(j), weights, strict=True):
+            target[rows] = e
+        turn_to_keys(j, weights[:2], weights[2], e_ref.at[h])
+
+    def from_segments(j, left, source):
+        _, mid, hi = bounds(j)
+        segs = segments(j)
+        shared = mm(jnp.concatenate([left[s][:, mid:hi] for s in range(2)], axis=0), source[segs[2]])
+        out = []
+        for s in range(2):
+            own = mm(left[s][:, :mid], source[segs[s]])
+            right = own[:, HALF:] + shared[s * HEAD_DIM : (s + 1) * HEAD_DIM, halves(s)]
+            out.append(jnp.concatenate([own[:, :HALF], right], axis=1))
+        return out
+
+    def mix(h, j, source):
+        lo, _, hi = bounds(j)
+        mixed = from_segments(j, [v_ref[s, h, :HEAD_DIM] for s in range(2)], source)
+        for s in range(2):
+            attended = mixed[s] * linv_ref[s, h, :, lo:hi]
+            o_ref[s, h, :, lo:hi] = attended
+            att_ref[s, h, :, lo:hi] = attended.astype(BF)
+
+    score(0, 0)
+    for j in range(1, nblk):
+        score(0, j)
+        softmax(0, j - 1, ds_ref)
+
+    def step(h, now, before):
         for j in range(nblk):
-            score(i, j, ds2_ref)
-            mix(i - 1, j, ds_ref)
-        for j in range(nblk):
-            score(lax.min(i + 1, heads_total - 1), j, ds_ref)
-            mix(i, j, ds2_ref)
-
-        @pl.when(i == 3)
+            score(h, j)
+            if j:
+                softmax(h, j - 1, now)
+            else:
+                softmax(h - 1, nblk - 1, before)
+            mix(h - 1, j, before)
+
+    @pl.loop(1, HEADS, step=2)
+    def _(h):
+        step(h, ds2_ref, ds_ref)
+        step(h + 1, ds_ref, ds2_ref)
+
+        @pl.when(h == 1)
         def _():
             send_weights()
 
-        @pl.when(i == 11)
+        @pl.when(h == 5)
         def _():
             exchange_weights()
+
+    softmax(HEADS - 1, nblk - 1, ds_ref)
+    for j in range(nblk):
+        mix(HEADS - 1, j, ds_ref)
 
     finish_weights()
 
@@ -365,7 +455,7 @@
         rows = (n * mgain).astype(BF)
         low = cot_ref[s]
         top = low.astype(F32)
-        result = hidden
+        scaled_ref[s] = hidden
         grad_rows = jnp.zeros((D, length), F32)
         for t in range(n_t):
             gu = w_ref[t, :, : 2 * hidden_local]
@@ -376,33 +466,23 @@
             sigma = 1.0 / (1.0 + jnp.exp(-gate))
             act = gate * sigma
             inner = (act * up).astype(BF)
+            inner_ref[s, t * hidden_local : (t + 1) * hidden_local] = inner
             grad_gate = (grad_inner * up * (sigma + act * (1.0 - sigma))).astype(BF)
             grad_up = (grad_inner * act).astype(BF)
             grad_both = jnp.concatenate([grad_gate, grad_up], axis=0)
-            result = result + mm(down, inner)
             grad_rows = grad_rows + mm(gu, grad_both)
             gu_piece = mm_nt(rows, grad_both)
             ffacc_ref[t, :D] += gu_piece[:, :hidden_local]
             ffacc_ref[t, D : 2 * D] += gu_piece[:, hidden_local:]
             ffacc_ref[t, 2 * D : 3 * D] += mm_nt(low, inner)
 
-        result_ref[s] = result.astype(BF)
         part, gain_part = norm_backward(grad_rows, n, r, mgain)
         grad_hidden = top + part
-        dh_ref[s] = grad_hidden
+        igrad_ref[s, 0] = grad_hidden
         branch = grad_hidden.astype(BF)
         outacc_ref[...] += mm_nt(attended, branch)
         gains_ref[:, 0:1] += gain_part
-        datt_ref[s] = mm(out_ref[...], branch).astype(BF).reshape(HEADS, HEAD_DIM, length)
-
-    def store_result(s):
-        return pltpu.make_async_copy(result_ref.at[s], result_hbm.at[s, 0], local_sem.at[s])
-
-    def store_igrad(s):
-        return pltpu.make_async_copy(igrad_ref.at[s], igrad_hbm.at[s, 0], local_sem.at[series + s])
-
-    for s in range(series):
-        store_result(s).start()
+        att_ref[s] = mm(out_ref[...], branch).astype(BF).reshape(HEADS, HEAD_DIM, length)
 
     share = ffout_ref.shape[1]
     for t in range(n_t):
@@ -454,7 +534,7 @@
 
     sum0 = GroupSum(index, count, to, 0, stage0, recv0, out0, sems0)
     sum1 = GroupSum(index, count, to, count - 18, stage1, recv1, out1, sems1)
-    sum2 = GroupSum(index, count, to, 1, stage2, recv2, out2, sems2)
+    sum2 = GroupSum(index, count, to, 7, stage2, recv2, out2, sems2)
 
     def head_grads(parts):
         total = None
@@ -462,63 +542,14 @@
             grads = jnp.concatenate([dproj_ref[s, c * HEADS + h] for c, h in parts], axis=0)
             piece = mm_nt(rows_ref[s], grads)
             total = piece if total is None else total + piece
-        return total
+        spare = -total.shape[1] % LANES
+        return jnp.concatenate([total, jnp.zeros((D, spare), F32)], axis=1)
 
     def put(stage, grads):
         for t in range(grads.shape[1] // LANES):
             tile = grads[:, t * LANES : (t + 1) * LANES].astype(BF)
             stage[t * GROUPS : (t + 1) * GROUPS] = tile.reshape(GROUPS, 16, LANES)
 
-
-    def place_of_head(i):
-        return lax.rem(i, series), i // series
-
-    def prepare(i, grad_all_ref):
-        s, h = place_of_head(i)
-        grad = (datt_ref[s, h].astype(F32) * linv_ref[s, h]).astype(BF)
-        delta = -jnp.sum(grad.astype(F32) * o_ref[s, h], axis=0, keepdims=True)
-        high = delta.astype(BF).astype(F32)
-        tail = jnp.where(tail_rows == 0, high, jnp.where(tail_rows == 1, delta - high, 0.0))
-        grad_all_ref[:HEAD_DIM] = grad
-        grad_all_ref[HEAD_DIM:] = tail.astype(BF)
-
-    def center(i, j, grad_all_ref, target):
-        s, h = place_of_head(i)
-        lo, hi = j * BLK, (j + 1) * BLK
-        weights = e_ref[s * HEADS + h, offset(j) : offset(j) + hi]
-        centred = mm_tn(v_ref[s, h, :, :hi], grad_all_ref[:, lo:hi])
-        target[offset(j) : offset(j) + hi] = centred.astype(BF) * weights
-
-    def unrotate(g, lo, hi):
-        a, b = g[:8], g[8:]
-        c, d = cosine[:, lo:hi], sine[:, lo:hi]
-        return jnp.concatenate([a * c + b * d, b * c - a * d], axis=0)
-
-    def grad_query(i, j, source):
-        s, h = place_of_head(i)
-        lo, hi = j * BLK, (j + 1) * BLK
-        g = mm(k_ref[s, h, :, :hi], source[offset(j) : offset(j) + hi]) * 0.25
-        dproj_ref[s, h, :, lo:hi] = unrotate(g, lo, hi).astype(BF)
-
-    def grad_key(i, j, source):
-        s, h = place_of_head(i)
-        lo, hi = j * BLK, (j + 1) * BLK
-        total = None
-        for q in range(j, nblk):
-            at = offset(q) + lo
-            piece = mm_nt(q_ref[s, h, :, q * BLK : (q + 1) * BLK], source[at : at + BLK])
-            total = piece if total is None else total + piece
-        dproj_ref[s, HEADS + h, :, lo:hi] = unrotate(total * 0.25, lo, hi).astype(BF)
-
-    def grad_value(i, j, grad_all_ref):
-        s, h = place_of_head(i)
-        lo, hi = j * BLK, (j + 1) * BLK
-        total = None
-        for q in range(j, nblk):
-            at = offset(q) + lo
-            piece = mm_nt(grad_all_ref[:HEAD_DIM, q * BLK : (q + 1) * BLK], e_ref[s * HEADS + h, at : at + BLK])
-            total = piece if total is None else total + piece
-        dproj_ref[s, 2 * HEADS + h, :, lo:hi] = total.astype(BF)
 
     def device_of(k):
         peer = lax.rem(place + k, peers)
@@ -537,72 +568,116 @@
     put(stage0, jnp.concatenate([outacc_ref[...], gains_ref[:, : 2 * LANES - D]], axis=1))
     sum0.go()
 
-    def products(i, j, source, grad_all_ref):
-        grad_query(i, j, source)
-        grad_value(i, j, grad_all_ref)
-        grad_key(i, j, source)
+    def prepare(h, grad_ref):
+        for s in range(2):
+            grad = (att_ref[s, h].astype(F32) * linv_ref[s, h]).astype(BF)
+            delta = -jnp.sum(grad.astype(F32) * o_ref[s, h], axis=0, keepdims=True)
+            high = delta.astype(BF).astype(F32)
+            tail = jnp.where(tail_rows == 0, high, jnp.where(tail_rows == 1, delta - high, 0.0))
+            grad_ref[s, :HEAD_DIM] = grad
+            grad_ref[s, HEAD_DIM:] = tail.astype(BF)
+
+    def center(h, i, grad_ref, target, turned):
+        lo, mid, hi = bounds(i)
+        segs = key_segments(i)
+        values = [v_ref[s, h] for s in range(2)]
+        shared = mm_tn(
+            jnp.concatenate([grad_ref[s, :, lo:mid] for s in range(2)], axis=0),
+            side_by_side(values[0][:, lo:mid], values[1][:, lo:mid]),
+        )
+        shared = shared.astype(BF) * e_ref[h, segs[2]]
+        target[segs[2]] = shared
+        own = []
+        for s in range(2):
+            centred = mm_tn(grad_ref[s, :, mid:], values[s][:, lo:hi])
+            own.append(centred.astype(BF) * e_ref[h, segs[s]])
+            target[segs[s]] = own[s]
+        turn_to_queries(i, own, shared, turned)
+
+    def from_key_segments(i, left, source):
+        lo, mid, _ = bounds(i)
+        segs = key_segments(i)
+        shared = mm(jnp.concatenate([left[s][:, lo:mid] for s in range(2)], axis=0), source[segs[2]])
+        out = []
+        for s in range(2):
+            own = mm(left[s][:, mid:], source[segs[s]])
+            first = own[:, :HALF] + shared[s * HEAD_DIM : (s + 1) * HEAD_DIM, halves(s)]
+            out.append(jnp.concatenate([first, own[:, HALF:]], axis=1))
+        return out
+
+    def unrotate(g, lo, hi):
+        a, b = g[:8], g[8:]
+        c, d = cosine[:, lo:hi], sine[:, lo:hi]
+        return jnp.concatenate([a * c + b * d, b * c - a * d], axis=0)
+
+    def products(h, source, turned, grad_ref, between):
+        queries = [q_ref[s, h] for s in range(2)]
+        grads = [grad_ref[s, :HEAD_DIM] for s in range(2)]
+        keys = [k_ref[s, h] for s in range(2)]
+        for j in range(nblk):
+            between(j)
+            lo, _, hi = bounds(j)
+            for s, g in enumerate(from_key_segments(j, grads, e_ref.at[h])):
+                dproj_ref[s, 2 * HEADS + h, :, lo:hi] = g.astype(BF)
+            for s, g in enumerate(from_key_segments(j, queries, source)):
+                dproj_ref[s, HEADS + h, :, lo:hi] = unrotate(g * 0.25, lo, hi).astype(BF)
+            for s, g in enumerate(from_segments(nblk - 1 - j, keys, turned)):
+                lo, _, hi = bounds(nblk - 1 - j)
+                dproj_ref[s, h, :, lo:hi] = unrotate(g * 0.25, lo, hi).astype(BF)
 
     prepare(0, ga_ref)
     for j in range(nblk):
-        center(0, j, ga_ref, ds_ref)
-
-    @pl.loop(0, heads_total - series, step=2)
-    def _(i):
-        prepare(i + 1, ga2_ref)
-        for j in range(nblk):
-            center(i + 1, j, ga2_ref, ds2_ref)
-            products(i, j, ds_ref, ga_ref)
-        prepare(i + 2, ga_ref)
-        for j in range(nblk):
-            center(i + 2, j, ga_ref, ds_ref)
-            products(i + 1, j, ds2_ref, ga2_ref)
-
-        @pl.when(i == 0)
+        center(0, j, ga_ref, ds_ref, dt_ref)
+    ff_send()
+
+    def step_back(h, source, turned, grad_ref, next_source, next_turned, next_grad_ref):
+        prepare(h + 1, next_grad_ref)
+        products(h, source, turned, grad_ref, lambda j: center(h + 1, j, next_grad_ref, next_source, next_turned))
+
+    even, odd = (ds_ref, dt_ref, ga_ref), (ds2_ref, dt2_ref, ga2_ref)
+
+    @pl.loop(0, HEADS - 3, step=2)
+    def _(h):
+        step_back(h, *even, *odd)
+        step_back(h + 1, *odd, *even)
+
+        @pl.when(h == 2)
         def _():
-            ff_send()
-
-        @pl.when(i == 3 * series)
+            put(stage1, head_grads(STAGE1))
+            sum1.go()
+
+        @pl.when(h == 4)
         def _():
             ff_reduce()
             sum0.reduce()
 
-        @pl.when(i == 5 * series)
-        def _():
-            put(stage1, head_grads(STAGE1))
-            sum1.go()
-
-        @pl.when(i == 7 * series)
-        def _():
-            sum1.reduce()
-            put(stage2, head_grads(STAGE2))
-            sum2.go()
-
-    i = heads_total - 2
-    prepare(i + 1, ga2_ref)
-    for j in range(nblk):
-        center(i + 1, j, ga2_ref, ds2_ref)
-        products(i, j, ds_ref, ga_ref)
-    for j in range(nblk):
-        products(i + 1, j, ds2_ref, ga2_ref)
+    step_back(HEADS - 3, *even, *odd)
+    sum1.reduce()
+    step_back(HEADS - 2, *odd, *even)
+    put(stage2, head_grads(STAGE2))
+    sum2.go()
+    products(HEADS - 1, *even, lambda j: None)
     sum3.go(*one_head_grads(LAST))
 
     def back(s):
         grad = dproj_ref[s].reshape(3 * D, length)
         grad_rows = mm(qkv_ref[...], grad)
-        n, r = norm_stats(scaled_ref[s])
+        n, r = norm_stats(scaled_series(s))
         part, _ = norm_backward(grad_rows, n, r, again)
-        igrad_ref[s] = (dh_ref[s] + part) * spread_inverse(s)
+        igrad_ref[s, 0] = (igrad_ref[s, 0] + part) * spread_inverse(s)
 
     for s in range(series):
         back(s)
         if s == 0:
             sum3.send()
-        store_igrad(s).start()
-
+    down_wide = jnp.concatenate([w_ref[t, :, 2 * hidden_local :] for t in range(n_t)], axis=1)
+    for s in range(series):
+        result_ref[s, 0] = (scaled_ref[s] + mm(down_wide, inner_ref[s])).astype(BF)
+
+    sum2.reduce()
     ff_finish()
     sum0.finish()
     sum1.finish()
-    sum2.reduce()
     fixed = sum(TILES) * LANES
     place_of = jnp.where(
         lax.broadcasted_iota(jnp.int32, (fixed + LANES, source_ref.shape[1]), 0) == source_ref[...], 1.0, 0.0
@@ -613,14 +688,12 @@
 
     tiles = tiles_of(out0, TILES[0]) + tiles_of(out1, TILES[1])
     mgaing_ref[...] = to_row(tiles[1][:, D - LANES : D - LANES + 1].astype(F32))
-    sums = mm(jnp.concatenate(tiles, axis=1), place_of[: fixed - LANES])
+    before = sum(TILES[:2]) * LANES
+    sums = mm(jnp.concatenate(tiles, axis=1), place_of[:before])
     outg_ref[...] = sums[:, 4 * LANES : 4 * LANES + D]
-    for s in range(series):
-        store_result(s).wait()
-        store_igrad(s).wait()
     sum3.reduce()
     sum2.finish()
-    sums = sums[:, : 3 * D] + mm(tiles_of(out2, 1)[0], place_of[fixed - LANES : fixed, : 3 * D])
+    sums = sums[:, : 3 * D] + mm(jnp.concatenate(tiles_of(out2, TILES[2]), axis=1), place_of[before:fixed, : 3 * D])
     sums = sums + mm(sum3.finish(), place_of[fixed:, : 3 * D])
     qkvg_ref[...] = sums
     againg_ref[...] = to_row(jnp.sum(sums * qkv_ref[...].astype(F32), axis=1, keepdims=True) / again)
@@ -647,28 +720,23 @@
 
 
 def copy_kernel(n, *refs):
-    sources, results, held, sems = refs[:n], refs[n : 2 * n], refs[2 * n : 3 * n], refs[3 * n]
-    takes = [pltpu.make_async_copy(sources[i], held[i], sems.at[0, i]) for i in range(n)]
-    gives = [pltpu.make_async_copy(held[i], results[i], sems.at[1, i]) for i in range(n)]
-    for copy in takes:
+    sems = refs[2 * n]
+    copies = [pltpu.make_async_copy(refs[i], refs[n + i], sems.at[i]) for i in range(n)]
+    for copy in copies:
         copy.start()
-    for take, give in zip(takes, gives, strict=True):
-        take.wait()
-        give.start()
-    for copy in gives:
+    for copy in copies:
         copy.wait()
 
 
 def hand_over(arrays):
     n = len(arrays)
-    place = pl.BlockSpec(memory_space=pltpu.HBM)
     return pl.pallas_call(
         functools.partial(copy_kernel, n),
         out_shape=[jax.ShapeDtypeStruct(a.shape, a.dtype) for a in arrays],
-        in_specs=[place] * n,
-        out_specs=[place] * n,
-        scratch_shapes=[pltpu.VMEM(a.shape, a.dtype) for a in arrays] + [pltpu.SemaphoreType.DMA((2, n))],
-    )(*arrays)
+        in_specs=[pl.BlockSpec(memory_space=pltpu.VMEM)] * n,
+        out_specs=[pl.BlockSpec(memory_space=pltpu.HBM)] * n,
+        scratch_shapes=[pltpu.SemaphoreType.DMA((n,))],
+    )(*[pltpu.with_memory_space_constraint(a, pltpu.VMEM) for a in arrays])
 
 
 def layer(n_dp, n_t, median_code, scale_code, raw, cot, qkv, out, again, gate, up, down, mgain):
@@ -676,7 +744,7 @@
     cosine, sine = rope_tables(length)
     source = column_sources()
     blocks = length // BLK
-    packed = BLK * blocks * (blocks + 1) // 2
+    packed = BLK * blocks * (blocks - 1) + (BLK + HALF) * blocks
     vmem = pl.BlockSpec(memory_space=pltpu.VMEM)
     smem = pl.BlockSpec(memory_space=pltpu.SMEM)
     anywhere = pl.BlockSpec(memory_space=pl.ANY)
@@ -687,6 +755,7 @@
     hidden = gate.shape[1]
     share = -(-3 * width // (16 * n_dp)) * 16
     dma = pltpu.SemaphoreType.DMA
+    landing = 2 * LANES * (len(TILES) * (count - 1) * 16 + (pairs * n_t - 1) * (share + 32))
     stages = []
     for n in TILES:
         stages += [
@@ -697,28 +766,31 @@
     return pl.pallas_call(
         functools.partial(kernel, n_dp, n_t),
         out_shape=[
-            jax.ShapeDtypeStruct(raw.shape, BF),
-            jax.ShapeDtypeStruct(raw.shape, F32),
-            jax.ShapeDtypeStruct((width, 3 * width), F32),
-            jax.ShapeDtypeStruct((width, width), F32),
-            jax.ShapeDtypeStruct((1, width), F32),
-            jax.ShapeDtypeStruct((width, hidden), F32),
-            jax.ShapeDtypeStruct((width, hidden), F32),
-            jax.ShapeDtypeStruct((width, hidden), F32),
-            jax.ShapeDtypeStruct((1, width), F32),
+            pltpu.VMEM(raw.shape, BF),
+            pltpu.VMEM(raw.shape, F32),
+            pltpu.VMEM((width, 3 * width), F32),
+            pltpu.VMEM((width, width), F32),
+            pltpu.VMEM((1, width), F32),
+            pltpu.VMEM((width, hidden), F32),
+            pltpu.VMEM((width, hidden), F32),
+            pltpu.VMEM((width, hidden), F32),
+            pltpu.VMEM((1, width), F32),
         ],
         in_specs=[smem, smem, anywhere, anywhere] + [vmem] * 10,
-        out_specs=[anywhere, anywhere] + [vmem] * 7,
+        out_specs=[vmem] * 9,
         scratch_shapes=[
             pltpu.VMEM(rows, BF),
             pltpu.VMEM(rows, BF),
-            pltpu.VMEM(rows, BF),
-            pltpu.VMEM(rows, F32),
-            pltpu.VMEM((series * HEADS, packed, BLK), BF),
+            pltpu.VMEM((HEADS, packed, BLK), BF),
+            pltpu.VMEM((2 * length - 2 * BLK - HALF, BLK), F32),
+            pltpu.VMEM((2 * length - HALF, BLK), F32),
+            pltpu.VMEM((2, 2, BLK), F32),
             pltpu.VMEM((packed, BLK), BF),
             pltpu.VMEM((packed, BLK), BF),
-            pltpu.VMEM((2 * HEAD_DIM, length), BF),
-            pltpu.VMEM((2 * HEAD_DIM, length), BF),
+            pltpu.VMEM((packed, BLK), BF),
+            pltpu.VMEM((packed, BLK), BF),
+            pltpu.VMEM((series, 2 * HEAD_DIM, length), BF),
+            pltpu.VMEM((series, 2 * HEAD_DIM, length), BF),
             pltpu.VMEM((series, HEADS, 2 * HEAD_DIM, length), BF),
             pltpu.VMEM(per_head, BF),
             pltpu.VMEM(per_head, BF),
@@ -726,12 +798,11 @@
             pltpu.VMEM(per_head, F32),
             pltpu.VMEM((series, HEADS, 1, length), F32),
             pltpu.VMEM(per_head, BF),
-            pltpu.VMEM(per_head, BF),
             pltpu.VMEM((series, 3 * HEADS, HEAD_DIM, length), BF),
             pltpu.VMEM(rows, BF),
             pltpu.VMEM(rows, F32),
-            pltpu.VMEM(rows, F32),
             pltpu.VMEM((n_t, width, 3 * hidden), BF),
+            pltpu.VMEM((series, n_t * hidden, length), BF),
             pltpu.VMEM((n_t, n_dp * share, hidden), F32),
             pltpu.VMEM((2, n_t, pairs, share, hidden), BF),
             pltpu.VMEM((n_t, pairs, share, hidden), BF),
@@ -744,7 +815,7 @@
             *one_head,
             dma((2 * series,)), dma((n_t,)), dma((n_t,)), dma((n_t,)), dma((n_t,)), dma((6,)), dma((4,)), dma((4,)), dma((4,)), dma((6,)),
         ],
-        compiler_params=pltpu.CompilerParams(vmem_limit_bytes=60 * 2**20, collective_id=0, has_side_effects=True),
+        compiler_params=pltpu.CompilerParams(vmem_limit_bytes=56 * 2**20 + landing, collective_id=0, has_side_effects=True),
     )(
         median_code, scale_code, raw, cot, qkv, out, again.reshape(1, -1), gate, up, down, mgain.reshape(1, -1), cosine, sine, source
     )

time: 65.3 us -> 57.8 us (0.89)
  Pallas kernels: 64.3 us -> 56.8 us
    pallas_call x1, Pallas kernels: 61.5 us -> 55.3 us  [layer(): pl.pallas_call(functools.partial(kernel, n_dp, n_t), out_shape=[pltpu.VME...]
    pallas_call x1, Pallas kernels: 2.84 us -> 1.5 us  [hand_over(): pl.pallas_call(functools.partial(copy_kernel, n), out_shape=[jax.ShapeDty...]
where the time goes in v5:
time: 57.8 us; the launch traced here: 57.6 us
  Pallas kernels  56.8 us (98%)
  between operations  0.81 us (1%)
    pallas_call x1, Pallas kernels, layer(): pl.pallas_call(functools.partial(kernel, n_dp, n_t), out_shape=[pltpu.VME...  55.3 us
    pallas_call x1, Pallas kernels, hand_over(): pl.pallas_call(functools.partial(copy_kernel, n), out_shape=[jax.ShapeDty...  1.5 us

profile of v5, /device:TPU:0, one launch (start us, length us, event | category | flops | bytes accessed | tf_op | source)
XLA Modules:
  0.0 57.6 jit_solution(13934172937079320368)
XLA Ops:
  0.6 55.3 %shard_map.205 = (bf16[2,1,144,1024]{3,2,1,0:T(8,128)(2,1)S(1)}, f32[2,1,144,1024]{3,2,1,0:T(8,128)S(1)}, f32[144,432]{1,0:T(8,128)S(1)}, f32[144,144]{1,0:T(8,1...) custom-call(s32[1,2]{1,0:T(1,128)} %bitcast.17, ...), custom_call_target="tpu_custom_call" | custom-call | tf_op jit(solution)/shard_map/pallas_call | solution.py:766
  56.0 1.5 %shard_map.206 = (bf16[2,1,144,1024]{3,2,1,0:T(8,128)(2,1)}, f32[2,1,144,1024]{3,2,1,0:T(8,128)}, f32[144,432]{1,0:T(8,128)}, f32[144,144]{1,0:T(8,128)}, f32[1,...) custom-call(bf16[2,1,144,1024]{3,2,1,0:T(8,128)(2,1)S(1)} %get-tuple-element, ...), custom_call_target="tpu_custom_call" | custom-call | tf_op jit(solution)/shard_map/pallas_call | solution.py:733

commit v6 on v5

--- a/solution.py
+++ b/solution.py
@@ -81,6 +81,15 @@
         pl.loop(first, last)(body)
 
 
+def split(k, n):
+    return divmod(k, n) if isinstance(k, int) else (k // n, lax.rem(k, n))
+
+
+def ring(size, mine):
+    known = [mine] + [lax.rem(mine + k, size) for k in range(1, size)] if size <= 40 else None
+    return lambda k: known[k] if known and isinstance(k, int) else lax.rem(mine + k, size)
+
+
 def remote(src, dst, send_sem, recv_sem, device):
     return pltpu.make_async_remote_copy(
         src_ref=src, dst_ref=dst, send_sem=send_sem, recv_sem=recv_sem, device_id=device, device_id_type=MESH
@@ -88,8 +97,8 @@
 
 
 class GroupSum:
-    def __init__(self, index, count, to, first, stage, recv, out, sems):
-        self.index, self.count, self.to, self.first = index, count, to, first
+    def __init__(self, index, count, to, here, other, first, stage, recv, out, sems):
+        self.index, self.count, self.to, self.here, self.other, self.first = index, count, to, here, other, first
         self.stage, self.recv, self.out = stage, recv, out
         self.send, self.land, self.spread, self.gather = (sems.at[i] for i in range(4))
         self.groups = stage.shape[0]
@@ -100,35 +109,34 @@
 
     def go(self):
         def part(g):
-            owner = lax.rem(g * self.stride + self.first, self.count)
+            owner = split(g * self.stride + self.first, self.count)[1]
 
             @pl.when(owner != self.index)
             def _():
-                slot = lax.rem(owner - self.index + self.count, self.count) - 1
-                remote(self.stage.at[g], self.recv.at[slot], self.send, self.land, self.to(owner)).start()
+                remote(self.stage.at[g], self.recv.at[self.index], self.send, self.land, self.to(owner)).start()
 
         each(0, self.groups, part)
 
     def _all_parts(self):
-        return remote(self.recv, self.recv, self.spread, self.land, self.to(self.index))
+        others = self.recv.at[pl.ds(0, self.count - 1)]
+        return remote(others, others, self.spread, self.land, self.here)
 
     def reduce(self):
         @pl.when(self.owner)
         def _():
             self._all_parts().wait_recv()
-            total = self.stage[self.mine].astype(F32) + jnp.sum(self.recv[...].astype(F32), axis=0)
-            self.out[self.mine] = total.astype(BF)
+            self.recv[self.index] = self.stage[self.mine]
+            self.out[self.mine] = jnp.sum(self.recv[...].astype(F32), axis=0).astype(BF)
 
             def whole(k):
-                device = self.to(lax.rem(self.index + k, self.count))
-                remote(self.out.at[self.mine], self.out.at[self.mine], self.spread, self.gather, device).start()
+                remote(self.out.at[self.mine], self.out.at[self.mine], self.spread, self.gather, self.other(k)).start()
 
             each(1, self.count, whole)
 
     def finish(self):
         def landed(n):
             stage, out = self.stage.at[pl.ds(0, n)], self.out.at[pl.ds(0, n)]
-            both = remote(stage, out, self.send, self.gather, self.to(self.index))
+            both = remote(stage, out, self.send, self.gather, self.here)
             both.wait_recv()
             both.wait_send()
 
@@ -184,17 +192,16 @@
 
 def kernel(
     n_dp, n_t,
-    median_ref, scale_ref, raw_hbm, cot_hbm, qkv_ref, out_ref, again_ref, gate_ref, up_ref, down_ref, mgain_ref, cos_ref, sin_ref,
+    median_ref, scale_ref, raw_ref, cot_ref, qkv_ref, out_ref, again_ref, gate_ref, up_ref, down_ref, mgain_ref, cos_ref, sin_ref,
     source_ref,
     result_ref, igrad_ref, qkvg_ref, outg_ref, againg_ref, gateg_ref, upg_ref, downg_ref, mgaing_ref,
-    raw_ref, cot_ref,
     e_ref, held0_ref, held1_ref, largest_ref, ds_ref, ds2_ref, dt_ref, dt2_ref, ga_ref, ga2_ref, qa_ref, q_ref, k_ref, v_ref, o_ref, linv_ref, att_ref, dproj_ref, rows_ref, scaled_ref,
     w_ref, inner_ref, ffacc_ref, ffstage_ref, ffpair_ref, ffhalf_ref, ffrecv_ref, ffout_ref, outacc_ref, gains_ref,
     stage0, recv0, out0, stage1, recv1, out1, stage2, recv2, out2, *rest,
 ):
-    local_sem, w_send, w_recv, w_send2, w_recv2, ff_sem, sems0, sems1, sems2, sems3 = rest[5:]
+    w_send, w_recv, w_send2, w_recv2, ff_sem, sems0, sems1, sems2, sems3 = rest[5:]
     held_refs = (held0_ref, held1_ref)
-    series, _, _, length = raw_hbm.shape
+    series, _, _, length = raw_ref.shape
     nblk = length // BLK
     hidden_local = gate_ref.shape[1]
     count = n_dp * n_t
@@ -205,18 +212,20 @@
     partner = (my_dp + 1 - 2 * core, my_t)
     pairs = n_dp // 2
 
+    here = (my_dp, my_t)
+    on_dp, on_t, on_pair = ring(n_dp, my_dp), ring(n_t, my_t), ring(pairs, pair)
+
     def to(device):
-        return (device // n_t, lax.rem(device, n_t))
-
-    loads = [pltpu.make_async_copy(raw_hbm.at[s, 0], raw_ref.at[s], local_sem.at[s]) for s in range(series)]
-    loads += [pltpu.make_async_copy(cot_hbm.at[s, 0], cot_ref.at[s], local_sem.at[series + s]) for s in range(series)]
-    for copy in loads:
-        copy.start()
+        return split(device, n_t)
+
+    def other(k):
+        along_dp, along_t = split(k, n_t)
+        return on_dp(along_dp), on_t(along_t)
 
     barrier = pltpu.get_barrier_semaphore()
 
     def greet(k):
-        pl.semaphore_signal(barrier, inc=1, device_id=to(lax.rem(index + k, count)), device_id_type=MESH)
+        pl.semaphore_signal(barrier, inc=1, device_id=other(k), device_id_type=MESH)
 
     each(1, count, greet)
 
@@ -227,14 +236,12 @@
         return 1.0 / jnp.full((1, length), scale_ref[0, s].astype(F32) * 0.25, F32)
 
     def scaled_series(s):
-        return (raw_ref[s].astype(F32) - median_ref[0, s].astype(F32) * 0.05) * spread_inverse(s)
+        return (raw_ref[s, 0].astype(F32) - median_ref[0, s].astype(F32) * 0.05) * spread_inverse(s)
 
     tail_rows = lax.broadcasted_iota(jnp.int32, (HEAD_DIM, length), 0)
     w_ref[0, :, :hidden_local] = gate_ref[...]
     w_ref[0, :, hidden_local : 2 * hidden_local] = up_ref[...]
     w_ref[0, :, 2 * hidden_local :] = down_ref[...]
-    for copy in loads:
-        copy.wait()
 
     @pl.loop(0, series)
     def _(s):
@@ -266,7 +273,7 @@
                 body(pl.ds(lo, hi - lo))
 
     def over_links(k, rows):
-        device = (my_dp, lax.rem(my_t + k, n_t))
+        device = (my_dp, on_t(k))
         return remote(w_ref.at[0, rows], w_ref.at[k, rows], w_send.at[k], w_recv.at[k], device)
 
     def within_pair(k, rows):
@@ -437,23 +444,21 @@
         def _():
             exchange_weights()
 
+    finish_weights()
     softmax(HEADS - 1, nblk - 1, ds_ref)
     for j in range(nblk):
         mix(HEADS - 1, j, ds_ref)
 
-    finish_weights()
-
     ffacc_ref[...] = jnp.zeros_like(ffacc_ref)
     outacc_ref[...] = jnp.zeros_like(outacc_ref)
     gains_ref[...] = jnp.zeros_like(gains_ref)
 
-    @pl.loop(0, series)
-    def _(s):
+    def feed_forward(s):
         attended = att_ref[s].reshape(D, length)
         hidden = scaled_ref[s] + mm_tn(out_ref[...], attended)
         n, r = norm_stats(hidden)
         rows = (n * mgain).astype(BF)
-        low = cot_ref[s]
+        low = cot_ref[s, 0]
         top = low.astype(F32)
         scaled_ref[s] = hidden
         grad_rows = jnp.zeros((D, length), F32)
@@ -474,8 +479,10 @@
             gu_piece = mm_nt(rows, grad_both)
             ffacc_ref[t, :D] += gu_piece[:, :hidden_local]
             ffacc_ref[t, D : 2 * D] += gu_piece[:, hidden_local:]
-            ffacc_ref[t, 2 * D : 3 * D] += mm_nt(low, inner)
-
+
+        down_piece = mm_nt(low, inner_ref[s])
+        for t in range(n_t):
+            ffacc_ref[t, 2 * D : 3 * D] += down_piece[:, t * hidden_local : (t + 1) * hidden_local]
         part, gain_part = norm_backward(grad_rows, n, r, mgain)
         grad_hidden = top + part
         igrad_ref[s, 0] = grad_hidden
@@ -484,13 +491,15 @@
         gains_ref[:, 0:1] += gain_part
         att_ref[s] = mm(out_ref[...], branch).astype(BF).reshape(HEADS, HEAD_DIM, length)
 
+    for s in range(series):
+        feed_forward(s)
+
     share = ffout_ref.shape[1]
     for t in range(n_t):
         staged = ffacc_ref[t].astype(BF).reshape(pairs, 2, share, hidden_local)
         for c in range(2):
             ffstage_ref[c, t] = staged[:, c]
     peers = pairs * n_t
-    place = pair * n_t + my_t
 
     def ff_pair():
         return remote(ffstage_ref.at[1 - core], ffpair_ref, ff_sem.at[0], ff_sem.at[1], partner)
@@ -502,15 +511,15 @@
         ffhalf_ref[...] = (ffstage_ref[core].astype(F32) + ffpair_ref[...].astype(F32)).astype(BF)
 
         def part(k):
-            peer = lax.rem(place + k, peers)
-            peer_pair, peer_t = peer // n_t, lax.rem(peer, n_t)
-            piece = ffhalf_ref.at[lax.rem(my_t - peer_t + n_t, n_t), peer_pair]
-            remote(piece, ffrecv_ref.at[k - 1], ff_sem.at[2], ff_sem.at[3], (2 * peer_pair + core, peer_t)).start()
+            along_pair, along_t = split(k, n_t)
+            peer_pair = on_pair(along_pair)
+            piece = ffhalf_ref.at[split(n_t - along_t, n_t)[1], peer_pair]
+            remote(piece, ffrecv_ref.at[k - 1], ff_sem.at[2], ff_sem.at[3], (2 * peer_pair + core, on_t(along_t))).start()
 
         each(1, peers, part)
 
     def ff_parts():
-        return remote(ffrecv_ref, ffrecv_ref, ff_sem.at[2], ff_sem.at[3], to(index))
+        return remote(ffrecv_ref, ffrecv_ref, ff_sem.at[2], ff_sem.at[3], here)
 
     def ff_reduce():
         ff_parts().wait_recv()
@@ -518,7 +527,7 @@
         ffout_ref[my_dp] = total.astype(BF)
 
         def whole(k):
-            device = (lax.rem(my_dp + k, n_dp), my_t)
+            device = (on_dp(k), my_t)
             remote(ffout_ref.at[my_dp], ffout_ref.at[my_dp], ff_sem.at[4], ff_sem.at[5], device).start()
 
         each(1, n_dp, whole)
@@ -526,15 +535,15 @@
     def ff_finish():
         ff_parts().wait_send()
         others = ffout_ref.at[pl.ds(0, n_dp - 1)]
-        remote(others, others, ff_sem.at[4], ff_sem.at[5], to(index)).wait()
+        remote(others, others, ff_sem.at[4], ff_sem.at[5], here).wait()
         sums = ffout_ref[...].astype(F32).reshape(-1, hidden_local)
         gateg_ref[...] = sums[:D]
         upg_ref[...] = sums[D : 2 * D]
         downg_ref[...] = sums[2 * D : 3 * D]
 
-    sum0 = GroupSum(index, count, to, 0, stage0, recv0, out0, sems0)
-    sum1 = GroupSum(index, count, to, count - 18, stage1, recv1, out1, sems1)
-    sum2 = GroupSum(index, count, to, 7, stage2, recv2, out2, sems2)
+    sum0 = GroupSum(index, count, to, here, other, 0, stage0, recv0, out0, sems0)
+    sum1 = GroupSum(index, count, to, here, other, count - 18, stage1, recv1, out1, sems1)
+    sum2 = GroupSum(index, count, to, here, other, 7, stage2, recv2, out2, sems2)
 
     def head_grads(parts):
         total = None
@@ -552,8 +561,8 @@
 
 
     def device_of(k):
-        peer = lax.rem(place + k, peers)
-        return (2 * (peer // n_t) + core, lax.rem(peer, n_t))
+        along_pair, along_t = split(k, n_t)
+        return (2 * on_pair(along_pair) + core, on_t(along_t))
 
     sum3 = HeadSum(*rest[:5], sems3, core, partner, device_of, peers)
 
@@ -653,9 +662,12 @@
 
     step_back(HEADS - 3, *even, *odd)
     sum1.reduce()
-    step_back(HEADS - 2, *odd, *even)
+    prepare(HEADS - 1, ga_ref)
+    products(HEADS - 2, *odd, lambda j: center(HEADS - 1, j, ga_ref, ds_ref, dt_ref) if j >= 2 else None)
     put(stage2, head_grads(STAGE2))
     sum2.go()
+    for j in range(2):
+        center(HEADS - 1, j, ga_ref, ds_ref, dt_ref)
     products(HEADS - 1, *even, lambda j: None)
     sum3.go(*one_head_grads(LAST))
 
@@ -747,7 +759,6 @@
     packed = BLK * blocks * (blocks - 1) + (BLK + HALF) * blocks
     vmem = pl.BlockSpec(memory_space=pltpu.VMEM)
     smem = pl.BlockSpec(memory_space=pltpu.SMEM)
-    anywhere = pl.BlockSpec(memory_space=pl.ANY)
     per_head = (series, HEADS, HEAD_DIM, length)
     rows = (series, width, length)
     count = n_dp * n_t
@@ -755,11 +766,11 @@
     hidden = gate.shape[1]
     share = -(-3 * width // (16 * n_dp)) * 16
     dma = pltpu.SemaphoreType.DMA
-    landing = 2 * LANES * (len(TILES) * (count - 1) * 16 + (pairs * n_t - 1) * (share + 32))
+    landing = 2 * LANES * (len(TILES) * count * 16 + (pairs * n_t - 1) * (share + 32))
     stages = []
     for n in TILES:
         stages += [
-            pltpu.VMEM((n * GROUPS, 16, LANES), BF), pltpu.VMEM((count - 1, 16, LANES), BF), pltpu.VMEM((n * GROUPS, 16, LANES), BF),
+            pltpu.VMEM((n * GROUPS, 16, LANES), BF), pltpu.VMEM((count, 16, LANES), BF), pltpu.VMEM((n * GROUPS, 16, LANES), BF),
         ]
     half = (2, 16, LANES)
     one_head = [pltpu.VMEM(shape, BF) for shape in ((2,) + half, half, half, (pairs * n_t - 1,) + half, (2,) + half)]
@@ -776,11 +787,9 @@
             pltpu.VMEM((width, hidden), F32),
             pltpu.VMEM((1, width), F32),
         ],
-        in_specs=[smem, smem, anywhere, anywhere] + [vmem] * 10,
+        in_specs=[smem, smem] + [vmem] * 12,
         out_specs=[vmem] * 9,
         scratch_shapes=[
-            pltpu.VMEM(rows, BF),
-            pltpu.VMEM(rows, BF),
             pltpu.VMEM((HEADS, packed, BLK), BF),
             pltpu.VMEM((2 * length - 2 * BLK - HALF, BLK), F32),
             pltpu.VMEM((2 * length - HALF, BLK), F32),
@@ -813,9 +822,9 @@
             pltpu.VMEM((width, LANES), F32),
             *stages,
             *one_head,
-            dma((2 * series,)), dma((n_t,)), dma((n_t,)), dma((n_t,)), dma((n_t,)), dma((6,)), dma((4,)), dma((4,)), dma((4,)), dma((6,)),
+            dma((n_t,)), dma((n_t,)), dma((n_t,)), dma((n_t,)), dma((6,)), dma((4,)), dma((4,)), dma((4,)), dma((6,)),
         ],
-        compiler_params=pltpu.CompilerParams(vmem_limit_bytes=56 * 2**20 + landing, collective_id=0, has_side_effects=True),
+        compiler_params=pltpu.CompilerParams(vmem_limit_bytes=57 * 2**20 + landing, collective_id=0, has_side_effects=True),
     )(
         median_code, scale_code, raw, cot, qkv, out, again.reshape(1, -1), gate, up, down, mgain.reshape(1, -1), cosine, sine, source
     )

time: 57.8 us -> 56.4 us (0.976)
  Pallas kernels: 56.8 us -> 55.4 us
    pallas_call x1, Pallas kernels: 55.3 us -> 53.9 us  [layer(): pl.pallas_call(functools.partial(kernel, n_dp, n_t), out_shape=[pltpu.VME...]
where the time goes in v6:
time: 56.4 us; the launch traced here: 56.2 us
  Pallas kernels  55.4 us (98%)
  between operations  0.81 us (1%)
    pallas_call x1, Pallas kernels, layer(): pl.pallas_call(functools.partial(kernel, n_dp, n_t), out_shape=[pltpu.VME...  53.9 us
    pallas_call x1, Pallas kernels, hand_over(): pl.pallas_call(functools.partial(copy_kernel, n), out_shape=[jax.ShapeDty...  1.5 us

profile of v6, /device:TPU:0, one launch (start us, length us, event | category | flops | bytes accessed | tf_op | source)
XLA Modules:
  0.0 56.2 jit_solution(850256465162017357)
XLA Ops:
  0.6 53.9 %shard_map.205 = (bf16[2,1,144,1024]{3,2,1,0:T(8,128)(2,1)S(1)}, f32[2,1,144,1024]{3,2,1,0:T(8,128)S(1)}, f32[144,432]{1,0:T(8,128)S(1)}, f32[144,144]{1,0:T(8,1...) custom-call(s32[1,2]{1,0:T(1,128)} %bitcast.17, ...), custom_call_target="tpu_custom_call" | custom-call | tf_op jit(solution)/shard_map/pallas_call | solution.py:777
  54.6 1.5 %shard_map.206 = (bf16[2,1,144,1024]{3,2,1,0:T(8,128)(2,1)}, f32[2,1,144,1024]{3,2,1,0:T(8,128)}, f32[144,432]{1,0:T(8,128)}, f32[144,144]{1,0:T(8,128)}, f32[1,...) custom-call(bf16[2,1,144,1024]{3,2,1,0:T(8,128)(2,1)S(1)} %get-tuple-element, ...), custom_call_target="tpu_custom_call" | custom-call | tf_op jit(solution)/shard_map/pallas_call | solution.py:745

commit v7 on v6

--- a/solution.py
+++ b/solution.py
@@ -243,8 +243,7 @@
     w_ref[0, :, hidden_local : 2 * hidden_local] = up_ref[...]
     w_ref[0, :, 2 * hidden_local :] = down_ref[...]
 
-    @pl.loop(0, series)
-    def _(s):
+    def project(s):
         scaled = scaled_series(s)
         scaled_ref[s] = scaled
         n, _ = norm_stats(scaled)
@@ -263,6 +262,9 @@
         v_ref[s, :, :HEAD_DIM] = values
         ones = jnp.where(tail_rows < 2, 1.0, 0.0).astype(BF)
         v_ref[s, :, HEAD_DIM:] = jnp.broadcast_to(ones[None], (HEADS, HEAD_DIM, length))
+
+    for s in range(series):
+        project(s)
 
     cut = 16 * ((GROUPS + 1) // 2)
 
@@ -574,8 +576,6 @@
             main, rest = (one, two) if main is None else (main + one, rest + two)
         return main, rest
 
-    put(stage0, jnp.concatenate([outacc_ref[...], gains_ref[:, : 2 * LANES - D]], axis=1))
-    sum0.go()
 
     def prepare(h, grad_ref):
         for s in range(2):
@@ -637,6 +637,8 @@
     prepare(0, ga_ref)
     for j in range(nblk):
         center(0, j, ga_ref, ds_ref, dt_ref)
+    put(stage0, jnp.concatenate([outacc_ref[...], gains_ref[:, : 2 * LANES - D]], axis=1))
+    sum0.go()
     ff_send()
 
     def step_back(h, source, turned, grad_ref, next_source, next_turned, next_grad_ref):

time: 56.4 us -> 56.3 us (level)
  no operation moved by 1% of the time
where the time goes in v7:
time: 56.3 us; the launch traced here: 56.2 us
  Pallas kernels  55.3 us (98%)
  between operations  0.83 us (1%)
    pallas_call x1, Pallas kernels, layer(): pl.pallas_call(functools.partial(kernel, n_dp, n_t), out_shape=[pltpu.VME...  53.8 us
    pallas_call x1, Pallas kernels, hand_over(): pl.pallas_call(functools.partial(copy_kernel, n), out_shape=[jax.ShapeDty...  1.5 us

profile of v7, /device:TPU:0, one launch (start us, length us, event | category | flops | bytes accessed | tf_op | source)
XLA Modules:
  0.0 56.2 jit_solution(13167889141960215709)
XLA Ops:
  0.6 53.8 %shard_map.205 = (bf16[2,1,144,1024]{3,2,1,0:T(8,128)(2,1)S(1)}, f32[2,1,144,1024]{3,2,1,0:T(8,128)S(1)}, f32[144,432]{1,0:T(8,128)S(1)}, f32[144,144]{1,0:T(8,1...) custom-call(s32[1,2]{1,0:T(1,128)} %bitcast.17, ...), custom_call_target="tpu_custom_call" | custom-call | tf_op jit(solution)/shard_map/pallas_call | solution.py:779
  54.5 1.5 %shard_map.206 = (bf16[2,1,144,1024]{3,2,1,0:T(8,128)(2,1)}, f32[2,1,144,1024]{3,2,1,0:T(8,128)}, f32[144,432]{1,0:T(8,128)}, f32[144,144]{1,0:T(8,128)}, f32[1,...) custom-call(bf16[2,1,144,1024]{3,2,1,0:T(8,128)(2,1)S(1)} %get-tuple-element, ...), custom_call_target="tpu_custom_call" | custom-call | tf_op jit(solution)/shard_map/pallas_call | solution.py:747
